TPU v7x, 256 devices: a whole 4x4x8 slice. The times are simulated.
256 devices in a mesh: gx: 16 (over y, x_lo, core), gy: 16 (over z, x_hi).
Axes of the slice: x: 4 (x_hi: 2, x_lo: 2; x = x_hi * 2 + x_lo), y: 4, z: 8, core: 2. Of those that a mesh axis runs over, the one named last changes fastest.
Arguments:
- features: bfloat16 [65536, 128], P(('gx', 'gy')), may hold values from -6 to 6
- w_sub: bfloat16 [27, 128, 128], replicated, may hold values from -0.1875 to 0.1875
- w_down: bfloat16 [1024, 256], replicated, may hold values from -0.25 to 0.25
- cell_ids: int32 [65536], P(('gx', 'gy')), may hold values from -1 to 511, as said below
- send_rows: int32 [73728], P(('gx', 'gy')), may hold values from 0 to 256, as said below
- map_in: int32 [27, 65536], P(None, ('gx', 'gy')), may hold values from 0 to 608, as said below
- map_out: int32 [27, 65536], P(None, ('gx', 'gy')), may hold values from 0 to 256, as said below
- cotangent: bfloat16 [16384, 256], P(('gx', 'gy')), may hold values from -6 to 6
Outputs:
- coarse: bfloat16 [16384, 256], P(('gx', 'gy'))
- feature_grad: bfloat16 [65536, 128], P(('gx', 'gy'))
- sub_grad: float32 [27, 128, 128], replicated
- down_grad: float32 [1024, 256], replicated
Inputs may be any that keep to these rules, and one draw needn't show every extreme that they name: `cell_ids`: in every region the used rows are 0 to count - 1, in increasing cell number; -1 marks unused rows; a region uses at most 256 rows and some region uses exactly 256. `send_rows`: the row of the voxel at each rim cell, 256 where the cell is empty; rim cells listed in increasing cell number. `map_in`: indices into lookup_table: below 256 own rows, 257 + g ghost row g; within each offset the pairs come in increasing output row, and unused entries stand at the end with the value 256. A pair exists exactly where the output voxel and the voxel at its offset both exist. `map_out`: the output row of each pair; 256 on unused entries at the end of each offset's list; each row appears at most once per offset.
All inputs are finite; a program needn't handle non-finite values.
Results may differ from a plain program's by a relative error of at most 0.015.
Values may be sent and summed in bfloat16 or wider, within the bound.
No kernel may reach another device: no remote copies, remote signals or barrier semaphores. Data moves between devices by JAX's collectives and lax.ppermute only.
A program may use at most 64 MiB of HBM per device.

v0:
```python
import jax
import jax.numpy as jnp
import numpy as np
from jax import lax
from jax.sharding import PartitionSpec as P

LX = 4
LY = 16
LZ = 8
U_DEV = 64


def shifted(value, axis, by):
    peers = lax.axis_size(axis)
    pairs = [(i, i + by) for i in range(peers) if 0 <= i + by < peers]
    return lax.ppermute(value, axis, pairs)


def with_halo(block, sides, width):
    for axis, dim in sides:
        count = lax.axis_size(axis)
        forward = [(i, i + 1) for i in range(count - 1)]
        backward = [(target, source) for source, target in forward]
        low = lax.ppermute(
            lax.slice_in_dim(block, block.shape[dim] - width, None, axis=dim), axis, forward
        )
        high = lax.ppermute(lax.slice_in_dim(block, 0, width, axis=dim), axis, backward)
        block = jnp.concatenate([low, block, high], axis=dim)
    return block


def frame_tables():
    cell_count = LX * LY * LZ
    cell_index = np.arange(cell_count)
    coord_x = cell_index // (LY * LZ)
    coord_y = cell_index // LZ % LY
    on_rim = (coord_x == 0) | (coord_x == LX - 1) | (coord_y == 0) | (coord_y == LY - 1)
    rim_place = np.full(cell_count, -1, np.int64)
    rim_place[on_rim] = np.arange(int(on_rim.sum()))
    depth_range = np.arange(LZ)
    neighbour_list, face_list, side_list = ([], [], [])
    for frame_x in range(-1, LX + 1):
        for frame_y in range(-1, LY + 1):
            if 0 <= frame_x < LX and 0 <= frame_y < LY:
                continue
            step_x = -1 if frame_x < 0 else 1 if frame_x >= LX else 0
            step_y = -1 if frame_y < 0 else 1 if frame_y >= LY else 0
            local_cell = ((frame_x - step_x * LX) * LY + (frame_y - step_y * LY)) * LZ + depth_range
            neighbour_list.append(np.full(LZ, (step_x + 1) * 3 + step_y + 1))
            face_list.append(rim_place[local_cell])
            if 0 <= frame_y < LY:
                first_place = (0 if frame_x < 0 else LY * LZ) + frame_y * LZ
            else:
                column = frame_x if 0 <= frame_x < LX else LX if frame_x < 0 else LX + 1
                first_place = 2 * LY * LZ + (0 if frame_y < 0 else (LX + 2) * LZ) + column * LZ
            side_list.append(first_place + depth_range)
    side_place = np.concatenate(side_list)

    def face_rows(spots):
        return np.concatenate(
            [rim_place[(spot_x * LY + spot_y) * LZ + depth_range] for spot_x, spot_y in spots]
        )

    return {
        "neighbour": np.concatenate(neighbour_list),
        "face": np.concatenate(face_list),
        "side_place": side_place,
        "side_order": np.argsort(side_place),
        "x_high": face_rows([(LX - 1, column_y) for column_y in range(LY)]),
        "x_low": face_rows([(0, column_y) for column_y in range(LY)]),
        "y_high": face_rows([(column_x, LY - 1) for column_x in range(LX)]),
        "y_low": face_rows([(column_x, 0) for column_x in range(LX)]),
    }


def assemble_grid(interior, ghost_rows):
    channels = interior.shape[-1]
    top_len = (LY + 2) * LZ
    top_plane = ghost_rows[:top_len].reshape(1, LY + 2, LZ, channels)
    side_cols = ghost_rows[top_len : top_len + 2 * LX * LZ].reshape(LX, 2, LZ, channels)
    bottom_plane = ghost_rows[top_len + 2 * LX * LZ :].reshape(1, LY + 2, LZ, channels)
    middle = jnp.concatenate([side_cols[:, :1], interior, side_cols[:, 1:]], 1)
    return jnp.concatenate([top_plane, middle, bottom_plane], 0)


def frame_of(grid):
    channels = grid.shape[-1]
    side_cols = jnp.stack([grid[1:-1, 0], grid[1:-1, -1]], 1)
    return jnp.concatenate(
        [
            grid[0].reshape(-1, channels),
            side_cols.reshape(-1, channels),
            grid[-1].reshape(-1, channels),
        ],
        0,
    )


def shifted_columns(padded, start_x, start_y, span_x, span_y, starts_z):
    channels = padded.shape[-1]
    slab = padded[start_x : start_x + span_x, start_y : start_y + span_y]
    columns = jnp.concatenate([slab[:, :, start_z : start_z + LZ] for start_z in starts_z], -1)
    return columns.reshape(span_x * span_y * LZ, 3 * channels)


def return_along_y(piece, step):
    return shifted(piece, "gy", step)


def return_along_x(piece, step):
    return shifted(piece, "gx", step)


def local(features, w_sub, w_down, cell_ids, send_rows, map_in, map_out, cotangent):
    frames = frame_tables()
    row_count, channels = features.shape
    cell_count = LX * LY * LZ
    zero_row = jnp.zeros((1, channels), jnp.bfloat16)
    padded = jnp.concatenate([features, zero_row], 0)
    rim_rows = padded[send_rows]
    face_count = rim_rows.shape[0]
    plane_x = LY * LZ
    plane_y = (LX + 2) * LZ
    inner_y = LX * LZ
    beside_all = with_halo(rim_rows[None, None], (("gx", 0), ("gy", 1)), 1)
    flat_rows = beside_all.reshape(9 * face_count, channels)
    ghost_rows = flat_rows[
        jnp.asarray(frames["neighbour"] * face_count + frames["face"], jnp.int32)
    ]
    cell_slot = jnp.where(cell_ids >= 0, cell_ids, cell_count)
    dense_flat = (
        jnp.zeros((cell_count + 1, channels), jnp.bfloat16).at[cell_slot].set(features)[:cell_count]
    )
    active = jnp.zeros((cell_count + 1, 1), jnp.float32).at[cell_slot].set(1.0)[:cell_count]
    active = active.reshape(LX, LY, LZ, 1)
    grid = assemble_grid(dense_flat.reshape(LX, LY, LZ, channels), ghost_rows)
    grid = jnp.pad(grid, ((0, 0), (0, 0), (1, 1), (0, 0)))
    pre_act = jnp.zeros((cell_count, channels), jnp.float32)
    for step_x in range(3):
        for step_y in range(3):
            first = step_x * 9 + step_y * 3
            columns = shifted_columns(grid, step_x, step_y, LX, LY, (0, 1, 2))
            kernel = w_sub[first : first + 3].reshape(3 * channels, channels)
            pre_act = pre_act + jnp.dot(columns, kernel, preferred_element_type=jnp.float32)
    pre_act = pre_act.reshape(LX, LY, LZ, channels)
    hidden = (jax.nn.silu(pre_act) * active).astype(jnp.bfloat16)
    coarse_input = hidden.reshape(LX // 2, 2, LY // 2, 2, LZ // 2, 2, channels).transpose(
        0, 2, 4, 1, 3, 5, 6
    )
    coarse_input = coarse_input.reshape(U_DEV, 8 * channels)
    coarse = jnp.dot(coarse_input, w_down, preferred_element_type=jnp.float32).astype(jnp.bfloat16)
    back_rows = lax.dot_general(
        cotangent, w_down, (((1,), (1,)), ((), ())), preferred_element_type=jnp.float32
    ).astype(jnp.bfloat16)
    hidden_grad = back_rows.reshape(LX // 2, LY // 2, LZ // 2, 2, 2, 2, channels).transpose(
        0, 3, 1, 4, 2, 5, 6
    )
    hidden_grad = hidden_grad.reshape(LX, LY, LZ, channels)
    sigmoid_value = jax.nn.sigmoid(pre_act)
    pre_grad = (
        hidden_grad.astype(jnp.float32)
        * sigmoid_value
        * (1.0 + pre_act * (1.0 - sigmoid_value))
        * active
    ).astype(jnp.bfloat16)
    down_local = lax.dot_general(
        coarse_input, cotangent, (((0,), (0,)), ((), ())), preferred_element_type=jnp.float32
    )
    grad_flat = pre_grad.reshape(cell_count, channels)
    grad_padded = jnp.pad(pre_grad, ((2, 2), (2, 2), (1, 1), (0, 0)))
    weight_parts = []
    table_dense = jnp.zeros(((LX + 2) * (LY + 2) * LZ, channels), jnp.float32)
    for step_x in range(3):
        for step_y in range(3):
            first = step_x * 9 + step_y * 3
            columns = shifted_columns(grid, step_x, step_y, LX, LY, (0, 1, 2))
            part_grad = lax.dot_general(
                columns, grad_flat, (((0,), (0,)), ((), ())), preferred_element_type=jnp.float32
            )
            weight_parts.append(part_grad.reshape(3, channels, channels))
            back_columns = shifted_columns(
                grad_padded, 2 - step_x, 2 - step_y, LX + 2, LY + 2, (2, 1, 0)
            )
            flipped = jnp.swapaxes(w_sub[first : first + 3], 1, 2).reshape(3 * channels, channels)
            table_dense = table_dense + jnp.dot(
                back_columns, flipped, preferred_element_type=jnp.float32
            )
    sub_local = jnp.concatenate(weight_parts, 0)
    table_dense = table_dense.reshape(LX + 2, LY + 2, LZ, channels)
    sub_grad, down_grad = lax.psum((sub_local, down_local), ("gx", "gy"))
    ghost_grad = frame_of(table_dense)
    side_grad = ghost_grad[jnp.asarray(frames["side_order"], jnp.int32)]
    grad_west = side_grad[:plane_x]
    grad_east = side_grad[plane_x : 2 * plane_x]
    grad_south = side_grad[2 * plane_x : 2 * plane_x + plane_y]
    grad_north = side_grad[2 * plane_x + plane_y :]
    return_high = return_along_y(grad_south, -1)
    return_low = return_along_y(grad_north, 1)
    grad_west = (
        grad_west.at[(LY - 1) * LZ :]
        .add(return_high[inner_y : inner_y + LZ])
        .at[:LZ]
        .add(return_low[inner_y : inner_y + LZ])
    )
    grad_east = (
        grad_east.at[(LY - 1) * LZ :]
        .add(return_high[inner_y + LZ :])
        .at[:LZ]
        .add(return_low[inner_y + LZ :])
    )
    return_east = return_along_x(grad_west, -1)
    return_west = return_along_x(grad_east, 1)
    rim_grad = jnp.zeros((face_count, channels), jnp.float32)
    rim_grad = rim_grad.at[frames["x_high"]].add(return_east).at[frames["x_low"]].add(return_west)
    rim_grad = (
        rim_grad.at[frames["y_high"]]
        .add(return_high[:inner_y])
        .at[frames["y_low"]]
        .add(return_low[:inner_y])
    )
    interior_grad = table_dense[1:-1, 1:-1].reshape(cell_count, channels)
    interior_grad = jnp.concatenate([interior_grad, jnp.zeros((1, channels), jnp.float32)], 0)
    own_grad = interior_grad[cell_slot]
    own_grad = (
        jnp.concatenate([own_grad, jnp.zeros((1, channels), jnp.float32)], 0)
        .at[send_rows]
        .add(rim_grad)[:row_count]
    )
    feature_grad = own_grad.astype(jnp.bfloat16)
    return (coarse, feature_grad, sub_grad, down_grad)


def solution(mesh):
    placed = (
        P(("gx", "gy"), None),
        P(),
        P(),
        P(("gx", "gy")),
        P(("gx", "gy")),
        P(None, ("gx", "gy")),
        P(None, ("gx", "gy")),
        P(("gx", "gy"), None),
    )
    return jax.shard_map(
        local,
        mesh=mesh,
        in_specs=placed,
        out_specs=(P(("gx", "gy"), None), P(("gx", "gy"), None), P(), P()),
        check_vma=False,
    )
```

profile of v0, /device:TPU:1, one launch (start us, length us, event | category | flops | bytes accessed | tf_op | source)
XLA Modules:
  0.0 360.8 jit_solution(8910161390339559812)
XLA Ops:
  9.3 1.4 gather_fusion
  10.7 5.1 %collective-permute-start.1 = (bf16[1,1,288,128]{3,2,1,0:T(8,128)(2,1)S(1)}, bf16[1,1,288,128]{3,2,1,0:T(8,128)(2,1)S(1)}, u32[]{:S(2)}, u32[]{:S(2)}) collective-permute-start(bf16[1,1,288,128]{3,2,1,0:T(8,128)(2,1)S(1)} %bitcast.218), channel_id=1, source_target_pairs={{16,0},{32,16},{48,32},{64,48},{80,64},{96,80},{112,96},{128,112},... | collective-permute-start | bytes 221192 | tf_op jit(solution)/shard_map/ppermute | solution.py:27
  15.9 1.9 collective-permute-start
  17.8 2.4 slice_bitcast_fusion.2
  20.5 1.4 scatter_custom_fusion.1
  22.8 1.5 scatter_custom_fusion
  32.5 1.3 collective-permute-start.3
  33.8 5.7 %collective-permute-start.2 = (bf16[3,1,288,128]{3,2,1,0:T(8,128)(2,1)S(1)}, bf16[3,1,288,128]{3,2,1,0:T(8,128)(2,1)S(1)}, u32[]{:S(2)}, u32[]{:S(2)}) collective-permute-start(bf16[3,1,288,128]{3,2,1,0:T(8,128)(2,1)S(1)} %pad_maximum_fusion.19), channel_id=1, source_target_pairs={{0,1},{1,2},{2,3},{3,4},{4,5},{5,6},{6,7},{7,8},{8,9},{9,10},{10,1... | collective-permute-start | bytes 663560 | tf_op jit(solution)/shard_map/ppermute | solution.py:24
  40.1 2.3 collective-permute-done.3
  42.3 4.8 %collective-permute-done.2 = bf16[3,1,288,128]{3,2,1,0:T(8,128)(2,1)S(1)} collective-permute-done((bf16[3,1,288,128]{3,2,1,0:T(8,128)(2,1)S(1)}, bf16[3,1,288,128]{3,2,1,0:T(8,128)(2,1)S(1)}, u32[]{:S(2)}, u32[]{:S(2)}) %collective-permute-start.2) | collective-permute-done | bytes 221216 | tf_op jit(solution)/shard_map/ppermute | solution.py:24
  47.2 1.4 gather_fusion.1
  54.7 1.3 pad_slice_fusion.1
  56.1 2.3 pad_slice_fusion.2
  58.3 1.9 copy.116
  60.3 2.0 copy.112
  69.2 1.3 fusion.47
  85.2 1.3 collective-permute-start.4
  86.5 6.2 %collective-permute-start.5 = (f32[48,128]{1,0:T(8,128)S(1)}, f32[48,128]{1,0:T(8,128)S(1)}, u32[]{:S(2)}, u32[]{:S(2)}) collective-permute-start(f32[48,128]{1,0:T(8,128)S(1)} %get-tuple-element.104), channel_id=1, source_target_pairs={{0,1},{1,2},{2,3},{3,4},{4,5},{5,6},{6,7},{7,8},{8,9},{9,10},{10,1... | collective-permute-start | bytes 73736 | tf_op jit(solution)/shard_map/ppermute | solution.py:16
  93.7 3.4 collective-permute-start.7
  97.1 2.1 collective-permute-start.6
  101.0 2.1 collective-permute-done.6
  107.4 2.1 scatter_fusion.1
  110.2 239.9 %all-reduce.8.cloned.1.call-done = (f32[27,128,128]{2,1,0:T(8,128)}, f32[1024,256]{1,0:T(8,128)}) async-done(((f32[27,128,128]{2,1,0:T(8,128)}, f32[1024,256]{1,0:T(8,128)}), (f32[27,128,128]{2,1,0:T(8,128)}, f32[1024,256]{1,0:T(8,128)})) %all-reduce.8.cloned.1.call-update) | async-done | bytes 2818064 | tf_op jit(solution)/shard_map/psum | solution.py:190
  350.1 3.0 copy.138
  (236 shorter events, 47.7 us)
Async XLA Ops:
  7.2 13.0 %copy-start = (bf16[1024,256]{1,0:T(8,128)(2,1)S(1)}, bf16[1024,256]{1,0:T(8,128)(2,1)}, u32[]{:S(2)}) copy-start(bf16[1024,256]{1,0:T(8,128)(2,1)} %param.28) | copy-start | bytes 1572868
  7.2 342.9 %all-reduce.8.cloned.1.call-start = ((), (), s32[]{:S(2)}) async-start(), calls=%async_computation | async-start | bytes 5636096 | tf_op jit(solution)/shard_map/psum | solution.py:190
  10.7 9.5 %copy-start.52 = (bf16[64,256]{1,0:T(8,128)(2,1)S(1)}, bf16[64,256]{1,0:T(8,128)(2,1)}, u32[]{:S(2)}) copy-start(bf16[64,256]{1,0:T(8,128)(2,1)} %param.31) | copy-start | bytes 98308
  10.7 9.7 %copy-start.60 = (s32[256]{0:T(256)S(1)}, s32[256]{0:T(256)}, u32[]{:S(2)}) copy-start(s32[256]{0:T(256)} %param.29) | copy-start | bytes 3076
  10.7 21.7 %collective-permute-start.1 = (bf16[1,1,288,128]{3,2,1,0:T(8,128)(2,1)S(1)}, bf16[1,1,288,128]{3,2,1,0:T(8,128)(2,1)S(1)}, u32[]{:S(2)}, u32[]{:S(2)}) collective-permute-start(bf16[1,1,288,128]{3,2,1,0:T(8,128)(2,1)S(1)} %bitcast.218), channel_id=1, source_target_pairs={{16,0},{32,16},{48,32},{64,48},{80,64},{96,80},{112,96},{128,112},... | collective-permute-start | bytes 221192 | tf_op jit(solution)/shard_map/ppermute | solution.py:27
  15.9 16.5 %collective-permute-start = (bf16[1,1,288,128]{3,2,1,0:T(8,128)(2,1)S(1)}, bf16[1,1,288,128]{3,2,1,0:T(8,128)(2,1)S(1)}, u32[]{:S(2)}, u32[]{:S(2)}) collective-permute-start(bf16[1,1,288,128]{3,2,1,0:T(8,128)(2,1)S(1)} %bitcast.219), channel_id=1, source_target_pairs={{0,16},{16,32},{32,48},{48,64},{64,80},{80,96},{96,112},{112,128},... | collective-permute-start | bytes 221192 | tf_op jit(solution)/shard_map/ppermute | solution.py:24
  25.5 14.0 %copy-start.58 = (s32[352]{0:T(512)S(1)}, s32[352]{0:T(512)}, u32[]{:S(2)}) copy-start(s32[352]{0:T(512)} %constant.171) | copy-start | bytes 4228
  25.5 14.0 %copy-start.59 = (s32[352]{0:T(512)S(1)}, s32[352]{0:T(512)}, u32[]{:S(2)}) copy-start(s32[352]{0:T(512)} %constant.173) | copy-start | bytes 4228
  32.5 9.9 %collective-permute-start.3 = (bf16[3,1,288,128]{3,2,1,0:T(8,128)(2,1)S(1)}, bf16[3,1,288,128]{3,2,1,0:T(8,128)(2,1)S(1)}, u32[]{:S(2)}, u32[]{:S(2)}) collective-permute-start(bf16[3,1,288,128]{3,2,1,0:T(8,128)(2,1)S(1)} %pad_maximum_fusion.19), channel_id=1, source_target_pairs={{1,0},{2,1},{3,2},{4,3},{5,4},{6,5},{7,6},{8,7},{9,8},{10,9},{11,1... | collective-permute-start | bytes 663560 | tf_op jit(solution)/shard_map/ppermute | solution.py:27
  33.8 13.3 %collective-permute-start.2 = (bf16[3,1,288,128]{3,2,1,0:T(8,128)(2,1)S(1)}, bf16[3,1,288,128]{3,2,1,0:T(8,128)(2,1)S(1)}, u32[]{:S(2)}, u32[]{:S(2)}) collective-permute-start(bf16[3,1,288,128]{3,2,1,0:T(8,128)(2,1)S(1)} %pad_maximum_fusion.19), channel_id=1, source_target_pairs={{0,1},{1,2},{2,3},{3,4},{4,5},{5,6},{6,7},{7,8},{8,9},{9,10},{10,1... | collective-permute-start | bytes 663560 | tf_op jit(solution)/shard_map/ppermute | solution.py:24
  52.0 1.6 copy-start.2
  63.4 1.9 copy-start.14
  67.3 3.2 copy-start.32
  67.3 3.2 copy-start.33
  67.3 3.2 copy-start.41
  69.2 1.5 copy-start.49
  79.3 1.5 copy-start.6
  79.6 1.5 copy-start.9
  85.2 7.6 %collective-permute-start.4 = (f32[48,128]{1,0:T(8,128)S(1)}, f32[48,128]{1,0:T(8,128)S(1)}, u32[]{:S(2)}, u32[]{:S(2)}) collective-permute-start(f32[48,128]{1,0:T(8,128)S(1)} %get-tuple-element.105), channel_id=1, source_target_pairs={{1,0},{2,1},{3,2},{4,3},{5,4},{6,5},{7,6},{8,7},{9,8},{10,9},{11,1... | collective-permute-start | bytes 73736 | tf_op jit(solution)/shard_map/ppermute | solution.py:16
  86.5 7.2 %collective-permute-start.5 = (f32[48,128]{1,0:T(8,128)S(1)}, f32[48,128]{1,0:T(8,128)S(1)}, u32[]{:S(2)}, u32[]{:S(2)}) collective-permute-start(f32[48,128]{1,0:T(8,128)S(1)} %get-tuple-element.104), channel_id=1, source_target_pairs={{0,1},{1,2},{2,3},{3,4},{4,5},{5,6},{6,7},{7,8},{8,9},{9,10},{10,1... | collective-permute-start | bytes 73736 | tf_op jit(solution)/shard_map/ppermute | solution.py:16
  93.7 10.5 %collective-permute-start.7 = (f32[128,128]{1,0:T(8,128)S(1)}, f32[128,128]{1,0:T(8,128)S(1)}, u32[]{:S(2)}, u32[]{:S(2)}) collective-permute-start(f32[128,128]{1,0:T(8,128)S(1)} %get-tuple-element.139), channel_id=1, source_target_pairs={{0,16},{16,32},{32,48},{48,64},{64,80},{80,96},{96,112},{112,128},... | collective-permute-start | bytes 196616 | tf_op jit(solution)/shard_map/ppermute | solution.py:16
  97.1 6.0 %collective-permute-start.6 = (f32[128,128]{1,0:T(8,128)S(1)}, f32[128,128]{1,0:T(8,128)S(1)}, u32[]{:S(2)}, u32[]{:S(2)}) collective-permute-start(f32[128,128]{1,0:T(8,128)S(1)} %get-tuple-element.140), channel_id=1, source_target_pairs={{16,0},{32,16},{48,32},{64,48},{80,64},{96,80},{112,96},{128,112},... | collective-permute-start | bytes 196616 | tf_op jit(solution)/shard_map/ppermute | solution.py:16
  100.1 7.3 %copy-start.56 = (s32[288]{0:T(512)S(1)}, s32[288]{0:T(512)}, u32[]{:S(2)}) copy-start(s32[288]{0:T(512)} %copy-done.55) | copy-start | bytes 3460
  350.1 3.0 copy-start.11
  (46 other events, 48.8 us)
Sparse Core Ops, SparseCore 0:
  84.1 265.8 all-reduce.7
where the time goes:
time: 363 us; the launch traced here: 361 us
  waiting for transfers between devices  250 us (69%)
  local copies, waits for them, and re-layouts  47.3 us (13%)
  starting transfers between devices  27.1 us (7%)
  between operations  15.2 us (4%)
  other arithmetic  11.2 us (3%)
  matrix products  10.2 us (3%)
    psum x1, waiting for transfers between devices, local(): sub_grad, down_grad = lax.psum((sub_local, down_local), ('gx', 'gy'))  240 us
    ppermute x4, starting transfers between devices, shifted(): return lax.ppermute(value, axis, pairs)  13 us
    unnamed x124, local copies, waits for them, and re-layouts  12.7 us
    dot_general x9, local copies, waits for them, and re-layouts, local(): lax.dot_general(columns, grad_flat, (((0,), (0,)), ((), ())), preferred_e...  9.73 us
    transpose x10, local copies, waits for them, and re-layouts, local(): jnp.swapaxes(w_sub[first:first + 3], 1, 2).reshape(3 * channels, channels)  8.48 us
    ppermute x2, starting transfers between devices, with_halo(): lax.ppermute(lax.slice_in_dim(block, block.shape[dim] - width, None, axis...  7.6 us
  transfers between devices with their start and end apart: 9, of which 5 were waited for; matrix products, arithmetic and copies ran while one was open for 7% of the time, Pallas kernels for 0%

commit v1 on v0

v1 whole, which is shorter than its diff:
```python
import jax
import jax.numpy as jnp
from jax import lax
from jax.experimental import pallas as pl
from jax.experimental.pallas import tpu as pltpu
from jax.sharding import PartitionSpec as P

LX = 4
LY = 16
LZ = 8
CELLS = LX * LY * LZ
U_DEV = 64
C = 128
C2 = 256
OFFSETS = 27
AXES = ("gx", "gy")
PEERS = 128
CHUNK = 24
HALF = PEERS * CHUNK
HALF_BLOCKS = HALF // C

F32 = jnp.float32
BF16 = jnp.bfloat16


def swap_pairs(count):
    even = [(k, k ^ 1) for k in range(count)]
    odd = [(k, k + 1 if k % 2 else k - 1) for k in range(count)]
    return even, [(k, m) for k, m in odd if 0 <= m < count]


def swap_both(first, second, axis):
    even, odd = swap_pairs(lax.axis_size(axis))
    return lax.ppermute(first, axis, even), lax.ppermute(second, axis, odd)


def parity(axis):
    return lax.rem(lax.axis_index(axis), 2)


def pick(flag, when_zero, when_one):
    mask = jnp.full(when_zero.shape, flag, jnp.int32) == 0
    return jnp.where(mask, when_zero, when_one)


def dot(left, right, dims=((1,), (0,))):
    return lax.dot_general(left, right, (dims, ((), ())), preferred_element_type=F32)


def cell_onehot(ids):
    cells = lax.broadcasted_iota(jnp.int32, (CELLS, ids.shape[1]), 0)
    return jnp.where(cells == ids, 1.0, 0.0).astype(BF16)


def corner_onehot(row_axis):
    place = lax.broadcasted_iota(jnp.int32, (CELLS, CELLS), row_axis)
    cell = lax.broadcasted_iota(jnp.int32, (CELLS, CELLS), 1 - row_axis)
    corner, row = place >> 6, place & 63
    x = ((row >> 5) << 1) + (corner >> 2)
    y = (((row >> 2) & 7) << 1) + ((corner >> 1) & 1)
    z = ((row & 3) << 1) + (corner & 1)
    return jnp.where(((x * LY + y) * LZ + z) == cell, 1.0, 0.0).astype(BF16)


def shift_z(value, step):
    rows = value.shape[0]
    z = lax.broadcasted_iota(jnp.int32, value.shape, 0) & (LZ - 1)
    if step == 1:
        return jnp.where(z == 0, 0.0, pltpu.roll(value, 1, 0))
    return jnp.where(z == LZ - 1, 0.0, pltpu.roll(value, rows - 1, 0))


def store_y_sides(grid, even_ref, odd_ref):
    low = grid[:, 0].reshape(LX * LZ, C)
    high = grid[:, LY - 1].reshape(LX * LZ, C)
    side = parity("gy")
    even_ref[...] = pick(side, high, low).astype(BF16)
    odd_ref[...] = pick(side, low, high).astype(BF16)


def y_halos(even_ref, odd_ref):
    even, odd = even_ref[...].astype(F32), odd_ref[...].astype(F32)
    side = parity("gy")
    low = pick(side, odd, even).reshape(LX, LZ, C)
    high = pick(side, even, odd).reshape(LX, LZ, C)
    return low, high


def build_kernel(ids_ref, features_ref, grid_ref, even_ref, odd_ref):
    dense = dot(cell_onehot(ids_ref[...]), features_ref[...])
    grid_ref[...] = dense.astype(BF16)
    store_y_sides(dense.reshape(LX, LY, LZ, C), even_ref, odd_ref)


def x_sides_kernel(grid_ref, y_even_ref, y_odd_ref, even_ref, odd_ref):
    plane = LY * LZ
    y_low, y_high = y_halos(y_even_ref, y_odd_ref)
    first = jnp.concatenate([y_low[0], grid_ref[:plane].astype(F32), y_high[0]], 0)
    last = jnp.concatenate([y_low[LX - 1], grid_ref[CELLS - plane :].astype(F32), y_high[LX - 1]], 0)
    side = parity("gx")
    even_ref[...] = pick(side, last, first).astype(BF16)
    odd_ref[...] = pick(side, first, last).astype(BF16)


def fill_padded(padded, grid_ref, y_even_ref, y_odd_ref, x_even_ref, x_odd_ref):
    y_low, y_high = y_halos(y_even_ref, y_odd_ref)
    x_even, x_odd = x_even_ref[...].astype(F32), x_odd_ref[...].astype(F32)
    side = parity("gx")
    padded[0] = pick(side, x_odd, x_even).reshape(LY + 2, LZ, C)
    padded[LX + 1] = pick(side, x_even, x_odd).reshape(LY + 2, LZ, C)
    padded[1 : LX + 1, 0] = y_low
    padded[1 : LX + 1, LY + 1] = y_high
    padded[1 : LX + 1, 1 : LY + 1] = grid_ref[...].astype(F32).reshape(LX, LY, LZ, C)


def columns(padded, step_x, step_y):
    window = padded[step_x : step_x + LX, step_y : step_y + LY]
    return window.reshape(CELLS, C).astype(BF16)


def main_kernel(
    ids_ref, grid_ref, y_even_ref, y_odd_ref, x_even_ref, x_odd_ref, w_sub_ref, w_down_ref, cot_ref,
    coarse_ref, grad_ref, grad_even_ref, grad_odd_ref, own_ref, send_ref, padded, sums,
):
    fill_padded(padded, grid_ref, y_even_ref, y_odd_ref, x_even_ref, x_odd_ref)
    parts = [jnp.zeros((CELLS, C), F32)] * 3
    for step_x in range(3):
        for step_y in range(3):
            window = columns(padded, step_x, step_y)
            first = step_x * 9 + step_y * 3
            parts = [parts[k] + dot(window, w_sub_ref[first + k]) for k in range(3)]
    pre_act = shift_z(parts[0], 1) + parts[1] + shift_z(parts[2], -1)
    active = dot(cell_onehot(ids_ref[...]), jnp.ones((ids_ref.shape[1], C), BF16)) > 0.5
    sigmoid = 1.0 / (1.0 + jnp.exp(-pre_act))
    hidden = jnp.where(active, pre_act * sigmoid, 0.0).astype(BF16)
    by_corner = dot(corner_onehot(0), hidden).astype(BF16)
    coarse_input = jnp.concatenate([by_corner[k * U_DEV : (k + 1) * U_DEV] for k in range(8)], 1)
    cot = cot_ref[...]
    w_down = w_down_ref[...]
    coarse_ref[...] = dot(coarse_input, w_down).astype(BF16)
    back_rows = dot(cot, w_down, ((1,), (1,))).astype(BF16)
    stacked = jnp.concatenate([back_rows[:, k * C : (k + 1) * C] for k in range(8)], 0)
    hidden_grad = dot(corner_onehot(1), stacked)
    pre_grad = hidden_grad * sigmoid * (1.0 + pre_act * (1.0 - sigmoid))
    pre_grad = jnp.where(active, pre_grad, 0.0).astype(BF16)
    grad_ref[...] = pre_grad
    grad = pre_grad.astype(F32)
    store_y_sides(grad.reshape(LX, LY, LZ, C), grad_even_ref, grad_odd_ref)
    spread = jnp.concatenate([shift_z(grad, -1), grad, shift_z(grad, 1)], 1).astype(BF16)
    for step_x in range(3):
        for step_y in range(3):
            first = (step_x * 9 + step_y * 3) * C
            taps = dot(columns(padded, step_x, step_y), spread, ((0,), (0,)))
            for k in range(3):
                sums[first + k * C : first + (k + 1) * C] = taps[:, k * C : (k + 1) * C]
    down = dot(coarse_input, cot, ((0,), (0,)))
    base = OFFSETS * C
    sums[base : base + 8 * C] = down[:, :C]
    sums[base + 8 * C : base + 16 * C] = down[:, C:]
    sums[base + 16 * C :] = jnp.zeros((2 * HALF - base - 16 * C, C), F32)
    mine = parity("gx")
    start = pl.multiple_of(mine * HALF, HALF)
    other = pl.multiple_of((1 - mine) * HALF, HALF)
    own_ref[...] = sums[pl.ds(start, HALF)].reshape(PEERS, CHUNK, C).astype(BF16)
    send_ref[...] = sums[pl.ds(other, HALF)].reshape(PEERS, CHUNK, C).astype(BF16)


def feature_kernel(ids_ref, grid_ref, y_even_ref, y_odd_ref, x_even_ref, x_odd_ref, w_sub_ref, out_ref, padded):
    fill_padded(padded, grid_ref, y_even_ref, y_odd_ref, x_even_ref, x_odd_ref)
    parts = [jnp.zeros((CELLS, C), F32)] * 3
    for step_x in range(3):
        for step_y in range(3):
            window = columns(padded, 2 - step_x, 2 - step_y)
            first = step_x * 9 + step_y * 3
            parts = [parts[k] + dot(window, w_sub_ref[first + k], ((1,), (1,))) for k in range(3)]
    total = shift_z(parts[0], -1) + parts[1] + shift_z(parts[2], 1)
    out_ref[...] = dot(cell_onehot(ids_ref[...]), total.astype(BF16), ((0,), (0,))).astype(BF16)


def unpack_kernel(own_ref, other_ref, sub_ref, down_ref, sums):
    mine = parity("gx")
    start = pl.multiple_of(mine * HALF, HALF)
    other = pl.multiple_of((1 - mine) * HALF, HALF)
    sums[pl.ds(start, HALF)] = own_ref[...].astype(F32).reshape(HALF, C)
    sums[pl.ds(other, HALF)] = other_ref[...].astype(F32).reshape(HALF, C)
    base = OFFSETS * C
    sub_ref[...] = sums[:base].reshape(OFFSETS, C, C)
    down_ref[:, :C] = sums[base : base + 8 * C]
    down_ref[:, C:] = sums[base + 8 * C : base + 16 * C]


def call(kernel, outs, scratch=()):
    def shape(dims, dtype):
        return jax.ShapeDtypeStruct(dims, dtype)

    return pl.pallas_call(
        kernel,
        out_shape=[shape(*out) for out in outs],
        scratch_shapes=list(scratch),
        compiler_params=pltpu.CompilerParams(vmem_limit_bytes=40 * 1024 * 1024),
    )


def halo(grid, y_even, y_odd):
    y_even, y_odd = swap_both(y_even, y_odd, "gy")
    rows = (LY + 2) * LZ
    sides = call(x_sides_kernel, [((rows, C), BF16)] * 2)(grid, y_even, y_odd)
    x_even, x_odd = swap_both(*sides, "gx")
    return grid, y_even, y_odd, x_even, x_odd


def core_swap(value):
    return lax.ppermute(value, "gx", swap_pairs(lax.axis_size("gx"))[0])


def reduce_all(own, send):
    rows, cols = lax.axis_size("gx"), lax.axis_size("gy")
    groups = [[i * cols + j for i in range(core, rows, 2) for j in range(cols)] for core in range(2)]

    def trade(value):
        return lax.all_to_all(value, AXES, 0, 0, axis_index_groups=groups, tiled=True)

    part = (own.astype(F32) + core_swap(send).astype(F32)).astype(BF16)
    mine = trade(part).astype(F32).sum(0).astype(BF16)
    whole = trade(jnp.broadcast_to(mine[None], (PEERS, CHUNK, C)))
    return whole, core_swap(whole)


def local(features, w_sub, w_down, cell_ids, send_rows, map_in, map_out, cotangent):
    ids = cell_ids[None]
    side = ((LX * LZ, C), BF16)
    dense = ((CELLS, C), BF16)
    packed = ((PEERS, CHUNK, C), BF16)
    padded = pltpu.VMEM((LX + 2, LY + 2, LZ, C), F32)
    sums = pltpu.VMEM((2 * HALF, C), F32)
    grid, y_even, y_odd = call(build_kernel, [dense, side, side])(ids, features)
    coarse, grad, grad_even, grad_odd, own, send = call(
        main_kernel, [((U_DEV, C2), BF16), dense, side, side, packed, packed], [padded, sums]
    )(ids, *halo(grid, y_even, y_odd), w_sub, w_down, cotangent)
    (feature_grad,) = call(feature_kernel, [((features.shape[0], C), BF16)], [padded])(
        ids, *halo(grad, grad_even, grad_odd), w_sub
    )
    sub_grad, down_grad = call(
        unpack_kernel, [((OFFSETS, C, C), F32), ((8 * C, C2), F32)], [sums]
    )(*reduce_all(own, send))
    return coarse, feature_grad, sub_grad, down_grad


def solution(mesh):
    rows = P(AXES, None)
    flat = P(AXES)
    maps = P(None, AXES)
    return jax.shard_map(
        local,
        mesh=mesh,
        in_specs=(rows, P(), P(), flat, flat, maps, maps, rows),
        out_specs=(rows, rows, P(), P()),
        check_vma=False,
    )
```

time: 363 us -> 121 us (0.33)
  the two profiles are of different devices: /device:TPU:1 before, /device:TPU:33 now
where the time goes in v1:
time: 121 us; the launch traced here: 120 us
  blocking collectives  68.3 us (56%)
  starting transfers between devices  19.8 us (16%)
  waiting for transfers between devices  18 us (15%)
  Pallas kernels  8.32 us (7%)
  local copies, waits for them, and re-layouts  4.59 us (4%)
    all_to_all x2, blocking collectives, trade(): lax.all_to_all(value, AXES, 0, 0, axis_index_groups=groups, tiled=True)  68.3 us
    ppermute x8, starting transfers between devices, swap_both(): return (lax.ppermute(first, axis, even), lax.ppermute(second, axis, odd))  16.7 us
    ppermute x8, waiting for transfers between devices, swap_both(): return (lax.ppermute(first, axis, even), lax.ppermute(second, axis, odd))  15.7 us
    unnamed x14, local copies, waits for them, and re-layouts  4.48 us
    pallas_call x1, Pallas kernels, local(): call(main_kernel, [((U_DEV, C2), BF16), dense, side, side, packed, packed...  4.04 us
    ppermute x2, starting transfers between devices, core_swap(): return lax.ppermute(value, 'gx', swap_pairs(lax.axis_size('gx'))[0])  3.11 us
  transfers between devices with their start and end apart: 10, of which 5 were waited for; matrix products, arithmetic and copies ran while one was open for 0% of the time, Pallas kernels for 2%

profile of v1, /device:TPU:33, one launch (start us, length us, event | category | flops | bytes accessed | tf_op | source)
XLA Modules:
  0.0 120.0 jit_solution(7509930552157401578)
XLA Ops:
  0.6 0.8 copy-done.3
  1.5 0.7 copy-done.5
  2.4 2.8 %collective-permute-start = (bf16[32,128]{1,0:T(8,128)(2,1)S(1)}, bf16[32,128]{1,0:T(8,128)(2,1)S(1)}, u32[]{:S(2)}, u32[]{:S(2)}) collective-permute-start(bf16[32,128]{1,0:T(8,128)(2,1)S(1)} %get-tuple-element.20), channel_id=1, source_target_pairs={{0,1},{1,0},{2,3},{3,2},{4,5},{5,4},{6,7},{7,6},{8,9},{9,8},{10,11... | collective-permute-start | bytes 24584 | tf_op jit(solution)/shard_map/ppermute | solution.py:34
  5.2 1.9 %collective-permute-start.1 = (bf16[32,128]{1,0:T(8,128)(2,1)S(1)}, bf16[32,128]{1,0:T(8,128)(2,1)S(1)}, u32[]{:S(2)}, u32[]{:S(2)}) collective-permute-start(bf16[32,128]{1,0:T(8,128)(2,1)S(1)} %get-tuple-element.21), channel_id=1, source_target_pairs={{1,2},{2,1},{3,4},{4,3},{5,6},{6,5},{7,8},{8,7},{9,10},{10,9},{11,... | collective-permute-start | bytes 24584 | tf_op jit(solution)/shard_map/ppermute | solution.py:34
  7.2 4.9 %collective-permute-done.1.y_odd_ref = bf16[32,128]{1,0:T(8,128)(2,1)S(1)} collective-permute-done((bf16[32,128]{1,0:T(8,128)(2,1)S(1)}, bf16[32,128]{1,0:T(8,128)(2,1)S(1)}, u32[]{:S(2)}, u32[]{:S(2)}) %collective-permute-start.1) | collective-permute-done | bytes 8224 | tf_op jit(solution)/shard_map/ppermute | solution.py:34
  12.0 2.2 %collective-permute-start.2 = (bf16[144,128]{1,0:T(8,128)(2,1)S(1)}, bf16[144,128]{1,0:T(8,128)(2,1)S(1)}, u32[]{:S(2)}, u32[]{:S(2)}) collective-permute-start(bf16[144,128]{1,0:T(8,128)(2,1)S(1)} %get-tuple-element.22), channel_id=1, source_target_pairs={{0,16},{16,0},{32,48},{48,32},{64,80},{80,64},{96,112},{112,96},{1... | collective-permute-start | bytes 110600 | tf_op jit(solution)/shard_map/ppermute | solution.py:34
  14.2 2.1 %collective-permute-start.3 = (bf16[144,128]{1,0:T(8,128)(2,1)S(1)}, bf16[144,128]{1,0:T(8,128)(2,1)S(1)}, u32[]{:S(2)}, u32[]{:S(2)}) collective-permute-start(bf16[144,128]{1,0:T(8,128)(2,1)S(1)} %get-tuple-element.23), channel_id=1, source_target_pairs={{16,32},{32,16},{48,64},{64,48},{80,96},{96,80},{112,128},{128,112... | collective-permute-start | bytes 110600 | tf_op jit(solution)/shard_map/ppermute | solution.py:34
  16.4 3.3 %collective-permute-done.3.x_odd_ref = bf16[144,128]{1,0:T(8,128)(2,1)S(1)} collective-permute-done((bf16[144,128]{1,0:T(8,128)(2,1)S(1)}, bf16[144,128]{1,0:T(8,128)(2,1)S(1)}, u32[]{:S(2)}, u32[]{:S(2)}) %collective-permute-start.3) | collective-permute-done | bytes 36896 | tf_op jit(solution)/shard_map/ppermute | solution.py:34
  19.6 1.2 copy-done
  20.8 1.0 copy-done.2
  21.8 0.8 copy-done.4
  22.6 4.0 %shard_map.86 = (bf16[64,256]{1,0:T(8,128)(2,1)}, bf16[512,128]{1,0:T(8,128)(2,1)S(1)}, bf16[32,128]{1,0:T(8,128)(2,1)S(1)}, bf16[32,128]{1,0:T(8,128)(2,1)S(1)}...) custom-call(s32[1,256]{1,0:T(1,128)S(1)} %bitcast.2, ...), custom_call_target="tpu_custom_call" | custom-call | tf_op jit(solution)/shard_map/pallas_call | solution.py:237
  26.7 2.3 %collective-permute-done.8 = bf16[128,24,128]{2,1,0:T(8,128)(2,1)S(1)} collective-permute-done((bf16[128,24,128]{2,1,0:T(8,128)(2,1)S(1)}, bf16[128,24,128]{2,1,0:T(8,128)(2,1)S(1)}, u32[]{:S(2)}, u32[]{:S(2)}) %collective-permute-start.8) | collective-permute-done | bytes 786464 | tf_op jit(solution)/shard_map/ppermute | solution.py:213
  29.2 38.0 %all_to_all.10 = bf16[128,24,128]{2,1,0:T(8,128)(2,1)S(1)} all-to-all(bf16[128,24,128]{2,1,0:T(8,128)(2,1)S(1)} %add_convert_fusion), channel_id=1, replica_groups={{0,1,2,3,4,5,6,7,8,9,10,11,12,13,14,15,32,33,34,35,36,37,38,39,40,41,42..., dimensions={0} | all-to-all | bytes 1572864 | tf_op jit(solution)/shard_map/all_to_all | solution.py:221
  67.5 30.3 %all_to_all.11.own_ref = bf16[128,24,128]{2,1,0:T(8,128)(2,1)S(1)} all-to-all(bf16[128,24,128]{2,1,0:T(8,128)(2,1)S(1)} %broadcast_in_dim.10), channel_id=1, replica_groups={{0,1,2,3,4,5,6,7,8,9,10,11,12,13,14,15,32,33,34,35,36,37,38,39,40,41,42..., dimensions={0} | all-to-all | bytes 1572864 | tf_op jit(solution)/shard_map/all_to_all | solution.py:221
  97.8 3.0 %collective-permute-start.9 = (bf16[128,24,128]{2,1,0:T(8,128)(2,1)S(1)}, bf16[128,24,128]{2,1,0:T(8,128)(2,1)S(1)}, u32[]{:S(2)}, u32[]{:S(2)}) collective-permute-start(bf16[128,24,128]{2,1,0:T(8,128)(2,1)S(1)} %all_to_all.11.own_ref), channel_id=1, source_target_pairs={{0,16},{16,0},{32,48},{48,32},{64,80},{80,64},{96,112},{112,96},{1... | collective-permute-start | bytes 2359304 | tf_op jit(solution)/shard_map/ppermute | solution.py:213
  100.8 1.6 %collective-permute-start.4 = (bf16[32,128]{1,0:T(8,128)(2,1)S(1)}, bf16[32,128]{1,0:T(8,128)(2,1)S(1)}, u32[]{:S(2)}, u32[]{:S(2)}) collective-permute-start(bf16[32,128]{1,0:T(8,128)(2,1)S(1)} %get-tuple-element.26), channel_id=1, source_target_pairs={{0,1},{1,0},{2,3},{3,2},{4,5},{5,4},{6,7},{7,6},{8,9},{9,8},{10,11... | collective-permute-start | bytes 24584 | tf_op jit(solution)/shard_map/ppermute | solution.py:34
  102.4 2.5 %collective-permute-start.5 = (bf16[32,128]{1,0:T(8,128)(2,1)S(1)}, bf16[32,128]{1,0:T(8,128)(2,1)S(1)}, u32[]{:S(2)}, u32[]{:S(2)}) collective-permute-start(bf16[32,128]{1,0:T(8,128)(2,1)S(1)} %get-tuple-element.27), channel_id=1, source_target_pairs={{1,2},{2,1},{3,4},{4,3},{5,6},{6,5},{7,8},{8,7},{9,10},{10,9},{11,... | collective-permute-start | bytes 24584 | tf_op jit(solution)/shard_map/ppermute | solution.py:34
  105.0 4.2 %collective-permute-done.5.y_odd_ref = bf16[32,128]{1,0:T(8,128)(2,1)S(1)} collective-permute-done((bf16[32,128]{1,0:T(8,128)(2,1)S(1)}, bf16[32,128]{1,0:T(8,128)(2,1)S(1)}, u32[]{:S(2)}, u32[]{:S(2)}) %collective-permute-start.5) | collective-permute-done | bytes 8224 | tf_op jit(solution)/shard_map/ppermute | solution.py:34
  109.2 1.5 %collective-permute-start.6 = (bf16[144,128]{1,0:T(8,128)(2,1)S(1)}, bf16[144,128]{1,0:T(8,128)(2,1)S(1)}, u32[]{:S(2)}, u32[]{:S(2)}) collective-permute-start(bf16[144,128]{1,0:T(8,128)(2,1)S(1)} %get-tuple-element.28), channel_id=1, source_target_pairs={{0,16},{16,0},{32,48},{48,32},{64,80},{80,64},{96,112},{112,96},{1... | collective-permute-start | bytes 110600 | tf_op jit(solution)/shard_map/ppermute | solution.py:34
  110.8 1.9 %collective-permute-start.7 = (bf16[144,128]{1,0:T(8,128)(2,1)S(1)}, bf16[144,128]{1,0:T(8,128)(2,1)S(1)}, u32[]{:S(2)}, u32[]{:S(2)}) collective-permute-start(bf16[144,128]{1,0:T(8,128)(2,1)S(1)} %get-tuple-element.29), channel_id=1, source_target_pairs={{16,32},{32,16},{48,64},{64,48},{80,96},{96,80},{112,128},{128,112... | collective-permute-start | bytes 110600 | tf_op jit(solution)/shard_map/ppermute | solution.py:34
  112.7 3.3 %collective-permute-done.7.x_odd_ref = bf16[144,128]{1,0:T(8,128)(2,1)S(1)} collective-permute-done((bf16[144,128]{1,0:T(8,128)(2,1)S(1)}, bf16[144,128]{1,0:T(8,128)(2,1)S(1)}, u32[]{:S(2)}, u32[]{:S(2)}) %collective-permute-start.7) | collective-permute-done | bytes 36896 | tf_op jit(solution)/shard_map/ppermute | solution.py:34
  116.0 2.1 %shard_map.88 = bf16[256,128]{1,0:T(8,128)(2,1)} custom-call(s32[1,256]{1,0:T(1,128)S(1)} %bitcast.3, bf16[512,128]{1,0:T(8,128)(2,1)S(1)} %get-tuple-element.25.grid_ref, bf16[32,128]{1,0:T(8,128)(2,1)S(1)} %collective-permute-done.4.y_even_ref, bf16[32,128]{1,0:T(8,128)(2,1)S(1)} %collective-permute-done.5.y_odd_ref, ...), custom_call_target="tpu_custom_call" | custom-call | tf_op jit(solution)/shard_map/pallas_call | solution.py:240
  118.1 1.9 %shard_map.89 = (f32[27,128,128]{2,1,0:T(8,128)}, f32[1024,256]{1,0:T(8,128)}) custom-call(bf16[128,24,128]{2,1,0:T(8,128)(2,1)S(1)} %all_to_all.11.own_ref, bf16[128,24,128]{2,1,0:T(8,128)(2,1)S(1)} %collective-permute-done.9.other_ref), custom_call_target="tpu_custom_call" | custom-call | tf_op jit(solution)/shard_map/pallas_call | solution.py:243
  (21 shorter events, 0.9 us)
Async XLA Ops:
  0.6 0.8 copy-start.3
  1.5 0.7 copy-start.5
  2.4 4.8 %collective-permute-start = (bf16[32,128]{1,0:T(8,128)(2,1)S(1)}, bf16[32,128]{1,0:T(8,128)(2,1)S(1)}, u32[]{:S(2)}, u32[]{:S(2)}) collective-permute-start(bf16[32,128]{1,0:T(8,128)(2,1)S(1)} %get-tuple-element.20), channel_id=1, source_target_pairs={{0,1},{1,0},{2,3},{3,2},{4,5},{5,4},{6,7},{7,6},{8,9},{9,8},{10,11... | collective-permute-start | bytes 24584 | tf_op jit(solution)/shard_map/ppermute | solution.py:34
  5.2 6.8 %collective-permute-start.1 = (bf16[32,128]{1,0:T(8,128)(2,1)S(1)}, bf16[32,128]{1,0:T(8,128)(2,1)S(1)}, u32[]{:S(2)}, u32[]{:S(2)}) collective-permute-start(bf16[32,128]{1,0:T(8,128)(2,1)S(1)} %get-tuple-element.21), channel_id=1, source_target_pairs={{1,2},{2,1},{3,4},{4,3},{5,6},{6,5},{7,8},{8,7},{9,10},{10,9},{11,... | collective-permute-start | bytes 24584 | tf_op jit(solution)/shard_map/ppermute | solution.py:34
  12.0 4.3 %collective-permute-start.2 = (bf16[144,128]{1,0:T(8,128)(2,1)S(1)}, bf16[144,128]{1,0:T(8,128)(2,1)S(1)}, u32[]{:S(2)}, u32[]{:S(2)}) collective-permute-start(bf16[144,128]{1,0:T(8,128)(2,1)S(1)} %get-tuple-element.22), channel_id=1, source_target_pairs={{0,16},{16,0},{32,48},{48,32},{64,80},{80,64},{96,112},{112,96},{1... | collective-permute-start | bytes 110600 | tf_op jit(solution)/shard_map/ppermute | solution.py:34
  14.2 5.4 %collective-permute-start.3 = (bf16[144,128]{1,0:T(8,128)(2,1)S(1)}, bf16[144,128]{1,0:T(8,128)(2,1)S(1)}, u32[]{:S(2)}, u32[]{:S(2)}) collective-permute-start(bf16[144,128]{1,0:T(8,128)(2,1)S(1)} %get-tuple-element.23), channel_id=1, source_target_pairs={{16,32},{32,16},{48,64},{64,48},{80,96},{96,80},{112,128},{128,112... | collective-permute-start | bytes 110600 | tf_op jit(solution)/shard_map/ppermute | solution.py:34
  19.6 1.2 copy-start
  20.8 1.0 copy-start.2
  21.8 0.8 copy-start.4
  26.6 2.4 %collective-permute-start.8 = (bf16[128,24,128]{2,1,0:T(8,128)(2,1)S(1)}, bf16[128,24,128]{2,1,0:T(8,128)(2,1)S(1)}, u32[]{:S(2)}, u32[]{:S(2)}) collective-permute-start(bf16[128,24,128]{2,1,0:T(8,128)(2,1)S(1)} %get-tuple-element.31), channel_id=1, source_target_pairs={{0,16},{16,0},{32,48},{48,32},{64,80},{80,64},{96,112},{112,96},{1... | collective-permute-start | bytes 2359304 | tf_op jit(solution)/shard_map/ppermute | solution.py:213
  67.2 48.8 %copy-start.1 = (bf16[27,128,128]{2,1,0:T(8,128)(2,1)S(1)}, bf16[27,128,128]{2,1,0:T(8,128)(2,1)}, u32[]{:S(2)}) copy-start(bf16[27,128,128]{2,1,0:T(8,128)(2,1)} %w_sub_ref.3) | copy-start | bytes 2654212
  67.2 48.8 %copy-start.6 = (s32[256]{0:T(256)S(1)}, s32[256]{0:T(256)}, u32[]{:S(2)}) copy-start(s32[256]{0:T(256)} %param.11) | copy-start | bytes 3076
  97.8 20.3 %collective-permute-start.9 = (bf16[128,24,128]{2,1,0:T(8,128)(2,1)S(1)}, bf16[128,24,128]{2,1,0:T(8,128)(2,1)S(1)}, u32[]{:S(2)}, u32[]{:S(2)}) collective-permute-start(bf16[128,24,128]{2,1,0:T(8,128)(2,1)S(1)} %all_to_all.11.own_ref), channel_id=1, source_target_pairs={{0,16},{16,0},{32,48},{48,32},{64,80},{80,64},{96,112},{112,96},{1... | collective-permute-start | bytes 2359304 | tf_op jit(solution)/shard_map/ppermute | solution.py:213
  100.8 4.2 %collective-permute-start.4 = (bf16[32,128]{1,0:T(8,128)(2,1)S(1)}, bf16[32,128]{1,0:T(8,128)(2,1)S(1)}, u32[]{:S(2)}, u32[]{:S(2)}) collective-permute-start(bf16[32,128]{1,0:T(8,128)(2,1)S(1)} %get-tuple-element.26), channel_id=1, source_target_pairs={{0,1},{1,0},{2,3},{3,2},{4,5},{5,4},{6,7},{7,6},{8,9},{9,8},{10,11... | collective-permute-start | bytes 24584 | tf_op jit(solution)/shard_map/ppermute | solution.py:34
  102.4 6.8 %collective-permute-start.5 = (bf16[32,128]{1,0:T(8,128)(2,1)S(1)}, bf16[32,128]{1,0:T(8,128)(2,1)S(1)}, u32[]{:S(2)}, u32[]{:S(2)}) collective-permute-start(bf16[32,128]{1,0:T(8,128)(2,1)S(1)} %get-tuple-element.27), channel_id=1, source_target_pairs={{1,2},{2,1},{3,4},{4,3},{5,6},{6,5},{7,8},{8,7},{9,10},{10,9},{11,... | collective-permute-start | bytes 24584 | tf_op jit(solution)/shard_map/ppermute | solution.py:34
  109.2 3.4 %collective-permute-start.6 = (bf16[144,128]{1,0:T(8,128)(2,1)S(1)}, bf16[144,128]{1,0:T(8,128)(2,1)S(1)}, u32[]{:S(2)}, u32[]{:S(2)}) collective-permute-start(bf16[144,128]{1,0:T(8,128)(2,1)S(1)} %get-tuple-element.28), channel_id=1, source_target_pairs={{0,16},{16,0},{32,48},{48,32},{64,80},{80,64},{96,112},{112,96},{1... | collective-permute-start | bytes 110600 | tf_op jit(solution)/shard_map/ppermute | solution.py:34
  110.8 5.3 %collective-permute-start.7 = (bf16[144,128]{1,0:T(8,128)(2,1)S(1)}, bf16[144,128]{1,0:T(8,128)(2,1)S(1)}, u32[]{:S(2)}, u32[]{:S(2)}) collective-permute-start(bf16[144,128]{1,0:T(8,128)(2,1)S(1)} %get-tuple-element.29), channel_id=1, source_target_pairs={{16,32},{32,16},{48,64},{64,48},{80,96},{96,80},{112,128},{128,112... | collective-permute-start | bytes 110600 | tf_op jit(solution)/shard_map/ppermute | solution.py:34

commit v2 on v1

v2 whole, which is shorter than its diff:
```python
import jax
import jax.numpy as jnp
from jax import lax
from jax.experimental import pallas as pl
from jax.experimental.pallas import tpu as pltpu
from jax.sharding import PartitionSpec as P

LX = 4
LY = 16
LZ = 8
CELLS = LX * LY * LZ
U_DEV = 64
C = 128
C2 = 256
OFFSETS = 27
AXES = ("gx", "gy")
CHUNK = 176
HALF = 16 * CHUNK
LONG = 1 << 33

F32 = jnp.float32
BF16 = jnp.bfloat16


def swap_pairs(count):
    even = [(k, k ^ 1) for k in range(count)]
    odd = [(k, k + 1 if k % 2 else k - 1) for k in range(count)]
    return even, [(k, m) for k, m in odd if 0 <= m < count]


def swap_both(first, second, axis):
    even, odd = swap_pairs(lax.axis_size(axis))
    second = lax.ppermute(second, axis, odd)
    return lax.ppermute(first, axis, even), second


def parity(axis):
    return lax.rem(lax.axis_index(axis), 2)


def pick(flag, when_zero, when_one):
    mask = jnp.full(when_zero.shape, flag, jnp.int32) == 0
    return jnp.where(mask, when_zero, when_one)


def dot(left, right, dims=((1,), (0,))):
    return lax.dot_general(left, right, (dims, ((), ())), preferred_element_type=F32)


def cell_onehot(ids):
    cells = lax.broadcasted_iota(jnp.int32, (CELLS, ids.shape[1]), 0)
    return jnp.where(cells == ids, 1.0, 0.0).astype(BF16)


def corner_onehot(row_axis):
    place = lax.broadcasted_iota(jnp.int32, (CELLS, CELLS), row_axis)
    cell = lax.broadcasted_iota(jnp.int32, (CELLS, CELLS), 1 - row_axis)
    corner, row = place >> 6, place & 63
    x = ((row >> 5) << 1) + (corner >> 2)
    y = (((row >> 2) & 7) << 1) + ((corner >> 1) & 1)
    z = ((row & 3) << 1) + (corner & 1)
    return jnp.where(((x * LY + y) * LZ + z) == cell, 1.0, 0.0).astype(BF16)


def shift_z(value, step):
    rows = value.shape[0]
    z = lax.broadcasted_iota(jnp.int32, value.shape, 0) & (LZ - 1)
    if step == 1:
        return jnp.where(z == 0, 0.0, pltpu.roll(value, 1, 0))
    return jnp.where(z == LZ - 1, 0.0, pltpu.roll(value, rows - 1, 0))


def y_sides(dense, hidden_grad):
    def face(near, edge):
        rows = [dense[:, near].reshape(2 * LX * LZ, C), hidden_grad[:, edge].reshape(LX * LZ, C)]
        return jnp.concatenate(rows, 0)

    return face(slice(0, 2), 0), face(slice(LY - 2, LY), LY - 1)


def split_y(rows):
    return rows[: 2 * LX * LZ].reshape(LX, 2 * LZ, C), rows[2 * LX * LZ :].reshape(LX, LZ, C)


def places_kernel(from_ref, to_ref):
    from_ref[...] = corner_onehot(1)
    to_ref[...] = corner_onehot(0)


def build_kernel(place_ref, ids, features, cot, w_down, grid_ref, hidden_ref, even_ref, odd_ref):
    onehot = cell_onehot(ids[...])
    dense = dot(onehot, features[...])
    active = dot(onehot, jnp.ones((onehot.shape[1], C), BF16)) > 0.5
    back_rows = dot(cot[...], w_down[...], ((1,), (1,))).astype(BF16)
    stacked = jnp.concatenate([back_rows[:, k * C : (k + 1) * C] for k in range(8)], 0)
    hidden_grad = jnp.where(active, dot(place_ref[...], stacked), 0.0)
    grid_ref[...] = dense.astype(BF16)
    hidden_ref[...] = hidden_grad.astype(BF16)
    low, high = y_sides(dense.reshape(LX, LY, LZ, C), hidden_grad.reshape(LX, LY, LZ, C))
    side = parity("gy")
    even_ref[...] = pick(side, high, low).astype(BF16)
    odd_ref[...] = pick(side, low, high).astype(BF16)


def y_halos(even_ref, odd_ref):
    even, odd = even_ref[...].astype(F32), odd_ref[...].astype(F32)
    side = parity("gy")
    return split_y(pick(side, odd, even)), split_y(pick(side, even, odd))


def x_sides_kernel(grid_ref, hidden_ref, y_even_ref, y_odd_ref, even_ref, odd_ref):
    plane = LY * LZ
    (low, low_grad), (high, high_grad) = y_halos(y_even_ref, y_odd_ref)

    def face(planes, edge):
        rows = []
        for x in planes:
            rows += [low[x], grid_ref[x * plane : (x + 1) * plane].astype(F32), high[x]]
        rows += [low_grad[edge], hidden_ref[edge * plane : (edge + 1) * plane].astype(F32), high_grad[edge]]
        return jnp.concatenate(rows, 0)

    first, last = face((0, 1), 0), face((LX - 2, LX - 1), LX - 1)
    side = parity("gx")
    even_ref[...] = pick(side, last, first).astype(BF16)
    odd_ref[...] = pick(side, first, last).astype(BF16)


def main_kernel(
    place_ref, ids_ref, grid_ref, hidden_ref, y_even_ref, y_odd_ref, x_even_ref, x_odd_ref, cot_ref, w_down_ref, w_sub,
    coarse_ref, grad_ref, own_ref, send_ref, padded, hidden_pad, sums,
):
    (low, low_grad), (high, high_grad) = y_halos(y_even_ref, y_odd_ref)
    x_even, x_odd = x_even_ref[...].astype(F32), x_odd_ref[...].astype(F32)
    side = parity("gx")
    for rows, at in ((pick(side, x_odd, x_even), 0), (pick(side, x_even, x_odd), LX + 2)):
        split = 2 * (LY + 4) * LZ
        padded[at : at + 2] = rows[:split].reshape(2, LY + 4, LZ, C)
        hidden_pad[0 if at == 0 else LX + 1] = rows[split:].reshape(LY + 2, LZ, C)
    padded[2 : LX + 2, 0:2] = low.reshape(LX, 2, LZ, C)
    padded[2 : LX + 2, LY + 2 :] = high.reshape(LX, 2, LZ, C)
    padded[2 : LX + 2, 2 : LY + 2] = grid_ref[...].astype(F32).reshape(LX, LY, LZ, C)
    hidden_pad[1 : LX + 1, 0] = low_grad
    hidden_pad[1 : LX + 1, LY + 1] = high_grad
    hidden_pad[1 : LX + 1, 1 : LY + 1] = hidden_ref[...].astype(F32).reshape(LX, LY, LZ, C)

    frame = (LX + 2) * (LY + 2) * LZ
    parts = [jnp.zeros((frame, C), F32)] * 3
    for step_x in range(3):
        for step_y in range(3):
            window = padded[step_x : step_x + LX + 2, step_y : step_y + LY + 2].reshape(frame, C).astype(BF16)
            first = step_x * 9 + step_y * 3
            parts = [parts[k] + dot(window, w_sub[first + k]) for k in range(3)]
    pre_act = shift_z(parts[0], 1) + parts[1] + shift_z(parts[2], -1)
    sigmoid = 1.0 / (1.0 + jnp.exp(-pre_act))
    hidden_grad = hidden_pad[...].reshape(frame, C)
    pre_grad = (hidden_grad * sigmoid * (1.0 + pre_act * (1.0 - sigmoid))).astype(BF16)
    grad_ref[...] = pre_grad

    def inner(value):
        return value.reshape(LX + 2, LY + 2, LZ, C)[1 : LX + 1, 1 : LY + 1].reshape(CELLS, C)

    active = dot(cell_onehot(ids_ref[...]), jnp.ones((ids_ref.shape[1], C), BF16)) > 0.5
    hidden = jnp.where(active, inner(pre_act * sigmoid), 0.0).astype(BF16)
    by_corner = dot(place_ref[...], hidden).astype(BF16)
    coarse_input = jnp.concatenate([by_corner[k * U_DEV : (k + 1) * U_DEV] for k in range(8)], 1)
    cot = cot_ref[...]
    coarse_ref[...] = dot(coarse_input, w_down_ref[...]).astype(BF16)
    grad = inner(pre_grad.astype(F32))
    spread = jnp.concatenate([shift_z(grad, -1), grad, shift_z(grad, 1)], 1).astype(BF16)
    for step_x in range(3):
        for step_y in range(3):
            first = (step_x * 9 + step_y * 3) * C
            window = padded[step_x + 1 : step_x + 1 + LX, step_y + 1 : step_y + 1 + LY]
            taps = dot(window.reshape(CELLS, C).astype(BF16), spread, ((0,), (0,)))
            for k in range(3):
                sums[first + k * C : first + (k + 1) * C] = taps[:, k * C : (k + 1) * C]
    down = dot(coarse_input, cot, ((0,), (0,)))
    base = OFFSETS * C
    sums[base : base + 8 * C] = down[:, :C]
    sums[base + 8 * C : base + 16 * C] = down[:, C:]
    sums[base + 16 * C :] = jnp.zeros((2 * HALF - base - 16 * C, C), F32)
    mine, other = halves()
    own_ref[...] = sums[mine].astype(BF16)
    send_ref[...] = sums[other].astype(BF16)


def halves():
    core = parity("gx")
    return pl.ds(pl.multiple_of(core * HALF, HALF), HALF), pl.ds(pl.multiple_of((1 - core) * HALF, HALF), HALF)


def feature_kernel(ids_ref, grad_ref, w_sub_ref, out_ref, padded):
    padded[...] = grad_ref[...].astype(F32).reshape(LX + 2, LY + 2, LZ, C)
    parts = [jnp.zeros((CELLS, C), F32)] * 3
    for step_x in range(3):
        for step_y in range(3):
            window = padded[2 - step_x : 2 - step_x + LX, 2 - step_y : 2 - step_y + LY]
            window = window.reshape(CELLS, C).astype(BF16)
            first = step_x * 9 + step_y * 3
            parts = [parts[k] + dot(window, w_sub_ref[first + k], ((1,), (1,))) for k in range(3)]
    total = shift_z(parts[0], -1) + parts[1] + shift_z(parts[2], 1)
    out_ref[...] = dot(cell_onehot(ids_ref[...]), total.astype(BF16), ((0,), (0,))).astype(BF16)


def add_kernel(own_ref, other_ref, out_ref):
    out_ref[...] = (own_ref[...].astype(F32) + other_ref[...].astype(F32)).astype(BF16)


def sum_kernel(parts_ref, out_ref):
    total = parts_ref[:CHUNK].astype(F32)
    for start in range(CHUNK, parts_ref.shape[0], CHUNK):
        total = total + parts_ref[start : start + CHUNK].astype(F32)
    total = total.astype(BF16)
    for start in range(0, out_ref.shape[0], CHUNK):
        out_ref[start : start + CHUNK] = total


def unpack_kernel(own_ref, other_ref, sub_ref, down_ref, sums):
    mine, other = halves()
    sums[mine] = own_ref[...].astype(F32)
    sums[other] = other_ref[...].astype(F32)
    base = OFFSETS * C
    sub_ref[...] = sums[:base].reshape(OFFSETS, C, C)
    down_ref[:, :C] = sums[base : base + 8 * C]
    down_ref[:, C:] = sums[base + 8 * C : base + 16 * C]


def call(kernel, outs, scratch=(), flops=0):
    return pl.pallas_call(
        kernel,
        out_shape=[jax.ShapeDtypeStruct(*out) for out in outs],
        scratch_shapes=list(scratch),
        cost_estimate=pl.CostEstimate(flops=flops, bytes_accessed=1 << 20, transcendentals=0),
        compiler_params=pltpu.CompilerParams(vmem_limit_bytes=40 * 1024 * 1024),
    )


def core_swap(value):
    return lax.ppermute(value, "gx", swap_pairs(lax.axis_size("gx"))[0])


def reduce_all(own, send):
    rows, cols = lax.axis_size("gx"), lax.axis_size("gy")
    plane = [
        [i * cols + j for i in range(core, rows, 2) for j in (first, first + 1)]
        for core in range(2)
        for first in range(0, cols, 2)
    ]
    depth = [[i * cols + j for j in range(side, cols, 2)] for i in range(rows) for side in range(2)]

    def trade(value, groups):
        return lax.all_to_all(value, AXES, 0, 0, axis_index_groups=groups, tiled=True)

    packed = ((HALF, C), BF16)
    (part,) = call(add_kernel, [packed])(own, core_swap(send))
    (mine,) = call(sum_kernel, [((len(depth[0]) * CHUNK, C), BF16)])(trade(part, plane))
    (total,) = call(sum_kernel, [packed])(trade(mine, depth))
    whole = trade(total, plane)
    return whole, core_swap(whole)


def local(features, w_sub, w_down, cell_ids, send_rows, map_in, map_out, cotangent):
    ids = cell_ids[None]
    rows = features.shape[0]
    dense = ((CELLS, C), BF16)
    y_side = ((3 * LX * LZ, C), BF16)
    x_side = (((2 * (LY + 4) + LY + 2) * LZ, C), BF16)
    frame = (((LX + 2) * (LY + 2) * LZ, C), BF16)
    packed = ((HALF, C), BF16)
    framed = pltpu.VMEM((LX + 2, LY + 2, LZ, C), F32)
    padded = pltpu.VMEM((LX + 4, LY + 4, LZ, C), F32)
    sums = pltpu.VMEM((2 * HALF, C), F32)

    place = ((CELLS, CELLS), BF16)
    from_corner, to_corner = call(places_kernel, [place, place], flops=LONG)()
    grid, hidden_grad, y_even, y_odd = call(build_kernel, [dense, dense, y_side, y_side], flops=LONG)(
        from_corner, ids, features, cotangent, w_down
    )
    y_even, y_odd = swap_both(y_even, y_odd, "gy")
    sides = call(x_sides_kernel, [x_side, x_side], flops=LONG)(grid, hidden_grad, y_even, y_odd)
    x_even, x_odd = swap_both(*sides, "gx")
    coarse, grad, own, send = call(
        main_kernel,
        [((U_DEV, C2), BF16), frame, packed, packed],
        [padded, framed, sums],
        1 << 31,
    )(to_corner, ids, grid, hidden_grad, y_even, y_odd, x_even, x_odd, cotangent, w_down, w_sub)
    (feature_grad,) = call(feature_kernel, [((rows, C), BF16)], [framed], flops=1 << 30)(ids, grad, w_sub)
    sub_grad, down_grad = call(
        unpack_kernel, [((OFFSETS, C, C), F32), ((8 * C, C2), F32)], [sums]
    )(*reduce_all(own, send))
    return coarse, feature_grad, sub_grad, down_grad


def solution(mesh):
    rows = P(AXES, None)
    flat = P(AXES)
    maps = P(None, AXES)
    return jax.shard_map(
        local,
        mesh=mesh,
        in_specs=(rows, P(), P(), flat, flat, maps, maps, rows),
        out_specs=(rows, rows, P(), P()),
        check_vma=False,
    )
```

time: 121 us -> 89.3 us (0.74)
  the two profiles are of different devices: /device:TPU:33 before, /device:TPU:1 now
where the time goes in v2:
time: 89.3 us; the launch traced here: 89.1 us
  blocking collectives  55.7 us (62%)
  starting transfers between devices  15.2 us (17%)
  Pallas kernels  9.77 us (11%)
  waiting for transfers between devices  6.98 us (8%)
    all_to_all x3, blocking collectives, trade(): lax.all_to_all(value, AXES, 0, 0, axis_index_groups=groups, tiled=True)  55.7 us
    ppermute x2, starting transfers between devices, swap_both(): return (lax.ppermute(first, axis, even), second)  7.53 us
    ppermute x2, starting transfers between devices, core_swap(): return lax.ppermute(value, 'gx', swap_pairs(lax.axis_size('gx'))[0])  5.15 us
    pallas_call x1, Pallas kernels, local(): call(main_kernel, [((U_DEV, C2), BF16), frame, packed, packed], [padded,...  4.34 us
    ppermute x2, waiting for transfers between devices, swap_both(): second = lax.ppermute(second, axis, odd)  4.23 us
    ppermute x2, starting transfers between devices, swap_both(): second = lax.ppermute(second, axis, odd)  2.56 us
    ppermute x2, waiting for transfers between devices, core_swap(): return lax.ppermute(value, 'gx', swap_pairs(lax.axis_size('gx'))[0])  2.18 us
    pallas_call x1, Pallas kernels, local(): call(feature_kernel, [((rows, C), BF16)], [framed], flops=1 << 30)  2.08 us
  transfers between devices with their start and end apart: 6, of which 3 were waited for; matrix products, arithmetic and copies ran while one was open for 0% of the time, Pallas kernels for 2%

profile of v2, /device:TPU:1, one launch (start us, length us, event | category | flops | bytes accessed | tf_op | source)
XLA Modules:
  0.0 89.1 jit_solution(17070609723005807049)
XLA Ops:
  0.7 0.4 shard_map.84
  1.1 0.3 copy-done.3
  1.4 0.3 copy-done.1
  1.7 0.7 shard_map.85
  2.4 3.7 %collective-permute-start = (bf16[96,128]{1,0:T(8,128)(2,1)S(1)}, bf16[96,128]{1,0:T(8,128)(2,1)S(1)}, u32[]{:S(2)}, u32[]{:S(2)}) collective-permute-start(bf16[96,128]{1,0:T(8,128)(2,1)S(1)} %get-tuple-element.22), channel_id=1, source_target_pairs={{0,1},{1,0},{2,3},{3,2},{4,5},{5,4},{6,7},{7,6},{8,9},{9,8},{10,11... | collective-permute-start | bytes 73736 | tf_op jit(solution)/shard_map/ppermute | solution.py:34
  6.0 0.7 collective-permute-start.1
  6.7 0.6 collective-permute-done.y_even_ref
  7.3 0.0 collective-permute-done.1.y_odd_ref
  7.3 0.1 shard_map.86
  7.3 3.9 %collective-permute-start.2 = (bf16[464,128]{1,0:T(8,128)(2,1)S(1)}, bf16[464,128]{1,0:T(8,128)(2,1)S(1)}, u32[]{:S(2)}, u32[]{:S(2)}) collective-permute-start(bf16[464,128]{1,0:T(8,128)(2,1)S(1)} %get-tuple-element.24), channel_id=1, source_target_pairs={{0,16},{16,0},{32,48},{48,32},{64,80},{80,64},{96,112},{112,96},{1... | collective-permute-start | bytes 356360 | tf_op jit(solution)/shard_map/ppermute | solution.py:34
  11.2 1.9 %collective-permute-start.3 = (bf16[464,128]{1,0:T(8,128)(2,1)S(1)}, bf16[464,128]{1,0:T(8,128)(2,1)S(1)}, u32[]{:S(2)}, u32[]{:S(2)}) collective-permute-start(bf16[464,128]{1,0:T(8,128)(2,1)S(1)} %get-tuple-element.25), channel_id=1, source_target_pairs={{16,32},{32,16},{48,64},{64,48},{80,96},{96,80},{112,128},{128,112... | collective-permute-start | bytes 356360 | tf_op jit(solution)/shard_map/ppermute | solution.py:33
  13.1 4.2 %collective-permute-done.3.x_odd_ref = bf16[464,128]{1,0:T(8,128)(2,1)S(1)} collective-permute-done((bf16[464,128]{1,0:T(8,128)(2,1)S(1)}, bf16[464,128]{1,0:T(8,128)(2,1)S(1)}, u32[]{:S(2)}, u32[]{:S(2)}) %collective-permute-start.3) | collective-permute-done | bytes 118816 | tf_op jit(solution)/shard_map/ppermute | solution.py:33
  17.4 4.3 %shard_map.87 = (bf16[64,256]{1,0:T(8,128)(2,1)}, bf16[864,128]{1,0:T(8,128)(2,1)S(1)}, bf16[2816,128]{1,0:T(8,128)(2,1)S(1)}, bf16[2816,128]{1,0:T(8,128)(2,1)S(1)}) custom-call(bf16[512,512]{1,0:T(8,128)(2,1)S(1)} %get-tuple-element.18.place_ref, s32[1,256]{1,0:T(1,128)S(1)} %bitcast.15, bf16[512,128]{1,0:T(8,128)(2,1)S(1)} %get-tuple-element.20.grid_ref, ...), custom_call_target="tpu_custom_call" | custom-call | flops 2147483648 | bytes 1048576 | tf_op jit(solution)/shard_map/pallas_call | solution.py:282
  21.7 0.1 collective-permute-start.4
  21.8 2.2 %collective-permute-done.4.other_ref = bf16[2816,128]{1,0:T(8,128)(2,1)S(1)} collective-permute-done((bf16[2816,128]{1,0:T(8,128)(2,1)S(1)}, bf16[2816,128]{1,0:T(8,128)(2,1)S(1)}, u32[]{:S(2)}, u32[]{:S(2)}) %collective-permute-start.4) | collective-permute-done | bytes 720928 | tf_op jit(solution)/shard_map/ppermute | solution.py:239
  24.0 0.2 shard_map.89
  24.2 22.8 %all_to_all.33 = bf16[16,176,128]{2,1,0:T(8,128)(2,1)S(1)} all-to-all(bf16[16,176,128]{2,1,0:T(8,128)(2,1)S(1)} %bitcast.9), channel_id=1, replica_groups={{0,1,32,33,64,65,96,97,128,129,160,161,192,193,224,225},{2,3,34,35,66,6..., dimensions={0} | all-to-all | bytes 1441792 | tf_op jit(solution)/shard_map/all_to_all | solution.py:252
  47.0 0.1 shard_map.90
  47.1 19.4 %all_to_all.34 = bf16[8,176,128]{2,1,0:T(8,128)(2,1)S(1)} all-to-all(bf16[8,176,128]{2,1,0:T(8,128)(2,1)S(1)} %bitcast.12), channel_id=1, replica_groups={{0,2,4,6,8,10,12,14},{1,3,5,7,9,11,13,15},{16,18,20,22,24,26,28,30},{17..., dimensions={0} | all-to-all | bytes 720896 | tf_op jit(solution)/shard_map/all_to_all | solution.py:252
  66.5 0.1 shard_map.91
  66.6 13.5 %all_to_all.35 = bf16[16,176,128]{2,1,0:T(8,128)(2,1)S(1)} all-to-all(bf16[16,176,128]{2,1,0:T(8,128)(2,1)S(1)} %bitcast.11), channel_id=1, replica_groups={{0,1,32,33,64,65,96,97,128,129,160,161,192,193,224,225},{2,3,34,35,66,6..., dimensions={0} | all-to-all | bytes 1441792 | tf_op jit(solution)/shard_map/all_to_all | solution.py:252
  80.0 5.1 %collective-permute-start.5 = (bf16[2816,128]{1,0:T(8,128)(2,1)S(1)}, bf16[2816,128]{1,0:T(8,128)(2,1)S(1)}, u32[]{:S(2)}, u32[]{:S(2)}) collective-permute-start(bf16[2816,128]{1,0:T(8,128)(2,1)S(1)} %bitcast.7), channel_id=1, source_target_pairs={{0,16},{16,0},{32,48},{48,32},{64,80},{80,64},{96,112},{112,96},{1... | collective-permute-start | bytes 2162696 | tf_op jit(solution)/shard_map/ppermute | solution.py:239
  85.1 2.1 %shard_map.88 = bf16[256,128]{1,0:T(8,128)(2,1)} custom-call(s32[1,256]{1,0:T(1,128)S(1)} %bitcast.16, bf16[864,128]{1,0:T(8,128)(2,1)S(1)} %get-tuple-element.27.grad_ref, bf16[27,128,128]{2,1,0:T(8,128)(2,1)S(1)} %copy-done), custom_call_target="tpu_custom_call" | custom-call | flops 1073741824 | bytes 1048576 | tf_op jit(solution)/shard_map/pallas_call | solution.py:288
  87.2 1.9 %shard_map.92 = (f32[27,128,128]{2,1,0:T(8,128)}, f32[1024,256]{1,0:T(8,128)}) custom-call(bf16[2816,128]{1,0:T(8,128)(2,1)S(1)} %bitcast.8, bf16[2816,128]{1,0:T(8,128)(2,1)S(1)} %collective-permute-done.5.other_ref), custom_call_target="tpu_custom_call" | custom-call | bytes 1048576 | tf_op jit(solution)/shard_map/pallas_call | solution.py:289
  (10 shorter events, 0.0 us)
Async XLA Ops:
  0.6 0.8 copy-start.3
  0.6 1.1 %copy-start.1 = (bf16[1024,256]{1,0:T(8,128)(2,1)S(1)}, bf16[1024,256]{1,0:T(8,128)(2,1)}, u32[]{:S(2)}) copy-start(bf16[1024,256]{1,0:T(8,128)(2,1)} %w_down_ref.1) | copy-start | bytes 1572868
  0.7 1.0 %copy-start.4 = (s32[256]{0:T(256)S(1)}, s32[256]{0:T(256)}, u32[]{:S(2)}) copy-start(s32[256]{0:T(256)} %param.11) | copy-start | bytes 3076
  0.7 1.0 %copy-start.2 = (bf16[256,128]{1,0:T(8,128)(2,1)S(1)}, bf16[256,128]{1,0:T(8,128)(2,1)}, u32[]{:S(2)}) copy-start(bf16[256,128]{1,0:T(8,128)(2,1)} %features.1) | copy-start | bytes 196612
  2.4 4.9 %collective-permute-start = (bf16[96,128]{1,0:T(8,128)(2,1)S(1)}, bf16[96,128]{1,0:T(8,128)(2,1)S(1)}, u32[]{:S(2)}, u32[]{:S(2)}) collective-permute-start(bf16[96,128]{1,0:T(8,128)(2,1)S(1)} %get-tuple-element.22), channel_id=1, source_target_pairs={{0,1},{1,0},{2,3},{3,2},{4,5},{5,4},{6,7},{7,6},{8,9},{9,8},{10,11... | collective-permute-start | bytes 73736 | tf_op jit(solution)/shard_map/ppermute | solution.py:34
  6.0 1.2 %collective-permute-start.1 = (bf16[96,128]{1,0:T(8,128)(2,1)S(1)}, bf16[96,128]{1,0:T(8,128)(2,1)S(1)}, u32[]{:S(2)}, u32[]{:S(2)}) collective-permute-start(bf16[96,128]{1,0:T(8,128)(2,1)S(1)} %get-tuple-element.23), channel_id=1, source_target_pairs={{1,2},{2,1},{3,4},{4,3},{5,6},{6,5},{7,8},{8,7},{9,10},{10,9},{11,... | collective-permute-start | bytes 73736 | tf_op jit(solution)/shard_map/ppermute | solution.py:33
  7.3 10.1 %copy-start = (bf16[27,128,128]{2,1,0:T(8,128)(2,1)S(1)}, bf16[27,128,128]{2,1,0:T(8,128)(2,1)}, u32[]{:S(2)}) copy-start(bf16[27,128,128]{2,1,0:T(8,128)(2,1)} %w_sub_ref.1) | copy-start | bytes 2654212
  7.3 5.8 %collective-permute-start.2 = (bf16[464,128]{1,0:T(8,128)(2,1)S(1)}, bf16[464,128]{1,0:T(8,128)(2,1)S(1)}, u32[]{:S(2)}, u32[]{:S(2)}) collective-permute-start(bf16[464,128]{1,0:T(8,128)(2,1)S(1)} %get-tuple-element.24), channel_id=1, source_target_pairs={{0,16},{16,0},{32,48},{48,32},{64,80},{80,64},{96,112},{112,96},{1... | collective-permute-start | bytes 356360 | tf_op jit(solution)/shard_map/ppermute | solution.py:34
  11.2 6.2 %collective-permute-start.3 = (bf16[464,128]{1,0:T(8,128)(2,1)S(1)}, bf16[464,128]{1,0:T(8,128)(2,1)S(1)}, u32[]{:S(2)}, u32[]{:S(2)}) collective-permute-start(bf16[464,128]{1,0:T(8,128)(2,1)S(1)} %get-tuple-element.25), channel_id=1, source_target_pairs={{16,32},{32,16},{48,64},{64,48},{80,96},{96,80},{112,128},{128,112... | collective-permute-start | bytes 356360 | tf_op jit(solution)/shard_map/ppermute | solution.py:33
  21.7 2.3 %collective-permute-start.4 = (bf16[2816,128]{1,0:T(8,128)(2,1)S(1)}, bf16[2816,128]{1,0:T(8,128)(2,1)S(1)}, u32[]{:S(2)}, u32[]{:S(2)}) collective-permute-start(bf16[2816,128]{1,0:T(8,128)(2,1)S(1)} %get-tuple-element.29), channel_id=1, source_target_pairs={{0,16},{16,0},{32,48},{48,32},{64,80},{80,64},{96,112},{112,96},{1... | collective-permute-start | bytes 2162696 | tf_op jit(solution)/shard_map/ppermute | solution.py:239
  80.0 7.1 %collective-permute-start.5 = (bf16[2816,128]{1,0:T(8,128)(2,1)S(1)}, bf16[2816,128]{1,0:T(8,128)(2,1)S(1)}, u32[]{:S(2)}, u32[]{:S(2)}) collective-permute-start(bf16[2816,128]{1,0:T(8,128)(2,1)S(1)} %bitcast.7), channel_id=1, source_target_pairs={{0,16},{16,0},{32,48},{48,32},{64,80},{80,64},{96,112},{112,96},{1... | collective-permute-start | bytes 2162696 | tf_op jit(solution)/shard_map/ppermute | solution.py:239

commit v3 on v2

--- a/solution.py
+++ b/solution.py
@@ -1,3 +1,5 @@
+import functools
+
 import jax
 import jax.numpy as jnp
 from jax import lax
@@ -102,15 +104,15 @@
     odd_ref[...] = pick(side, low, high).astype(BF16)
 
 
-def y_halos(even_ref, odd_ref):
+def y_halos(odd_ref, even_ref):
     even, odd = even_ref[...].astype(F32), odd_ref[...].astype(F32)
     side = parity("gy")
     return split_y(pick(side, odd, even)), split_y(pick(side, even, odd))
 
 
-def x_sides_kernel(grid_ref, hidden_ref, y_even_ref, y_odd_ref, even_ref, odd_ref):
+def x_sides_kernel(grid_ref, hidden_ref, y_odd_ref, y_even_ref, even_ref, odd_ref):
     plane = LY * LZ
-    (low, low_grad), (high, high_grad) = y_halos(y_even_ref, y_odd_ref)
+    (low, low_grad), (high, high_grad) = y_halos(y_odd_ref, y_even_ref)
 
     def face(planes, edge):
         rows = []
@@ -126,10 +128,10 @@
 
 
 def main_kernel(
-    place_ref, ids_ref, grid_ref, hidden_ref, y_even_ref, y_odd_ref, x_even_ref, x_odd_ref, cot_ref, w_down_ref, w_sub,
+    place_ref, ids_ref, grid_ref, hidden_ref, y_odd_ref, y_even_ref, x_odd_ref, x_even_ref, cot_ref, w_down_ref, w_sub,
     coarse_ref, grad_ref, own_ref, send_ref, padded, hidden_pad, sums,
 ):
-    (low, low_grad), (high, high_grad) = y_halos(y_even_ref, y_odd_ref)
+    (low, low_grad), (high, high_grad) = y_halos(y_odd_ref, y_even_ref)
     x_even, x_odd = x_even_ref[...].astype(F32), x_odd_ref[...].astype(F32)
     side = parity("gx")
     for rows, at in ((pick(side, x_odd, x_even), 0), (pick(side, x_even, x_odd), LX + 2)):
@@ -189,7 +191,8 @@
     return pl.ds(pl.multiple_of(core * HALF, HALF), HALF), pl.ds(pl.multiple_of((1 - core) * HALF, HALF), HALF)
 
 
-def feature_kernel(ids_ref, grad_ref, w_sub_ref, out_ref, padded):
+def feature_kernel(ids_ref, grad_ref, w_sub_ref, out_ref, done_ref, padded):
+    done_ref[...] = jnp.zeros_like(done_ref)
     padded[...] = grad_ref[...].astype(F32).reshape(LX + 2, LY + 2, LZ, C)
     parts = [jnp.zeros((CELLS, C), F32)] * 3
     for step_x in range(3):
@@ -215,23 +218,46 @@
         out_ref[start : start + CHUNK] = total
 
 
-def unpack_kernel(own_ref, other_ref, sub_ref, down_ref, sums):
-    mine, other = halves()
-    sums[mine] = own_ref[...].astype(F32)
-    sums[other] = other_ref[...].astype(F32)
-    base = OFFSETS * C
-    sub_ref[...] = sums[:base].reshape(OFFSETS, C, C)
-    down_ref[:, :C] = sums[base : base + 8 * C]
-    down_ref[:, C:] = sums[base + 8 * C : base + 16 * C]
-
-
-def call(kernel, outs, scratch=(), flops=0):
+def pair_kernel(own_ref, other_ref, *refs):
+    out_ref = refs[-1]
+    total = (own_ref[...].astype(F32) + other_ref[...].astype(F32)).astype(BF16)
+    for start in range(0, out_ref.shape[0], CHUNK):
+        out_ref[start : start + CHUNK] = total
+
+
+def unpack_kernel(other, data_ref, *refs):
+    sub_hbm, down_hbm, blocks, down, sems = refs[-5:]
+    held = parity("gx") ^ other
+    blocks[...] = data_ref[...].astype(F32).reshape(HALF // C, C, C)
+    first = HALF // C
+
+    @pl.when(held == 0)
+    def _():
+        copy = pltpu.make_async_copy(blocks, sub_hbm.at[:first], sems.at[0])
+        copy.start()
+        copy.wait()
+
+    @pl.when(held == 1)
+    def _():
+        rest = OFFSETS - first
+        copy = pltpu.make_async_copy(blocks.at[:rest], sub_hbm.at[first:], sems.at[0])
+        copy.start()
+        for k in range(2):
+            down[:, k * C : (k + 1) * C] = blocks[rest + 8 * k : rest + 8 * (k + 1)].reshape(8 * C, C)
+        second = pltpu.make_async_copy(down, down_hbm, sems.at[1])
+        second.start()
+        copy.wait()
+        second.wait()
+
+
+def call(kernel, outs, scratch=(), flops=0, **options):
     return pl.pallas_call(
         kernel,
         out_shape=[jax.ShapeDtypeStruct(*out) for out in outs],
         scratch_shapes=list(scratch),
         cost_estimate=pl.CostEstimate(flops=flops, bytes_accessed=1 << 20, transcendentals=0),
         compiler_params=pltpu.CompilerParams(vmem_limit_bytes=40 * 1024 * 1024),
+        **options,
     )
 
 
@@ -239,22 +265,25 @@
     return lax.ppermute(value, "gx", swap_pairs(lax.axis_size("gx"))[0])
 
 
-def reduce_all(own, send):
+def reduce_all(own, send, after):
     rows, cols = lax.axis_size("gx"), lax.axis_size("gy")
     plane = [
         [i * cols + j for i in range(core, rows, 2) for j in (first, first + 1)]
         for core in range(2)
         for first in range(0, cols, 2)
     ]
-    depth = [[i * cols + j for j in range(side, cols, 2)] for i in range(rows) for side in range(2)]
 
     def trade(value, groups):
         return lax.all_to_all(value, AXES, 0, 0, axis_index_groups=groups, tiled=True)
 
     packed = ((HALF, C), BF16)
     (part,) = call(add_kernel, [packed])(own, core_swap(send))
-    (mine,) = call(sum_kernel, [((len(depth[0]) * CHUNK, C), BF16)])(trade(part, plane))
-    (total,) = call(sum_kernel, [packed])(trade(mine, depth))
+    (total,) = call(sum_kernel, [((CHUNK, C), BF16)])(trade(part, plane))
+    for flip in (1, 2, 7):
+        pairs = [(j, ((j >> 1) ^ flip) * 2 + (j & 1)) for j in range(cols)]
+        copies = HALF if flip == 7 else CHUNK
+        extra = (after,) if flip == 2 else ()
+        (total,) = call(pair_kernel, [((copies, C), BF16)])(total, lax.ppermute(total, "gy", pairs), *extra)
     whole = trade(total, plane)
     return whole, core_swap(whole)
 
@@ -277,18 +306,28 @@
         from_corner, ids, features, cotangent, w_down
     )
     y_even, y_odd = swap_both(y_even, y_odd, "gy")
-    sides = call(x_sides_kernel, [x_side, x_side], flops=LONG)(grid, hidden_grad, y_even, y_odd)
+    sides = call(x_sides_kernel, [x_side, x_side], flops=LONG)(grid, hidden_grad, y_odd, y_even)
     x_even, x_odd = swap_both(*sides, "gx")
     coarse, grad, own, send = call(
         main_kernel,
         [((U_DEV, C2), BF16), frame, packed, packed],
         [padded, framed, sums],
         1 << 31,
-    )(to_corner, ids, grid, hidden_grad, y_even, y_odd, x_even, x_odd, cotangent, w_down, w_sub)
-    (feature_grad,) = call(feature_kernel, [((rows, C), BF16)], [framed], flops=1 << 30)(ids, grad, w_sub)
+    )(to_corner, ids, grid, hidden_grad, y_odd, y_even, x_odd, x_even, cotangent, w_down, w_sub)
+    feature_grad, done = call(feature_kernel, [((rows, C), BF16), ((16, C), BF16)], [framed], flops=LONG)(ids, grad, w_sub)
+    whole, other = reduce_all(own, send, done)
+    grads = [((OFFSETS, C, C), F32), ((8 * C, C2), F32)]
+    scratch = [pltpu.VMEM((HALF // C, C, C), F32), pltpu.VMEM((8 * C, C2), F32), pltpu.SemaphoreType.DMA((2,))]
+    in_hbm = [pl.BlockSpec(memory_space=pltpu.HBM)] * 2
+    grads_own = call(functools.partial(unpack_kernel, 0), grads, scratch, LONG, out_specs=in_hbm)(whole)
     sub_grad, down_grad = call(
-        unpack_kernel, [((OFFSETS, C, C), F32), ((8 * C, C2), F32)], [sums]
-    )(*reduce_all(own, send))
+        functools.partial(unpack_kernel, 1),
+        grads,
+        scratch,
+        in_specs=[pl.BlockSpec(memory_space=pltpu.VMEM), *in_hbm],
+        out_specs=in_hbm,
+        input_output_aliases={1: 0, 2: 1},
+    )(other, *grads_own)
     return coarse, feature_grad, sub_grad, down_grad
 
 

time: 89.3 us -> 83.6 us (0.936); the launches traced: 89.1 us -> 82.4 us
  blocking collectives: 55.7 us -> 34.7 us
  starting transfers between devices: 15.2 us -> 26.4 us
  waiting for transfers between devices: 6.98 us -> 9.61 us
    all_to_all x3 -> x2, blocking collectives: 55.7 us -> 34.7 us  [trade(): lax.all_to_all(value, AXES, 0, 0, axis_index_groups=groups, tiled=True)]
    ppermute x0 -> x3, starting transfers between devices: none -> 8.8 us  [reduce_all(): lax.ppermute(total, 'gy', pairs)]
    ppermute x2, starting transfers between devices: 2.56 us -> 5.62 us  [swap_both(): second = lax.ppermute(second, axis, odd)]
    ppermute x0 -> x3, waiting for transfers between devices: none -> 2.88 us  [reduce_all(): lax.ppermute(total, 'gy', pairs)]
    ppermute x2, waiting for transfers between devices: 4.23 us -> 2.72 us  [swap_both(): second = lax.ppermute(second, axis, odd)]
    ppermute x2, starting transfers between devices: 7.53 us -> 6.58 us  [swap_both(): return (lax.ppermute(first, axis, even), second)]
    pallas_call x4 -> x7, Pallas kernels: 4.15 us -> 4.65 us  [the longest x1 2.07 us: local(): call(feature_kernel, [((rows, C), BF16), ((16, C), BF16)], [framed], flop...]
  transfers between devices with their start and end apart: 6 -> 9, of which waited for: 3 -> 6; matrix products, arithmetic and copies ran while one was open for 0% -> 0% of each run, Pallas kernels for 2% -> 4%
where the time goes in v3:
time: 83.6 us; the launch traced here: 82.4 us
  blocking collectives  34.7 us (42%)
  starting transfers between devices  26.4 us (32%)
  Pallas kernels  10.3 us (12%)
  waiting for transfers between devices  9.61 us (11%)
    all_to_all x2, blocking collectives, trade(): lax.all_to_all(value, AXES, 0, 0, axis_index_groups=groups, tiled=True)  34.7 us
    ppermute x3, starting transfers between devices, reduce_all(): lax.ppermute(total, 'gy', pairs)  8.8 us
    ppermute x2, starting transfers between devices, swap_both(): return (lax.ppermute(first, axis, even), second)  6.58 us
    ppermute x2, starting transfers between devices, swap_both(): second = lax.ppermute(second, axis, odd)  5.62 us
    ppermute x2, starting transfers between devices, core_swap(): return lax.ppermute(value, 'gx', swap_pairs(lax.axis_size('gx'))[0])  5.42 us
    pallas_call x1, Pallas kernels, local(): call(main_kernel, [((U_DEV, C2), BF16), frame, packed, packed], [padded,...  4.34 us
    ppermute x3, waiting for transfers between devices, reduce_all(): lax.ppermute(total, 'gy', pairs)  2.88 us
    ppermute x2, waiting for transfers between devices, core_swap(): return lax.ppermute(value, 'gx', swap_pairs(lax.axis_size('gx'))[0])  2.8 us
  transfers between devices with their start and end apart: 9, of which 6 were waited for; matrix products, arithmetic and copies ran while one was open for 0% of the time, Pallas kernels for 4%

profile of v3, /device:TPU:1, one launch (start us, length us, event | category | flops | bytes accessed | tf_op | source)
XLA Modules:
  0.0 82.4 jit_solution(143347974407706965)
XLA Ops:
  0.7 0.4 shard_map.84
  1.1 0.3 copy-done.3
  1.4 0.3 copy-done.1
  1.7 0.7 shard_map.85
  2.4 0.7 collective-permute-start
  3.1 6.5 %collective-permute-start.1 = (bf16[96,128]{1,0:T(8,128)(2,1)S(1)}, bf16[96,128]{1,0:T(8,128)(2,1)S(1)}, u32[]{:S(2)}, u32[]{:S(2)}) collective-permute-start(bf16[96,128]{1,0:T(8,128)(2,1)S(1)} %get-tuple-element.27), channel_id=1, source_target_pairs={{0,1},{1,0},{2,3},{3,2},{4,5},{5,4},{6,7},{7,6},{8,9},{9,8},{10,11... | collective-permute-start | bytes 73736 | tf_op jit(solution)/shard_map/ppermute | solution.py:36
  9.5 1.2 %collective-permute-done.1.y_even_ref = bf16[96,128]{1,0:T(8,128)(2,1)S(1)} collective-permute-done((bf16[96,128]{1,0:T(8,128)(2,1)S(1)}, bf16[96,128]{1,0:T(8,128)(2,1)S(1)}, u32[]{:S(2)}, u32[]{:S(2)}) %collective-permute-start.1) | collective-permute-done | bytes 24608 | tf_op jit(solution)/shard_map/ppermute | solution.py:36
  10.8 5.0 %collective-permute-start.2 = (bf16[464,128]{1,0:T(8,128)(2,1)S(1)}, bf16[464,128]{1,0:T(8,128)(2,1)S(1)}, u32[]{:S(2)}, u32[]{:S(2)}) collective-permute-start(bf16[464,128]{1,0:T(8,128)(2,1)S(1)} %get-tuple-element.28), channel_id=1, source_target_pairs={{16,32},{32,16},{48,64},{64,48},{80,96},{96,80},{112,128},{128,112... | collective-permute-start | bytes 356360 | tf_op jit(solution)/shard_map/ppermute | solution.py:35
  15.9 2.7 %collective-permute-done.2.x_odd_ref = bf16[464,128]{1,0:T(8,128)(2,1)S(1)} collective-permute-done((bf16[464,128]{1,0:T(8,128)(2,1)S(1)}, bf16[464,128]{1,0:T(8,128)(2,1)S(1)}, u32[]{:S(2)}, u32[]{:S(2)}) %collective-permute-start.2) | collective-permute-done | bytes 118816 | tf_op jit(solution)/shard_map/ppermute | solution.py:35
  18.6 4.3 %shard_map.87 = (bf16[64,256]{1,0:T(8,128)(2,1)}, bf16[864,128]{1,0:T(8,128)(2,1)S(1)}, bf16[2816,128]{1,0:T(8,128)(2,1)S(1)}, bf16[2816,128]{1,0:T(8,128)(2,1)S(1)}) custom-call(bf16[512,512]{1,0:T(8,128)(2,1)S(1)} %get-tuple-element.22.place_ref, s32[1,256]{1,0:T(1,128)S(1)} %bitcast.11, bf16[512,128]{1,0:T(8,128)(2,1)S(1)} %get-tuple-element.24.grid_ref, ...), custom_call_target="tpu_custom_call" | custom-call | flops 2147483648 | bytes 1048576 | tf_op jit(solution)/shard_map/pallas_call | solution.py:311
  23.1 2.2 %collective-permute-done.4.other_ref = bf16[2816,128]{1,0:T(8,128)(2,1)S(1)} collective-permute-done((bf16[2816,128]{1,0:T(8,128)(2,1)S(1)}, bf16[2816,128]{1,0:T(8,128)(2,1)S(1)}, u32[]{:S(2)}, u32[]{:S(2)}) %collective-permute-start.4) | collective-permute-done | bytes 720928 | tf_op jit(solution)/shard_map/ppermute | solution.py:265
  25.2 0.2 shard_map.89
  25.4 21.2 %all_to_all.22 = bf16[16,176,128]{2,1,0:T(8,128)(2,1)S(1)} all-to-all(bf16[16,176,128]{2,1,0:T(8,128)(2,1)S(1)} %bitcast.5), channel_id=1, replica_groups={{0,1,32,33,64,65,96,97,128,129,160,161,192,193,224,225},{2,3,34,35,66,6..., dimensions={0} | all-to-all | bytes 1441792 | tf_op jit(solution)/shard_map/all_to_all | solution.py:277
  46.7 1.7 %collective-permute-start.5 = (bf16[176,128]{1,0:T(8,128)(2,1)S(1)}, bf16[176,128]{1,0:T(8,128)(2,1)S(1)}, u32[]{:S(2)}, u32[]{:S(2)}) collective-permute-start(bf16[176,128]{1,0:T(8,128)(2,1)S(1)} %shard_map.90.own_ref), channel_id=1, source_target_pairs={{0,2},{1,3},{2,0},{3,1},{4,6},{5,7},{6,4},{7,5},{8,10},{9,11},{10,... | collective-permute-start | bytes 135176 | tf_op jit(solution)/shard_map/ppermute | solution.py:286
  48.4 1.4 %collective-permute-done.5.other_ref = bf16[176,128]{1,0:T(8,128)(2,1)S(1)} collective-permute-done((bf16[176,128]{1,0:T(8,128)(2,1)S(1)}, bf16[176,128]{1,0:T(8,128)(2,1)S(1)}, u32[]{:S(2)}, u32[]{:S(2)}) %collective-permute-start.5) | collective-permute-done | bytes 45088 | tf_op jit(solution)/shard_map/ppermute | solution.py:286
  49.9 4.3 %collective-permute-start.6 = (bf16[176,128]{1,0:T(8,128)(2,1)S(1)}, bf16[176,128]{1,0:T(8,128)(2,1)S(1)}, u32[]{:S(2)}, u32[]{:S(2)}) collective-permute-start(bf16[176,128]{1,0:T(8,128)(2,1)S(1)} %shard_map.91.own_ref), channel_id=1, source_target_pairs={{0,4},{1,5},{2,6},{3,7},{4,0},{5,1},{6,2},{7,3},{8,12},{9,13},{10,... | collective-permute-start | bytes 135176 | tf_op jit(solution)/shard_map/ppermute | solution.py:286
  54.2 2.1 %shard_map.88 = (bf16[256,128]{1,0:T(8,128)(2,1)}, bf16[16,128]{1,0:T(8,128)(2,1)S(1)}) custom-call(s32[1,256]{1,0:T(1,128)S(1)} %bitcast.12, bf16[864,128]{1,0:T(8,128)(2,1)S(1)} %get-tuple-element.31.grad_ref, bf16[27,128,128]{2,1,0:T(8,128)(2,1)S(1)} %copy-done), custom_call_target="tpu_custom_call" | custom-call | flops 8589934592 | bytes 1048576 | tf_op jit(solution)/shard_map/pallas_call | solution.py:317
  56.3 2.8 %collective-permute-start.7 = (bf16[176,128]{1,0:T(8,128)(2,1)S(1)}, bf16[176,128]{1,0:T(8,128)(2,1)S(1)}, u32[]{:S(2)}, u32[]{:S(2)}) collective-permute-start(bf16[176,128]{1,0:T(8,128)(2,1)S(1)} %shard_map.92.own_ref), channel_id=1, source_target_pairs={{0,14},{1,15},{2,12},{3,13},{4,10},{5,11},{6,8},{7,9},{8,6},{9,7},... | collective-permute-start | bytes 135176 | tf_op jit(solution)/shard_map/ppermute | solution.py:286
  59.1 1.4 %collective-permute-done.7.other_ref = bf16[176,128]{1,0:T(8,128)(2,1)S(1)} collective-permute-done((bf16[176,128]{1,0:T(8,128)(2,1)S(1)}, bf16[176,128]{1,0:T(8,128)(2,1)S(1)}, u32[]{:S(2)}, u32[]{:S(2)}) %collective-permute-start.7) | collective-permute-done | bytes 45088 | tf_op jit(solution)/shard_map/ppermute | solution.py:286
  60.6 13.5 %all_to_all.23 = bf16[16,176,128]{2,1,0:T(8,128)(2,1)S(1)} all-to-all(bf16[16,176,128]{2,1,0:T(8,128)(2,1)S(1)} %bitcast.6), channel_id=1, replica_groups={{0,1,32,33,64,65,96,97,128,129,160,161,192,193,224,225},{2,3,34,35,66,6..., dimensions={0} | all-to-all | bytes 1441792 | tf_op jit(solution)/shard_map/all_to_all | solution.py:277
  74.1 5.3 %collective-permute-start.8 = (bf16[2816,128]{1,0:T(8,128)(2,1)S(1)}, bf16[2816,128]{1,0:T(8,128)(2,1)S(1)}, u32[]{:S(2)}, u32[]{:S(2)}) collective-permute-start(bf16[2816,128]{1,0:T(8,128)(2,1)S(1)} %bitcast.8), channel_id=1, source_target_pairs={{0,16},{16,0},{32,48},{48,32},{64,80},{80,64},{96,112},{112,96},{1... | collective-permute-start | bytes 2162696 | tf_op jit(solution)/shard_map/ppermute | solution.py:265
  79.4 1.2 %shard_map.94 = (f32[27,128,128]{2,1,0:T(8,128)}, f32[1024,256]{1,0:T(8,128)}) custom-call(bf16[2816,128]{1,0:T(8,128)(2,1)S(1)} %bitcast.9), custom_call_target="tpu_custom_call" | custom-call | flops 8589934592 | bytes 1048576 | tf_op jit(solution)/shard_map/pallas_call | solution.py:322
  80.6 0.6 collective-permute-done.8.data_ref
  81.2 1.2 %shard_map.95 = (f32[27,128,128]{2,1,0:T(8,128)}, f32[1024,256]{1,0:T(8,128)}) custom-call(bf16[2816,128]{1,0:T(8,128)(2,1)S(1)} %collective-permute-done.8.data_ref, f32[27,128,128]{2,1,0:T(8,128)} %get-tuple-element.36.refs_0_, f32[1024,256]{1,0:T(8,128)} %get-tuple-element.37.refs_1_), custom_call_target="tpu_custom_call", output_to_operand_aliasing={{0}: (1, {}), {1}: (2, {})} | custom-call | bytes 1048576 | tf_op jit(solution)/shard_map/pallas_call | solution.py:323
  (18 shorter events, 0.5 us)
Async XLA Ops:
  0.6 0.8 copy-start.3
  0.6 1.1 %copy-start.1 = (bf16[1024,256]{1,0:T(8,128)(2,1)S(1)}, bf16[1024,256]{1,0:T(8,128)(2,1)}, u32[]{:S(2)}) copy-start(bf16[1024,256]{1,0:T(8,128)(2,1)} %w_down_ref.1) | copy-start | bytes 1572868
  0.7 1.0 %copy-start.4 = (s32[256]{0:T(256)S(1)}, s32[256]{0:T(256)}, u32[]{:S(2)}) copy-start(s32[256]{0:T(256)} %param.11) | copy-start | bytes 3076
  0.7 1.0 %copy-start.2 = (bf16[256,128]{1,0:T(8,128)(2,1)S(1)}, bf16[256,128]{1,0:T(8,128)(2,1)}, u32[]{:S(2)}) copy-start(bf16[256,128]{1,0:T(8,128)(2,1)} %features.1) | copy-start | bytes 196612
  2.4 7.2 %collective-permute-start = (bf16[96,128]{1,0:T(8,128)(2,1)S(1)}, bf16[96,128]{1,0:T(8,128)(2,1)S(1)}, u32[]{:S(2)}, u32[]{:S(2)}) collective-permute-start(bf16[96,128]{1,0:T(8,128)(2,1)S(1)} %get-tuple-element.26), channel_id=1, source_target_pairs={{1,2},{2,1},{3,4},{4,3},{5,6},{6,5},{7,8},{8,7},{9,10},{10,9},{11,... | collective-permute-start | bytes 73736 | tf_op jit(solution)/shard_map/ppermute | solution.py:35
  3.1 7.7 %collective-permute-start.1 = (bf16[96,128]{1,0:T(8,128)(2,1)S(1)}, bf16[96,128]{1,0:T(8,128)(2,1)S(1)}, u32[]{:S(2)}, u32[]{:S(2)}) collective-permute-start(bf16[96,128]{1,0:T(8,128)(2,1)S(1)} %get-tuple-element.27), channel_id=1, source_target_pairs={{0,1},{1,0},{2,3},{3,2},{4,5},{5,4},{6,7},{7,6},{8,9},{9,8},{10,11... | collective-permute-start | bytes 73736 | tf_op jit(solution)/shard_map/ppermute | solution.py:36
  10.8 7.9 %copy-start = (bf16[27,128,128]{2,1,0:T(8,128)(2,1)S(1)}, bf16[27,128,128]{2,1,0:T(8,128)(2,1)}, u32[]{:S(2)}) copy-start(bf16[27,128,128]{2,1,0:T(8,128)(2,1)} %w_sub_ref.1) | copy-start | bytes 2654212
  10.8 7.8 %collective-permute-start.2 = (bf16[464,128]{1,0:T(8,128)(2,1)S(1)}, bf16[464,128]{1,0:T(8,128)(2,1)S(1)}, u32[]{:S(2)}, u32[]{:S(2)}) collective-permute-start(bf16[464,128]{1,0:T(8,128)(2,1)S(1)} %get-tuple-element.28), channel_id=1, source_target_pairs={{16,32},{32,16},{48,64},{64,48},{80,96},{96,80},{112,128},{128,112... | collective-permute-start | bytes 356360 | tf_op jit(solution)/shard_map/ppermute | solution.py:35
  15.8 2.8 %collective-permute-start.3 = (bf16[464,128]{1,0:T(8,128)(2,1)S(1)}, bf16[464,128]{1,0:T(8,128)(2,1)S(1)}, u32[]{:S(2)}, u32[]{:S(2)}) collective-permute-start(bf16[464,128]{1,0:T(8,128)(2,1)S(1)} %get-tuple-element.29), channel_id=1, source_target_pairs={{0,16},{16,0},{32,48},{48,32},{64,80},{80,64},{96,112},{112,96},{1... | collective-permute-start | bytes 356360 | tf_op jit(solution)/shard_map/ppermute | solution.py:36
  23.0 2.3 %collective-permute-start.4 = (bf16[2816,128]{1,0:T(8,128)(2,1)S(1)}, bf16[2816,128]{1,0:T(8,128)(2,1)S(1)}, u32[]{:S(2)}, u32[]{:S(2)}) collective-permute-start(bf16[2816,128]{1,0:T(8,128)(2,1)S(1)} %get-tuple-element.34), channel_id=1, source_target_pairs={{0,16},{16,0},{32,48},{48,32},{64,80},{80,64},{96,112},{112,96},{1... | collective-permute-start | bytes 2162696 | tf_op jit(solution)/shard_map/ppermute | solution.py:265
  46.7 3.2 %collective-permute-start.5 = (bf16[176,128]{1,0:T(8,128)(2,1)S(1)}, bf16[176,128]{1,0:T(8,128)(2,1)S(1)}, u32[]{:S(2)}, u32[]{:S(2)}) collective-permute-start(bf16[176,128]{1,0:T(8,128)(2,1)S(1)} %shard_map.90.own_ref), channel_id=1, source_target_pairs={{0,2},{1,3},{2,0},{3,1},{4,6},{5,7},{6,4},{7,5},{8,10},{9,11},{10,... | collective-permute-start | bytes 135176 | tf_op jit(solution)/shard_map/ppermute | solution.py:286
  49.9 6.4 %collective-permute-start.6 = (bf16[176,128]{1,0:T(8,128)(2,1)S(1)}, bf16[176,128]{1,0:T(8,128)(2,1)S(1)}, u32[]{:S(2)}, u32[]{:S(2)}) collective-permute-start(bf16[176,128]{1,0:T(8,128)(2,1)S(1)} %shard_map.91.own_ref), channel_id=1, source_target_pairs={{0,4},{1,5},{2,6},{3,7},{4,0},{5,1},{6,2},{7,3},{8,12},{9,13},{10,... | collective-permute-start | bytes 135176 | tf_op jit(solution)/shard_map/ppermute | solution.py:286
  56.3 4.2 %collective-permute-start.7 = (bf16[176,128]{1,0:T(8,128)(2,1)S(1)}, bf16[176,128]{1,0:T(8,128)(2,1)S(1)}, u32[]{:S(2)}, u32[]{:S(2)}) collective-permute-start(bf16[176,128]{1,0:T(8,128)(2,1)S(1)} %shard_map.92.own_ref), channel_id=1, source_target_pairs={{0,14},{1,15},{2,12},{3,13},{4,10},{5,11},{6,8},{7,9},{8,6},{9,7},... | collective-permute-start | bytes 135176 | tf_op jit(solution)/shard_map/ppermute | solution.py:286
  74.1 7.1 %collective-permute-start.8 = (bf16[2816,128]{1,0:T(8,128)(2,1)S(1)}, bf16[2816,128]{1,0:T(8,128)(2,1)S(1)}, u32[]{:S(2)}, u32[]{:S(2)}) collective-permute-start(bf16[2816,128]{1,0:T(8,128)(2,1)S(1)} %bitcast.8), channel_id=1, source_target_pairs={{0,16},{16,0},{32,48},{48,32},{64,80},{80,64},{96,112},{112,96},{1... | collective-permute-start | bytes 2162696 | tf_op jit(solution)/shard_map/ppermute | solution.py:265

commit v4 on v3

v4 whole, which is shorter than its diff:
```python
import functools

import jax
import jax.numpy as jnp
from jax import lax
from jax.experimental import pallas as pl
from jax.experimental.pallas import tpu as pltpu
from jax.sharding import PartitionSpec as P

LX = 4
LY = 16
LZ = 8
CELLS = LX * LY * LZ
U_DEV = 64
C = 128
C2 = 256
OFFSETS = 27
AXES = ("gx", "gy")
CHUNK = 176
HALF = 16 * CHUNK
LONG = 1 << 33

F32 = jnp.float32
BF16 = jnp.bfloat16


def swap_pairs(count):
    even = [(k, k ^ 1) for k in range(count)]
    odd = [(k, k + 1 if k % 2 else k - 1) for k in range(count)]
    return even, [(k, m) for k, m in odd if 0 <= m < count]


def swap(value, axis, kind):
    return lax.ppermute(value, axis, swap_pairs(lax.axis_size(axis))[kind])


def swap_both(first, second, axis):
    second = swap(second, axis, 1)
    return swap(first, axis, 0), second


def parity(axis):
    return lax.rem(lax.axis_index(axis), 2)


def pick(flag, when_zero, when_one):
    mask = jnp.full(when_zero.shape, flag, jnp.int32) == 0
    return jnp.where(mask, when_zero, when_one)


def dot(left, right, dims=((1,), (0,))):
    return lax.dot_general(left, right, (dims, ((), ())), preferred_element_type=F32)


def cell_onehot(ids):
    cells = lax.broadcasted_iota(jnp.int32, (CELLS, ids.shape[1]), 0)
    return jnp.where(cells == ids, 1.0, 0.0).astype(BF16)


def corner_onehot(row_axis):
    place = lax.broadcasted_iota(jnp.int32, (CELLS, CELLS), row_axis)
    cell = lax.broadcasted_iota(jnp.int32, (CELLS, CELLS), 1 - row_axis)
    corner, row = place >> 6, place & 63
    x = ((row >> 5) << 1) + (corner >> 2)
    y = (((row >> 2) & 7) << 1) + ((corner >> 1) & 1)
    z = ((row & 3) << 1) + (corner & 1)
    return jnp.where(((x * LY + y) * LZ + z) == cell, 1.0, 0.0).astype(BF16)


def shift_z(value, step):
    rows = value.shape[0]
    z = lax.broadcasted_iota(jnp.int32, value.shape, 0) & (LZ - 1)
    if step == 1:
        return jnp.where(z == 0, 0.0, pltpu.roll(value, 1, 0))
    return jnp.where(z == LZ - 1, 0.0, pltpu.roll(value, rows - 1, 0))


def y_sides(dense, hidden_grad):
    def face(near, edge):
        rows = [dense[:, near].reshape(2 * LX * LZ, C), hidden_grad[:, edge].reshape(LX * LZ, C)]
        return jnp.concatenate(rows, 0)

    return face(slice(0, 2), 0), face(slice(LY - 2, LY), LY - 1)


def split_y(rows):
    return rows[: 2 * LX * LZ].reshape(LX, 2 * LZ, C), rows[2 * LX * LZ :].reshape(LX, LZ, C)


def places_kernel(from_ref, to_ref):
    from_ref[...] = corner_onehot(1)
    to_ref[...] = corner_onehot(0)


def build_kernel(place_ref, ids, features, cot, w_down, grid_ref, hidden_ref, even_ref, odd_ref, x_odd_ref):
    onehot = cell_onehot(ids[...])
    dense = dot(onehot, features[...])
    active = dot(onehot, jnp.ones((onehot.shape[1], C), BF16)) > 0.5
    back_rows = dot(cot[...], w_down[...], ((1,), (1,))).astype(BF16)
    stacked = jnp.concatenate([back_rows[:, k * C : (k + 1) * C] for k in range(8)], 0)
    hidden_grad = jnp.where(active, dot(place_ref[...], stacked), 0.0)
    grid_ref[...] = dense.astype(BF16)
    hidden_ref[...] = hidden_grad.astype(BF16)
    low, high = y_sides(dense.reshape(LX, LY, LZ, C), hidden_grad.reshape(LX, LY, LZ, C))
    side = parity("gy")
    even_ref[...] = pick(side, high, low).astype(BF16)
    odd_ref[...] = pick(side, low, high).astype(BF16)
    first = x_face(dense, hidden_grad, 0)
    last = x_face(dense, hidden_grad, LX - 1)
    x_odd_ref[...] = pick(parity("gx"), first, last).astype(BF16)


def x_face(dense, hidden_grad, edge):
    plane = LY * LZ
    near = dense[: 2 * plane] if edge == 0 else dense[CELLS - 2 * plane :]
    return jnp.concatenate([near, hidden_grad[edge * plane : (edge + 1) * plane]], 0)


def y_halos(odd_ref, even_ref):
    even, odd = even_ref[...].astype(F32), odd_ref[...].astype(F32)
    side = parity("gy")
    return split_y(pick(side, odd, even)), split_y(pick(side, even, odd))


def x_sides_kernel(grid_ref, hidden_ref, y_odd_ref, y_even_ref, even_ref, odd_ref):
    (low, low_grad), (high, high_grad) = y_halos(y_odd_ref, y_even_ref)

    def corners(near, edge):
        rows = []
        for x in near:
            rows += [low[x], high[x]]
        return jnp.concatenate([*rows, low_grad[edge], high_grad[edge]], 0)

    first, last = corners((0, 1), 0), corners((LX - 2, LX - 1), LX - 1)
    dense, hidden_grad = grid_ref[...].astype(F32), hidden_ref[...].astype(F32)
    side = parity("gx")
    face = pick(side, x_face(dense, hidden_grad, LX - 1), x_face(dense, hidden_grad, 0))
    even_ref[...] = jnp.concatenate([face, pick(side, last, first)], 0).astype(BF16)
    odd_ref[...] = pick(side, first, last).astype(BF16)


def store_side(planes, rows):
    face, corner = 2 * LY * LZ, 3 * LY * LZ
    planes[:, 2 : LY + 2] = rows[:face].reshape(2, LY, LZ, C)
    ends = rows[corner : corner + 8 * LZ].reshape(2, 4, LZ, C)
    planes[:, 0:2] = ends[:, 0:2]
    planes[:, LY + 2 :] = ends[:, 2:4]
    grads = corner + 8 * LZ
    return jnp.concatenate([rows[grads : grads + LZ], rows[face:corner], rows[grads + LZ :]], 0)


def kernel_rows(w_sub, step_x):
    rows = []
    for step_y in range(3):
        first = step_x * 9 + step_y * 3
        rows.append(jnp.concatenate([w_sub[first + k] for k in range(3)], 1))
    return jnp.concatenate(rows, 0)


def frame_rows(planes):
    rows = planes.shape[0] * (LY + 2) * LZ
    return jnp.concatenate([planes[:, k : k + LY + 2].reshape(rows, C).astype(BF16) for k in range(3)], 1)


def fold(taps):
    return shift_z(taps[:, :C], 1) + taps[:, C : 2 * C] + shift_z(taps[:, 2 * C :], -1)


def unfold(grad):
    return jnp.concatenate([shift_z(grad, -1), grad, shift_z(grad, 1)], 1).astype(BF16)


def activate(pre_act, hidden_grad):
    sigmoid = 1.0 / (1.0 + jnp.exp(-pre_act))
    pre_grad = hidden_grad * sigmoid * (1.0 + pre_act * (1.0 - sigmoid))
    return pre_act * sigmoid, pre_grad.astype(BF16)


def inner_rows(value):
    return value[:, 1 : LY + 1].reshape(value.shape[0] * LY * LZ, C)


def early_kernel(grid_ref, hidden_ref, y_odd_ref, y_even_ref, w_sub, mid, hidden_mid, pre_ref, taps_ref):
    (low, low_grad), (high, high_grad) = y_halos(y_odd_ref, y_even_ref)
    mid[:, 0:2] = low.reshape(LX, 2, LZ, C)
    mid[:, LY + 2 :] = high.reshape(LX, 2, LZ, C)
    mid[:, 2 : LY + 2] = grid_ref[...].astype(F32).reshape(LX, LY, LZ, C)
    hidden_mid[:, 0] = low_grad
    hidden_mid[:, LY + 1] = high_grad
    hidden_mid[:, 1 : LY + 1] = hidden_ref[...].astype(F32).reshape(LX, LY, LZ, C)
    rows = frame_rows(mid[...])
    pre_ref[...] = jnp.zeros_like(pre_ref)
    for step_x in range(3):
        part = fold(dot(rows, kernel_rows(w_sub, step_x)))
        pre_ref[2 - step_x : 2 - step_x + LX] += part.reshape(LX, LY + 2, LZ, C)
    _, grad = activate(inner_rows(pre_ref[2:4]), inner_rows(hidden_mid[1:3]))
    spread = unfold(grad.astype(F32))
    for group in range(9):
        step_x, step_y = group // 3, group % 3
        window = mid[step_x : step_x + 2, step_y + 1 : step_y + 1 + LY].reshape(2 * LY * LZ, C)
        taps = dot(window.astype(BF16), spread, ((0,), (0,)))
        for k in range(3):
            taps_ref[(3 * group + k) * C : (3 * group + k + 1) * C] = taps[:, k * C : (k + 1) * C]


def store_half(half, out_ref, mid, side, spread_ref, hidden_ref, place_ref, cot, taps_ref):
    blocks = HALF // C

    def plane(x, step_y):
        source = side[x + 2 if x < 0 else x - 2] if x < 0 or x >= LX else mid[x]
        return source[step_y + 1 : step_y + 1 + LY].reshape(LY * LZ, C)

    for group in range(8) if half == 0 else (7, 8):
        step_x, step_y = group // 3, group % 3
        held = [k for k in range(3) if (3 * group + k) // blocks == half]
        window = jnp.concatenate([plane(step_x - 1, step_y), plane(LX + step_x - 2, step_y)], 0)
        spread = spread_ref[:, held[0] * C : (held[-1] + 1) * C]
        taps = dot(window.astype(BF16), spread, ((0,), (0,)))
        for k in held:
            block = 3 * group + k
            total = taps[:, (k - held[0]) * C : (k - held[0] + 1) * C] + taps_ref[block * C : (block + 1) * C]
            at = (block - half * blocks) * C
            out_ref[at : at + C] = total.astype(BF16)
    if half == 1:
        down = dot(coarse_rows(place_ref, hidden_ref), cot[...], ((0,), (0,))).astype(BF16)
        at = (OFFSETS - blocks) * C
        out_ref[at : at + 8 * C] = down[:, :C]
        out_ref[at + 8 * C : at + 16 * C] = down[:, C:]
        out_ref[at + 16 * C :] = jnp.zeros((HALF - at - 16 * C, C), BF16)


def coarse_rows(place_ref, hidden_ref):
    by_corner = dot(place_ref[...], hidden_ref[...]).astype(BF16)
    return jnp.concatenate([by_corner[k * U_DEV : (k + 1) * U_DEV] for k in range(8)], 1)


def store_of(other, out_ref, *refs):
    held = parity("gx") ^ other
    for half in range(2):
        pl.when(held == half)(functools.partial(store_half, half, out_ref, *refs))


def main_kernel(
    place_ref, ids_ref, mid, hidden_mid, pre_ref, taps_ref, x_odd_ref, x_ends_ref, x_even_ref, cot_ref, w_sub,
    send_ref, grad_ref, spread_ref, hidden_ref, side,
):
    x_odd = jnp.concatenate([x_odd_ref[...].astype(F32), x_ends_ref[...].astype(F32)], 0)
    x_even = x_even_ref[...].astype(F32)
    flag = parity("gx")
    low_grad = store_side(side.at[0:2], pick(flag, x_odd, x_even))
    high_grad = store_side(side.at[2:4], pick(flag, x_even, x_odd))
    column = (LY + 2) * LZ
    centre = kernel_rows(w_sub, 1)
    rows = frame_rows(side[0:2])
    outer = fold(dot(rows, kernel_rows(w_sub, 0)))
    first = pre_ref[0].reshape(column, C) + outer[:column] + fold(dot(rows[column:], centre))
    second = pre_ref[1].reshape(column, C) + outer[column:]
    rows = frame_rows(side[2:4])
    outer = fold(dot(rows, kernel_rows(w_sub, 2)))
    last = pre_ref[LX + 1].reshape(column, C) + outer[column:] + fold(dot(rows[:column], centre))
    before = pre_ref[LX].reshape(column, C) + outer[:column]
    pre_act = jnp.concatenate([first, second, pre_ref[2:LX].reshape(2 * column, C), before, last], 0)
    hidden_grad = jnp.concatenate([low_grad, hidden_mid[...].reshape(LX * column, C), high_grad], 0)
    hidden, pre_grad = activate(pre_act, hidden_grad)
    grad_ref[...] = pre_grad

    def framed(value):
        return value.reshape(LX + 2, LY + 2, LZ, C)

    grad = framed(pre_grad.astype(F32))
    spread_ref[...] = unfold(inner_rows(jnp.concatenate([grad[1:2], grad[LX : LX + 1]], 0)))
    active = dot(cell_onehot(ids_ref[...]), jnp.ones((ids_ref.shape[1], C), BF16)) > 0.5
    hidden_ref[...] = jnp.where(active, inner_rows(framed(hidden)[1 : LX + 1]), 0.0).astype(BF16)
    store_of(1, send_ref, mid, side, spread_ref, hidden_ref, place_ref, cot_ref, taps_ref)


def late_kernel(place_ref, mid, side, spread_ref, hidden_ref, cot_ref, taps_ref, w_down_ref, own_ref, coarse_ref):
    coarse_ref[...] = dot(coarse_rows(place_ref, hidden_ref), w_down_ref[...]).astype(BF16)
    store_of(0, own_ref, mid, side, spread_ref, hidden_ref, place_ref, cot_ref, taps_ref)


def feature_kernel(ids_ref, grad_ref, w_sub_ref, out_ref, done_ref, padded):
    done_ref[...] = jnp.zeros_like(done_ref)
    padded[...] = grad_ref[...].astype(F32).reshape(LX + 2, LY + 2, LZ, C)
    parts = [jnp.zeros((CELLS, C), F32)] * 3
    for step_x in range(3):
        for step_y in range(3):
            window = padded[2 - step_x : 2 - step_x + LX, 2 - step_y : 2 - step_y + LY]
            window = window.reshape(CELLS, C).astype(BF16)
            first = step_x * 9 + step_y * 3
            parts = [parts[k] + dot(window, w_sub_ref[first + k], ((1,), (1,))) for k in range(3)]
    total = shift_z(parts[0], -1) + parts[1] + shift_z(parts[2], 1)
    out_ref[...] = dot(cell_onehot(ids_ref[...]), total.astype(BF16), ((0,), (0,))).astype(BF16)


def add_kernel(own_ref, other_ref, out_ref):
    out_ref[...] = (own_ref[...].astype(F32) + other_ref[...].astype(F32)).astype(BF16)


def sum_kernel(parts_ref, out_ref):
    total = parts_ref[:CHUNK].astype(F32)
    for start in range(CHUNK, parts_ref.shape[0], CHUNK):
        total = total + parts_ref[start : start + CHUNK].astype(F32)
    total = total.astype(BF16)
    for start in range(0, out_ref.shape[0], CHUNK):
        out_ref[start : start + CHUNK] = total


def pair_kernel(own_ref, other_ref, *refs):
    out_ref = refs[-1]
    total = (own_ref[...].astype(F32) + other_ref[...].astype(F32)).astype(BF16)
    for start in range(0, out_ref.shape[0], CHUNK):
        out_ref[start : start + CHUNK] = total


def unpack_kernel(other, data_ref, *refs):
    sub_hbm, down_hbm, blocks, down, sems = refs[-5:]
    held = parity("gx") ^ other
    first = HALF // C
    rest = OFFSETS - first

    def widen(start, stop):
        rows = data_ref[start * C : stop * C].astype(F32)
        blocks[start:stop] = rows.reshape(stop - start, C, C)

    @pl.when(held == 0)
    def _():
        copies = []
        for k, (start, stop) in enumerate(((0, 6), (6, 12), (12, 17), (17, first))):
            widen(start, stop)
            copies.append(pltpu.make_async_copy(blocks.at[start:stop], sub_hbm.at[start:stop], sems.at[k]))
            copies[-1].start()
        for copy in copies:
            copy.wait()

    @pl.when(held == 1)
    def _():
        widen(0, rest)
        copies = [pltpu.make_async_copy(blocks.at[:rest], sub_hbm.at[first:], sems.at[0])]
        copies[0].start()
        for k, (start, stop) in enumerate(((0, 3), (3, 6), (6, 8))):
            for column in range(2):
                at = (rest + 8 * column + start) * C
                rows = data_ref[at : at + (stop - start) * C].astype(F32)
                down[start * C : stop * C, column * C : (column + 1) * C] = rows
            part = pl.ds(start * C, (stop - start) * C)
            copies.append(pltpu.make_async_copy(down.at[part], down_hbm.at[part], sems.at[k + 1]))
            copies[-1].start()
        for copy in copies:
            copy.wait()


def call(kernel, outs, scratch=(), flops=0, **options):
    return pl.pallas_call(
        kernel,
        out_shape=[jax.ShapeDtypeStruct(*out) for out in outs],
        scratch_shapes=list(scratch),
        cost_estimate=pl.CostEstimate(flops=flops, bytes_accessed=1 << 20, transcendentals=0),
        compiler_params=pltpu.CompilerParams(vmem_limit_bytes=40 * 1024 * 1024),
        **options,
    )


def reduce_all(own, send, after):
    rows, cols = lax.axis_size("gx"), lax.axis_size("gy")
    plane = [
        [i * cols + j for i in range(core, rows, 2) for j in (first, first + 1)]
        for core in range(2)
        for first in range(0, cols, 2)
    ]

    def trade(value, groups):
        return lax.all_to_all(value, AXES, 0, 0, axis_index_groups=groups, tiled=True)

    packed = ((HALF, C), BF16)
    (part,) = call(add_kernel, [packed])(own, swap(send, "gx", 0))
    (total,) = call(sum_kernel, [((CHUNK, C), BF16)])(trade(part, plane))
    for flip in (1, 2, 6):
        pairs = [(j, ((j >> 1) ^ flip) * 2 + (j & 1)) for j in range(cols)]
        copies = HALF if flip == 6 else CHUNK
        extra = (after,) if flip == 2 else ()
        (total,) = call(pair_kernel, [((copies, C), BF16)])(total, lax.ppermute(total, "gy", pairs), *extra)
    whole = trade(total, plane)
    return whole, swap(whole, "gx", 0)


def local(features, w_sub, w_down, cell_ids, send_rows, map_in, map_out, cotangent):
    ids = cell_ids[None]
    rows = features.shape[0]
    dense = ((CELLS, C), BF16)
    y_side = ((3 * LX * LZ, C), BF16)
    x_face_rows, x_ends = 3 * LY * LZ, 10 * LZ
    frame = (((LX + 2) * (LY + 2) * LZ, C), BF16)
    packed = ((HALF, C), BF16)
    framed = pltpu.VMEM((LX + 2, LY + 2, LZ, C), F32)

    place = ((CELLS, CELLS), BF16)
    from_corner, to_corner = call(places_kernel, [place, place], flops=LONG)()
    outs = [dense, dense, y_side, y_side, ((x_face_rows, C), BF16)]
    grid, hidden_grad, y_even, y_odd, x_odd = call(build_kernel, outs, flops=LONG)(
        from_corner, ids, features, cotangent, w_down
    )
    y_even, y_odd = swap_both(y_even, y_odd, "gy")
    x_odd = swap(x_odd, "gx", 1)
    outs = [((x_face_rows + x_ends, C), BF16), ((x_ends, C), BF16)]
    x_even, x_far = call(x_sides_kernel, outs, flops=LONG)(grid, hidden_grad, y_odd, y_even)
    x_even, x_far = swap_both(x_even, x_far, "gx")
    planes = (LX, LY + 4, LZ, C)
    early = call(
        early_kernel,
        [(planes, F32), ((LX, LY + 2, LZ, C), F32), ((LX + 2, LY + 2, LZ, C), F32), ((OFFSETS * C, C), F32)],
        flops=LONG,
    )(grid, hidden_grad, y_odd, y_even, w_sub)
    mid, taps = early[0], early[3]
    spread = ((2 * LY * LZ, 3 * C), BF16)
    send, grad, *kept = call(main_kernel, [packed, frame, spread, dense, (planes, F32)], flops=LONG)(
        to_corner, ids, *early, x_odd, x_far, x_even, cotangent, w_sub
    )
    spread, hidden, side = kept
    own, coarse = call(late_kernel, [packed, ((U_DEV, C2), BF16)], flops=LONG)(
        to_corner, mid, side, spread, hidden, cotangent, taps, w_down
    )
    feature_grad, done = call(feature_kernel, [((rows, C), BF16), ((16, C), BF16)], [framed], flops=LONG)(ids, grad, w_sub)
    whole, other = reduce_all(own, send, done)
    grads = [((OFFSETS, C, C), F32), ((8 * C, C2), F32)]
    scratch = [pltpu.VMEM((HALF // C, C, C), F32), pltpu.VMEM((8 * C, C2), F32), pltpu.SemaphoreType.DMA((4,))]
    in_hbm = [pl.BlockSpec(memory_space=pltpu.HBM)] * 2
    grads_own = call(functools.partial(unpack_kernel, 0), grads, scratch, LONG, out_specs=in_hbm)(whole)
    sub_grad, down_grad = call(
        functools.partial(unpack_kernel, 1),
        grads,
        scratch,
        in_specs=[pl.BlockSpec(memory_space=pltpu.VMEM), *in_hbm],
        out_specs=in_hbm,
        input_output_aliases={1: 0, 2: 1},
    )(other, *grads_own)
    return coarse, feature_grad, sub_grad, down_grad


def solution(mesh):
    rows = P(AXES, None)
    flat = P(AXES)
    maps = P(None, AXES)
    return jax.shard_map(
        local,
        mesh=mesh,
        in_specs=(rows, P(), P(), flat, flat, maps, maps, rows),
        out_specs=(rows, rows, P(), P()),
        check_vma=False,
    )
```

time: 83.6 us -> 79 us (0.945); the launches traced: 82.4 us -> 78.8 us
  waiting for transfers between devices: 9.61 us -> 5.65 us
  blocking collectives: 34.7 us -> 33.1 us
  starting transfers between devices: 26.4 us -> 28 us
    ppermute x6 -> x7, waiting for transfers between devices: 6.74 us -> 2.43 us  [swap(): return lax.ppermute(value, axis, swap_pairs(lax.axis_size(axis))[kind])]
    all_to_all x2, blocking collectives: 34.7 us -> 33.1 us  [trade(): lax.all_to_all(value, AXES, 0, 0, axis_index_groups=groups, tiled=True)]
    ppermute x6 -> x7, starting transfers between devices: 17.6 us -> 18.7 us  [swap(): return lax.ppermute(value, axis, swap_pairs(lax.axis_size(axis))[kind])]
    pallas_call x4 -> x6, Pallas kernels: 5.25 us -> 5.66 us  [the longest x1 1.9 us: local(): call(late_kernel, [packed, ((U_DEV, C2), BF16)], flops=LONG)]
  transfers between devices with their start and end apart: 9 -> 10, of which waited for: 6 -> 5; matrix products, arithmetic and copies ran while one was open for 0% -> 0% of each run, Pallas kernels for 4% -> 9%
where the time goes in v4:
time: 79 us; the launch traced here: 78.8 us
  blocking collectives  33.1 us (42%)
  starting transfers between devices  28 us (35%)
  Pallas kernels  10.6 us (13%)
  waiting for transfers between devices  5.65 us (7%)
  between operations  0.8 us (1%)
    all_to_all x2, blocking collectives, trade(): lax.all_to_all(value, AXES, 0, 0, axis_index_groups=groups, tiled=True)  33.1 us
    ppermute x7, starting transfers between devices, swap(): return lax.ppermute(value, axis, swap_pairs(lax.axis_size(axis))[kind])  18.7 us
    ppermute x3, starting transfers between devices, reduce_all(): lax.ppermute(total, 'gy', pairs)  9.34 us
    ppermute x3, waiting for transfers between devices, reduce_all(): lax.ppermute(total, 'gy', pairs)  3.22 us
    ppermute x7, waiting for transfers between devices, swap(): return lax.ppermute(value, axis, swap_pairs(lax.axis_size(axis))[kind])  2.43 us
    pallas_call x1, Pallas kernels, local(): call(feature_kernel, [((rows, C), BF16), ((16, C), BF16)], [framed], flop...  2.07 us
    pallas_call x1, Pallas kernels, local(): call(late_kernel, [packed, ((U_DEV, C2), BF16)], flops=LONG)  1.9 us
    pallas_call x1, Pallas kernels, local(): call(early_kernel, [(planes, F32), ((LX, LY + 2, LZ, C), F32), ((LX + 2,...  1.61 us
  transfers between devices with their start and end apart: 10, of which 5 were waited for; matrix products, arithmetic and copies ran while one was open for 0% of the time, Pallas kernels for 9%

profile of v4, /device:TPU:1, one launch (start us, length us, event | category | flops | bytes accessed | tf_op | source)
XLA Modules:
  0.0 78.8 jit_solution(16569660272282802293)
XLA Ops:
  0.7 0.4 shard_map.84
  1.1 0.3 copy-done.3
  1.4 0.3 copy-done.1
  1.7 0.7 shard_map.85
  2.4 0.7 collective-permute-start
  3.1 6.5 %collective-permute-start.1 = (bf16[96,128]{1,0:T(8,128)(2,1)S(1)}, bf16[96,128]{1,0:T(8,128)(2,1)S(1)}, u32[]{:S(2)}, u32[]{:S(2)}) collective-permute-start(bf16[96,128]{1,0:T(8,128)(2,1)S(1)} %get-tuple-element.35), channel_id=1, source_target_pairs={{0,1},{1,0},{2,3},{3,2},{4,5},{5,4},{6,7},{7,6},{8,9},{9,8},{10,11... | collective-permute-start | bytes 73736 | tf_op jit(solution)/shard_map/ppermute | solution.py:34
  9.5 4.2 %collective-permute-start.2 = (bf16[384,128]{1,0:T(8,128)(2,1)S(1)}, bf16[384,128]{1,0:T(8,128)(2,1)S(1)}, u32[]{:S(2)}, u32[]{:S(2)}) collective-permute-start(bf16[384,128]{1,0:T(8,128)(2,1)S(1)} %get-tuple-element.40), channel_id=1, source_target_pairs={{16,32},{32,16},{48,64},{64,48},{80,96},{96,80},{112,128},{128,112... | collective-permute-start | bytes 294920 | tf_op jit(solution)/shard_map/ppermute | solution.py:34
  13.9 2.1 %collective-permute-start.3 = (bf16[80,128]{1,0:T(8,128)(2,1)S(1)}, bf16[80,128]{1,0:T(8,128)(2,1)S(1)}, u32[]{:S(2)}, u32[]{:S(2)}) collective-permute-start(bf16[80,128]{1,0:T(8,128)(2,1)S(1)} %get-tuple-element.41), channel_id=1, source_target_pairs={{16,32},{32,16},{48,64},{64,48},{80,96},{96,80},{112,128},{128,112... | collective-permute-start | bytes 61448 | tf_op jit(solution)/shard_map/ppermute | solution.py:34
  16.0 1.6 %shard_map.86 = (f32[4,20,8,128]{3,2,1,0:T(8,128)S(1)}, f32[4,18,8,128]{3,2,1,0:T(8,128)S(1)}, f32[6,18,8,128]{3,2,1,0:T(8,128)S(1)}, f32[3456,128]{1,0:T(8,128)S(1)}) custom-call(bf16[512,128]{1,0:T(8,128)(2,1)S(1)} %get-tuple-element.32.grid_ref, bf16[512,128]{1,0:T(8,128)(2,1)S(1)} %get-tuple-element.33.hidden_ref, ...), custom_call_target="tpu_custom_call" | custom-call | flops 8589934592 | bytes 1048576 | tf_op jit(solution)/shard_map/pallas_call | solution.py:409
  17.6 1.5 %collective-permute-done.3.x_ends_ref = bf16[80,128]{1,0:T(8,128)(2,1)S(1)} collective-permute-done((bf16[80,128]{1,0:T(8,128)(2,1)S(1)}, bf16[80,128]{1,0:T(8,128)(2,1)S(1)}, u32[]{:S(2)}, u32[]{:S(2)}) %collective-permute-start.3) | collective-permute-done | bytes 20512 | tf_op jit(solution)/shard_map/ppermute | solution.py:34
  19.1 1.3 %shard_map.88 = (bf16[2816,128]{1,0:T(8,128)(2,1)S(1)}, bf16[864,128]{1,0:T(8,128)(2,1)S(1)}, bf16[256,384]{1,0:T(8,128)(2,1)S(1)}, bf16[512,128]{1,0:T(8,128)(2,1)S(1)}, f32[4,20,8,128]{3,2,1,0:T(8,128)S(1)}) custom-call(bf16[512,512]{1,0:T(8,128)(2,1)S(1)} %get-tuple-element.30.place_ref, s32[1,256]{1,0:T(1,128)S(1)} %bitcast.11, ...), custom_call_target="tpu_custom_call" | custom-call | flops 8589934592 | bytes 1048576 | tf_op jit(solution)/shard_map/pallas_call | solution.py:416
  20.5 1.9 %shard_map.89 = (bf16[2816,128]{1,0:T(8,128)(2,1)S(1)}, bf16[64,256]{1,0:T(8,128)(2,1)}) custom-call(bf16[512,512]{1,0:T(8,128)(2,1)S(1)} %get-tuple-element.30.place_ref, f32[4,20,8,128]{3,2,1,0:T(8,128)S(1)} %get-tuple-element.36.mid, f32[4,20,8,128]{3,2,1,0:T(8,128)S(1)} %get-tuple-element.43.side, bf16[256,384]{1,0:T(8,128)(2,1)S(1)} %get-tuple-element.44.spread_ref, ...), custom_call_target="tpu_custom_call" | custom-call | flops 8589934592 | bytes 1048576 | tf_op jit(solution)/shard_map/pallas_call | solution.py:420
  22.8 19.2 %all_to_all.22 = bf16[16,176,128]{2,1,0:T(8,128)(2,1)S(1)} all-to-all(bf16[16,176,128]{2,1,0:T(8,128)(2,1)S(1)} %bitcast.5), channel_id=1, replica_groups={{0,1,32,33,64,65,96,97,128,129,160,161,192,193,224,225},{2,3,34,35,66,6..., dimensions={0} | all-to-all | bytes 1441792 | tf_op jit(solution)/shard_map/all_to_all | solution.py:373
  42.1 1.7 %collective-permute-start.6 = (bf16[176,128]{1,0:T(8,128)(2,1)S(1)}, bf16[176,128]{1,0:T(8,128)(2,1)S(1)}, u32[]{:S(2)}, u32[]{:S(2)}) collective-permute-start(bf16[176,128]{1,0:T(8,128)(2,1)S(1)} %shard_map.92.own_ref), channel_id=1, source_target_pairs={{0,2},{1,3},{2,0},{3,1},{4,6},{5,7},{6,4},{7,5},{8,10},{9,11},{10,... | collective-permute-start | bytes 135176 | tf_op jit(solution)/shard_map/ppermute | solution.py:382
  43.8 1.4 %collective-permute-done.6.other_ref = bf16[176,128]{1,0:T(8,128)(2,1)S(1)} collective-permute-done((bf16[176,128]{1,0:T(8,128)(2,1)S(1)}, bf16[176,128]{1,0:T(8,128)(2,1)S(1)}, u32[]{:S(2)}, u32[]{:S(2)}) %collective-permute-start.6) | collective-permute-done | bytes 45088 | tf_op jit(solution)/shard_map/ppermute | solution.py:382
  45.3 4.3 %collective-permute-start.7 = (bf16[176,128]{1,0:T(8,128)(2,1)S(1)}, bf16[176,128]{1,0:T(8,128)(2,1)S(1)}, u32[]{:S(2)}, u32[]{:S(2)}) collective-permute-start(bf16[176,128]{1,0:T(8,128)(2,1)S(1)} %shard_map.93.own_ref), channel_id=1, source_target_pairs={{0,4},{1,5},{2,6},{3,7},{4,0},{5,1},{6,2},{7,3},{8,12},{9,13},{10,... | collective-permute-start | bytes 135176 | tf_op jit(solution)/shard_map/ppermute | solution.py:382
  49.6 2.1 %shard_map.90 = (bf16[256,128]{1,0:T(8,128)(2,1)}, bf16[16,128]{1,0:T(8,128)(2,1)S(1)}) custom-call(s32[1,256]{1,0:T(1,128)S(1)} %bitcast.12, bf16[864,128]{1,0:T(8,128)(2,1)S(1)} %get-tuple-element.47.grad_ref, bf16[27,128,128]{2,1,0:T(8,128)(2,1)S(1)} %copy-done), custom_call_target="tpu_custom_call" | custom-call | flops 8589934592 | bytes 1048576 | tf_op jit(solution)/shard_map/pallas_call | solution.py:423
  51.6 3.3 %collective-permute-start.8 = (bf16[176,128]{1,0:T(8,128)(2,1)S(1)}, bf16[176,128]{1,0:T(8,128)(2,1)S(1)}, u32[]{:S(2)}, u32[]{:S(2)}) collective-permute-start(bf16[176,128]{1,0:T(8,128)(2,1)S(1)} %shard_map.94.own_ref), channel_id=1, source_target_pairs={{0,12},{1,13},{2,14},{3,15},{4,8},{5,9},{6,10},{7,11},{8,4},{9,5},... | collective-permute-start | bytes 135176 | tf_op jit(solution)/shard_map/ppermute | solution.py:382
  55.0 1.8 %collective-permute-done.8.other_ref = bf16[176,128]{1,0:T(8,128)(2,1)S(1)} collective-permute-done((bf16[176,128]{1,0:T(8,128)(2,1)S(1)}, bf16[176,128]{1,0:T(8,128)(2,1)S(1)}, u32[]{:S(2)}, u32[]{:S(2)}) %collective-permute-start.8) | collective-permute-done | bytes 45088 | tf_op jit(solution)/shard_map/ppermute | solution.py:382
  56.8 13.9 %all_to_all.23 = bf16[16,176,128]{2,1,0:T(8,128)(2,1)S(1)} all-to-all(bf16[16,176,128]{2,1,0:T(8,128)(2,1)S(1)} %bitcast.6), channel_id=1, replica_groups={{0,1,32,33,64,65,96,97,128,129,160,161,192,193,224,225},{2,3,34,35,66,6..., dimensions={0} | all-to-all | bytes 1441792 | tf_op jit(solution)/shard_map/all_to_all | solution.py:373
  70.7 5.1 %collective-permute-start.9 = (bf16[2816,128]{1,0:T(8,128)(2,1)S(1)}, bf16[2816,128]{1,0:T(8,128)(2,1)S(1)}, u32[]{:S(2)}, u32[]{:S(2)}) collective-permute-start(bf16[2816,128]{1,0:T(8,128)(2,1)S(1)} %bitcast.8), channel_id=1, source_target_pairs={{0,16},{16,0},{32,48},{48,32},{64,80},{80,64},{96,112},{112,96},{1... | collective-permute-start | bytes 2162696 | tf_op jit(solution)/shard_map/ppermute | solution.py:34
  75.8 1.1 %shard_map.96 = (f32[27,128,128]{2,1,0:T(8,128)}, f32[1024,256]{1,0:T(8,128)}) custom-call(bf16[2816,128]{1,0:T(8,128)(2,1)S(1)} %bitcast.9), custom_call_target="tpu_custom_call" | custom-call | flops 8589934592 | bytes 1048576 | tf_op jit(solution)/shard_map/pallas_call | solution.py:428
  76.9 0.7 collective-permute-done.9.data_ref
  77.6 1.1 %shard_map.97 = (f32[27,128,128]{2,1,0:T(8,128)}, f32[1024,256]{1,0:T(8,128)}) custom-call(bf16[2816,128]{1,0:T(8,128)(2,1)S(1)} %collective-permute-done.9.data_ref, f32[27,128,128]{2,1,0:T(8,128)} %get-tuple-element.52.refs_0_, f32[1024,256]{1,0:T(8,128)} %get-tuple-element.53.refs_1_), custom_call_target="tpu_custom_call", output_to_operand_aliasing={{0}: (1, {}), {1}: (2, {})} | custom-call | bytes 1048576 | tf_op jit(solution)/shard_map/pallas_call | solution.py:429
  (22 shorter events, 0.9 us)
Async XLA Ops:
  0.6 0.8 copy-start.3
  0.6 1.1 %copy-start.1 = (bf16[1024,256]{1,0:T(8,128)(2,1)S(1)}, bf16[1024,256]{1,0:T(8,128)(2,1)}, u32[]{:S(2)}) copy-start(bf16[1024,256]{1,0:T(8,128)(2,1)} %w_down_ref.1) | copy-start | bytes 1572868
  0.7 1.0 %copy-start.4 = (s32[256]{0:T(256)S(1)}, s32[256]{0:T(256)}, u32[]{:S(2)}) copy-start(s32[256]{0:T(256)} %param.11) | copy-start | bytes 3076
  0.7 1.0 %copy-start.2 = (bf16[256,128]{1,0:T(8,128)(2,1)S(1)}, bf16[256,128]{1,0:T(8,128)(2,1)}, u32[]{:S(2)}) copy-start(bf16[256,128]{1,0:T(8,128)(2,1)} %features.1) | copy-start | bytes 196612
  2.4 11.4 %collective-permute-start = (bf16[96,128]{1,0:T(8,128)(2,1)S(1)}, bf16[96,128]{1,0:T(8,128)(2,1)S(1)}, u32[]{:S(2)}, u32[]{:S(2)}) collective-permute-start(bf16[96,128]{1,0:T(8,128)(2,1)S(1)} %get-tuple-element.34), channel_id=1, source_target_pairs={{1,2},{2,1},{3,4},{4,3},{5,6},{6,5},{7,8},{8,7},{9,10},{10,9},{11,... | collective-permute-start | bytes 73736 | tf_op jit(solution)/shard_map/ppermute | solution.py:34
  3.1 10.7 %collective-permute-start.1 = (bf16[96,128]{1,0:T(8,128)(2,1)S(1)}, bf16[96,128]{1,0:T(8,128)(2,1)S(1)}, u32[]{:S(2)}, u32[]{:S(2)}) collective-permute-start(bf16[96,128]{1,0:T(8,128)(2,1)S(1)} %get-tuple-element.35), channel_id=1, source_target_pairs={{0,1},{1,0},{2,3},{3,2},{4,5},{5,4},{6,7},{7,6},{8,9},{9,8},{10,11... | collective-permute-start | bytes 73736 | tf_op jit(solution)/shard_map/ppermute | solution.py:34
  9.5 9.6 %collective-permute-start.2 = (bf16[384,128]{1,0:T(8,128)(2,1)S(1)}, bf16[384,128]{1,0:T(8,128)(2,1)S(1)}, u32[]{:S(2)}, u32[]{:S(2)}) collective-permute-start(bf16[384,128]{1,0:T(8,128)(2,1)S(1)} %get-tuple-element.40), channel_id=1, source_target_pairs={{16,32},{32,16},{48,64},{64,48},{80,96},{96,80},{112,128},{128,112... | collective-permute-start | bytes 294920 | tf_op jit(solution)/shard_map/ppermute | solution.py:34
  13.8 2.2 %copy-start = (bf16[27,128,128]{2,1,0:T(8,128)(2,1)S(1)}, bf16[27,128,128]{2,1,0:T(8,128)(2,1)}, u32[]{:S(2)}) copy-start(bf16[27,128,128]{2,1,0:T(8,128)(2,1)} %w_sub_ref.1) | copy-start | bytes 2654212
  13.9 5.2 %collective-permute-start.3 = (bf16[80,128]{1,0:T(8,128)(2,1)S(1)}, bf16[80,128]{1,0:T(8,128)(2,1)S(1)}, u32[]{:S(2)}, u32[]{:S(2)}) collective-permute-start(bf16[80,128]{1,0:T(8,128)(2,1)S(1)} %get-tuple-element.41), channel_id=1, source_target_pairs={{16,32},{32,16},{48,64},{64,48},{80,96},{96,80},{112,128},{128,112... | collective-permute-start | bytes 61448 | tf_op jit(solution)/shard_map/ppermute | solution.py:34
  15.9 3.2 %collective-permute-start.4 = (bf16[464,128]{1,0:T(8,128)(2,1)S(1)}, bf16[464,128]{1,0:T(8,128)(2,1)S(1)}, u32[]{:S(2)}, u32[]{:S(2)}) collective-permute-start(bf16[464,128]{1,0:T(8,128)(2,1)S(1)} %get-tuple-element.42), channel_id=1, source_target_pairs={{0,16},{16,0},{32,48},{48,32},{64,80},{80,64},{96,112},{112,96},{1... | collective-permute-start | bytes 356360 | tf_op jit(solution)/shard_map/ppermute | solution.py:34
  20.4 2.3 %collective-permute-start.5 = (bf16[2816,128]{1,0:T(8,128)(2,1)S(1)}, bf16[2816,128]{1,0:T(8,128)(2,1)S(1)}, u32[]{:S(2)}, u32[]{:S(2)}) collective-permute-start(bf16[2816,128]{1,0:T(8,128)(2,1)S(1)} %get-tuple-element.50), channel_id=1, source_target_pairs={{0,16},{16,0},{32,48},{48,32},{64,80},{80,64},{96,112},{112,96},{1... | collective-permute-start | bytes 2162696 | tf_op jit(solution)/shard_map/ppermute | solution.py:34
  42.1 3.2 %collective-permute-start.6 = (bf16[176,128]{1,0:T(8,128)(2,1)S(1)}, bf16[176,128]{1,0:T(8,128)(2,1)S(1)}, u32[]{:S(2)}, u32[]{:S(2)}) collective-permute-start(bf16[176,128]{1,0:T(8,128)(2,1)S(1)} %shard_map.92.own_ref), channel_id=1, source_target_pairs={{0,2},{1,3},{2,0},{3,1},{4,6},{5,7},{6,4},{7,5},{8,10},{9,11},{10,... | collective-permute-start | bytes 135176 | tf_op jit(solution)/shard_map/ppermute | solution.py:382
  45.3 6.4 %collective-permute-start.7 = (bf16[176,128]{1,0:T(8,128)(2,1)S(1)}, bf16[176,128]{1,0:T(8,128)(2,1)S(1)}, u32[]{:S(2)}, u32[]{:S(2)}) collective-permute-start(bf16[176,128]{1,0:T(8,128)(2,1)S(1)} %shard_map.93.own_ref), channel_id=1, source_target_pairs={{0,4},{1,5},{2,6},{3,7},{4,0},{5,1},{6,2},{7,3},{8,12},{9,13},{10,... | collective-permute-start | bytes 135176 | tf_op jit(solution)/shard_map/ppermute | solution.py:382
  51.6 5.1 %collective-permute-start.8 = (bf16[176,128]{1,0:T(8,128)(2,1)S(1)}, bf16[176,128]{1,0:T(8,128)(2,1)S(1)}, u32[]{:S(2)}, u32[]{:S(2)}) collective-permute-start(bf16[176,128]{1,0:T(8,128)(2,1)S(1)} %shard_map.94.own_ref), channel_id=1, source_target_pairs={{0,12},{1,13},{2,14},{3,15},{4,8},{5,9},{6,10},{7,11},{8,4},{9,5},... | collective-permute-start | bytes 135176 | tf_op jit(solution)/shard_map/ppermute | solution.py:382
  70.7 6.9 %collective-permute-start.9 = (bf16[2816,128]{1,0:T(8,128)(2,1)S(1)}, bf16[2816,128]{1,0:T(8,128)(2,1)S(1)}, u32[]{:S(2)}, u32[]{:S(2)}) collective-permute-start(bf16[2816,128]{1,0:T(8,128)(2,1)S(1)} %bitcast.8), channel_id=1, source_target_pairs={{0,16},{16,0},{32,48},{48,32},{64,80},{80,64},{96,112},{112,96},{1... | collective-permute-start | bytes 2162696 | tf_op jit(solution)/shard_map/ppermute | solution.py:34

commit v5 on v4

--- a/solution.py
+++ b/solution.py
@@ -16,8 +16,9 @@
 C2 = 256
 OFFSETS = 27
 AXES = ("gx", "gy")
-CHUNK = 176
-HALF = 16 * CHUNK
+PEERS = 32
+CHUNK = 88
+HALF = PEERS * CHUNK
 LONG = 1 << 33
 
 F32 = jnp.float32
@@ -298,19 +299,20 @@
 
 
 def sum_kernel(parts_ref, out_ref):
-    total = parts_ref[:CHUNK].astype(F32)
-    for start in range(CHUNK, parts_ref.shape[0], CHUNK):
-        total = total + parts_ref[start : start + CHUNK].astype(F32)
-    total = total.astype(BF16)
-    for start in range(0, out_ref.shape[0], CHUNK):
-        out_ref[start : start + CHUNK] = total
+    total = parts_ref[0].astype(F32)
+    for k in range(1, PEERS):
+        total = total + parts_ref[k].astype(F32)
+    out_ref[...] = total.astype(BF16)
 
 
 def pair_kernel(own_ref, other_ref, *refs):
     out_ref = refs[-1]
     total = (own_ref[...].astype(F32) + other_ref[...].astype(F32)).astype(BF16)
-    for start in range(0, out_ref.shape[0], CHUNK):
-        out_ref[start : start + CHUNK] = total
+    if len(out_ref.shape) == 2:
+        out_ref[...] = total
+    else:
+        for k in range(PEERS):
+            out_ref[k] = total
 
 
 def unpack_kernel(other, data_ref, *refs):
@@ -363,24 +365,22 @@
 
 def reduce_all(own, send, after):
     rows, cols = lax.axis_size("gx"), lax.axis_size("gy")
-    plane = [
-        [i * cols + j for i in range(core, rows, 2) for j in (first, first + 1)]
+    blocks = [
+        [i * cols + j for i in range(core, rows, 2) for j in range(first, first + 4)]
         for core in range(2)
-        for first in range(0, cols, 2)
+        for first in range(0, cols, 4)
     ]
 
-    def trade(value, groups):
-        return lax.all_to_all(value, AXES, 0, 0, axis_index_groups=groups, tiled=True)
-
-    packed = ((HALF, C), BF16)
-    (part,) = call(add_kernel, [packed])(own, swap(send, "gx", 0))
-    (total,) = call(sum_kernel, [((CHUNK, C), BF16)])(trade(part, plane))
-    for flip in (1, 2, 6):
+    def trade(value):
+        return lax.all_to_all(value, AXES, 0, 0, axis_index_groups=blocks, tiled=True)
+
+    chunk = (CHUNK, C)
+    (part,) = call(add_kernel, [((HALF, C), BF16)])(own, swap(send, "gx", 0))
+    (total,) = call(sum_kernel, [(chunk, BF16)])(trade(part.reshape(PEERS, *chunk)))
+    for flip, shape, extra in ((2, chunk, (after,)), (6, (PEERS, *chunk), ())):
         pairs = [(j, ((j >> 1) ^ flip) * 2 + (j & 1)) for j in range(cols)]
-        copies = HALF if flip == 6 else CHUNK
-        extra = (after,) if flip == 2 else ()
-        (total,) = call(pair_kernel, [((copies, C), BF16)])(total, lax.ppermute(total, "gy", pairs), *extra)
-    whole = trade(total, plane)
+        (total,) = call(pair_kernel, [(shape, BF16)])(total, lax.ppermute(total, "gy", pairs), *extra)
+    whole = trade(total).reshape(HALF, C)
     return whole, swap(whole, "gx", 0)
 
 

time: 79 us -> 78.1 us (0.989)
  starting transfers between devices: 28 us -> 24.3 us
  blocking collectives: 33.1 us -> 36.5 us
    all_to_all x2, blocking collectives: 33.1 us -> 36.5 us  [trade(): lax.all_to_all(value, AXES, 0, 0, axis_index_groups=blocks, tiled=True)]
    ppermute x3 -> x2, starting transfers between devices: 9.34 us -> 6.53 us  [reduce_all(): lax.ppermute(total, 'gy', pairs)]
    ppermute x7, starting transfers between devices: 18.7 us -> 17.8 us  [swap(): return lax.ppermute(value, axis, swap_pairs(lax.axis_size(axis))[kind])]
    ppermute x3 -> x2, waiting for transfers between devices: 3.22 us -> 2.62 us  [reduce_all(): lax.ppermute(total, 'gy', pairs)]
  transfers between devices with their start and end apart: 10 -> 9, of which waited for: 5 -> 4; matrix products, arithmetic and copies ran while one was open for 0% -> 0% of each run, Pallas kernels for 9% -> 9%
where the time goes in v5:
time: 78.1 us; the launch traced here: 77.9 us
  blocking collectives  36.5 us (47%)
  starting transfers between devices  24.3 us (31%)
  Pallas kernels  10.6 us (14%)
  waiting for transfers between devices  5.05 us (6%)
  between operations  0.79 us (1%)
    all_to_all x2, blocking collectives, trade(): lax.all_to_all(value, AXES, 0, 0, axis_index_groups=blocks, tiled=True)  36.5 us
    ppermute x7, starting transfers between devices, swap(): return lax.ppermute(value, axis, swap_pairs(lax.axis_size(axis))[kind])  17.8 us
    ppermute x2, starting transfers between devices, reduce_all(): lax.ppermute(total, 'gy', pairs)  6.53 us
    ppermute x2, waiting for transfers between devices, reduce_all(): lax.ppermute(total, 'gy', pairs)  2.62 us
    ppermute x7, waiting for transfers between devices, swap(): return lax.ppermute(value, axis, swap_pairs(lax.axis_size(axis))[kind])  2.43 us
    pallas_call x1, Pallas kernels, local(): call(feature_kernel, [((rows, C), BF16), ((16, C), BF16)], [framed], flop...  2.07 us
    pallas_call x1, Pallas kernels, local(): call(late_kernel, [packed, ((U_DEV, C2), BF16)], flops=LONG)  1.9 us
    pallas_call x1, Pallas kernels, local(): call(early_kernel, [(planes, F32), ((LX, LY + 2, LZ, C), F32), ((LX + 2,...  1.61 us
  transfers between devices with their start and end apart: 9, of which 4 were waited for; matrix products, arithmetic and copies ran while one was open for 0% of the time, Pallas kernels for 9%

profile of v5, /device:TPU:1, one launch (start us, length us, event | category | flops | bytes accessed | tf_op | source)
XLA Modules:
  0.0 77.9 jit_solution(8665255193396590525)
XLA Ops:
  0.7 0.4 shard_map.84
  1.1 0.3 copy-done.3
  1.4 0.3 copy-done.1
  1.7 0.7 shard_map.85
  2.4 0.7 collective-permute-start
  3.1 6.5 %collective-permute-start.1 = (bf16[96,128]{1,0:T(8,128)(2,1)S(1)}, bf16[96,128]{1,0:T(8,128)(2,1)S(1)}, u32[]{:S(2)}, u32[]{:S(2)}) collective-permute-start(bf16[96,128]{1,0:T(8,128)(2,1)S(1)} %get-tuple-element.35), channel_id=1, source_target_pairs={{0,1},{1,0},{2,3},{3,2},{4,5},{5,4},{6,7},{7,6},{8,9},{9,8},{10,11... | collective-permute-start | bytes 73736 | tf_op jit(solution)/shard_map/ppermute | solution.py:35
  9.5 4.2 %collective-permute-start.2 = (bf16[384,128]{1,0:T(8,128)(2,1)S(1)}, bf16[384,128]{1,0:T(8,128)(2,1)S(1)}, u32[]{:S(2)}, u32[]{:S(2)}) collective-permute-start(bf16[384,128]{1,0:T(8,128)(2,1)S(1)} %get-tuple-element.40), channel_id=1, source_target_pairs={{16,32},{32,16},{48,64},{64,48},{80,96},{96,80},{112,128},{128,112... | collective-permute-start | bytes 294920 | tf_op jit(solution)/shard_map/ppermute | solution.py:35
  13.9 2.1 %collective-permute-start.3 = (bf16[80,128]{1,0:T(8,128)(2,1)S(1)}, bf16[80,128]{1,0:T(8,128)(2,1)S(1)}, u32[]{:S(2)}, u32[]{:S(2)}) collective-permute-start(bf16[80,128]{1,0:T(8,128)(2,1)S(1)} %get-tuple-element.41), channel_id=1, source_target_pairs={{16,32},{32,16},{48,64},{64,48},{80,96},{96,80},{112,128},{128,112... | collective-permute-start | bytes 61448 | tf_op jit(solution)/shard_map/ppermute | solution.py:35
  16.0 1.6 %shard_map.86 = (f32[4,20,8,128]{3,2,1,0:T(8,128)S(1)}, f32[4,18,8,128]{3,2,1,0:T(8,128)S(1)}, f32[6,18,8,128]{3,2,1,0:T(8,128)S(1)}, f32[3456,128]{1,0:T(8,128)S(1)}) custom-call(bf16[512,128]{1,0:T(8,128)(2,1)S(1)} %get-tuple-element.32.grid_ref, bf16[512,128]{1,0:T(8,128)(2,1)S(1)} %get-tuple-element.33.hidden_ref, ...), custom_call_target="tpu_custom_call" | custom-call | flops 8589934592 | bytes 1048576 | tf_op jit(solution)/shard_map/pallas_call | solution.py:409
  17.6 1.5 %collective-permute-done.3.x_ends_ref = bf16[80,128]{1,0:T(8,128)(2,1)S(1)} collective-permute-done((bf16[80,128]{1,0:T(8,128)(2,1)S(1)}, bf16[80,128]{1,0:T(8,128)(2,1)S(1)}, u32[]{:S(2)}, u32[]{:S(2)}) %collective-permute-start.3) | collective-permute-done | bytes 20512 | tf_op jit(solution)/shard_map/ppermute | solution.py:35
  19.1 1.3 %shard_map.88 = (bf16[2816,128]{1,0:T(8,128)(2,1)S(1)}, bf16[864,128]{1,0:T(8,128)(2,1)S(1)}, bf16[256,384]{1,0:T(8,128)(2,1)S(1)}, bf16[512,128]{1,0:T(8,128)(2,1)S(1)}, f32[4,20,8,128]{3,2,1,0:T(8,128)S(1)}) custom-call(bf16[512,512]{1,0:T(8,128)(2,1)S(1)} %get-tuple-element.30.place_ref, s32[1,256]{1,0:T(1,128)S(1)} %bitcast.7, ...), custom_call_target="tpu_custom_call" | custom-call | flops 8589934592 | bytes 1048576 | tf_op jit(solution)/shard_map/pallas_call | solution.py:416
  20.5 1.9 %shard_map.89 = (bf16[2816,128]{1,0:T(8,128)(2,1)S(1)}, bf16[64,256]{1,0:T(8,128)(2,1)}) custom-call(bf16[512,512]{1,0:T(8,128)(2,1)S(1)} %get-tuple-element.30.place_ref, f32[4,20,8,128]{3,2,1,0:T(8,128)S(1)} %get-tuple-element.36.mid, f32[4,20,8,128]{3,2,1,0:T(8,128)S(1)} %get-tuple-element.43.side, bf16[256,384]{1,0:T(8,128)(2,1)S(1)} %get-tuple-element.44.spread_ref, ...), custom_call_target="tpu_custom_call" | custom-call | flops 8589934592 | bytes 1048576 | tf_op jit(solution)/shard_map/pallas_call | solution.py:420
  22.4 0.3 collective-permute-done.5.other_ref
  22.7 0.2 shard_map.91
  22.8 21.2 %all_to_all.10.parts_ref = bf16[32,88,128]{2,1,0:T(8,128)(2,1)S(1)} all-to-all(bf16[32,88,128]{2,1,0:T(8,128)(2,1)S(1)} %bitcast.3), channel_id=1, replica_groups={{0,1,2,3,32,33,34,35,64,65,66,67,96,97,98,99,128,129,130,131,160,161,16..., dimensions={0} | all-to-all | bytes 1441792 | tf_op jit(solution)/shard_map/all_to_all | solution.py:375
  44.1 4.3 %collective-permute-start.6 = (bf16[88,128]{1,0:T(8,128)(2,1)S(1)}, bf16[88,128]{1,0:T(8,128)(2,1)S(1)}, u32[]{:S(2)}, u32[]{:S(2)}) collective-permute-start(bf16[88,128]{1,0:T(8,128)(2,1)S(1)} %shard_map.92.own_ref), channel_id=1, source_target_pairs={{0,4},{1,5},{2,6},{3,7},{4,0},{5,1},{6,2},{7,3},{8,12},{9,13},{10,... | collective-permute-start | bytes 67592 | tf_op jit(solution)/shard_map/ppermute | solution.py:382
  48.4 2.1 %shard_map.90 = (bf16[256,128]{1,0:T(8,128)(2,1)}, bf16[16,128]{1,0:T(8,128)(2,1)S(1)}) custom-call(s32[1,256]{1,0:T(1,128)S(1)} %bitcast.8, bf16[864,128]{1,0:T(8,128)(2,1)S(1)} %get-tuple-element.47.grad_ref, bf16[27,128,128]{2,1,0:T(8,128)(2,1)S(1)} %copy-done), custom_call_target="tpu_custom_call" | custom-call | flops 8589934592 | bytes 1048576 | tf_op jit(solution)/shard_map/pallas_call | solution.py:423
  50.5 2.2 %collective-permute-start.7 = (bf16[88,128]{1,0:T(8,128)(2,1)S(1)}, bf16[88,128]{1,0:T(8,128)(2,1)S(1)}, u32[]{:S(2)}, u32[]{:S(2)}) collective-permute-start(bf16[88,128]{1,0:T(8,128)(2,1)S(1)} %shard_map.93.own_ref), channel_id=1, source_target_pairs={{0,12},{1,13},{2,14},{3,15},{4,8},{5,9},{6,10},{7,11},{8,4},{9,5},... | collective-permute-start | bytes 67592 | tf_op jit(solution)/shard_map/ppermute | solution.py:382
  52.7 2.6 %collective-permute-done.7.other_ref = bf16[88,128]{1,0:T(8,128)(2,1)S(1)} collective-permute-done((bf16[88,128]{1,0:T(8,128)(2,1)S(1)}, bf16[88,128]{1,0:T(8,128)(2,1)S(1)}, u32[]{:S(2)}, u32[]{:S(2)}) %collective-permute-start.7) | collective-permute-done | bytes 22560 | tf_op jit(solution)/shard_map/ppermute | solution.py:382
  55.4 15.3 %all_to_all.11 = bf16[32,88,128]{2,1,0:T(8,128)(2,1)S(1)} all-to-all(bf16[32,88,128]{2,1,0:T(8,128)(2,1)S(1)} %shard_map.94), channel_id=1, replica_groups={{0,1,2,3,32,33,34,35,64,65,66,67,96,97,98,99,128,129,130,131,160,161,16..., dimensions={0} | all-to-all | bytes 1441792 | tf_op jit(solution)/shard_map/all_to_all | solution.py:375
  70.7 4.2 %collective-permute-start.8 = (bf16[2816,128]{1,0:T(8,128)(2,1)S(1)}, bf16[2816,128]{1,0:T(8,128)(2,1)S(1)}, u32[]{:S(2)}, u32[]{:S(2)}) collective-permute-start(bf16[2816,128]{1,0:T(8,128)(2,1)S(1)} %bitcast.4), channel_id=1, source_target_pairs={{0,16},{16,0},{32,48},{48,32},{64,80},{80,64},{96,112},{112,96},{1... | collective-permute-start | bytes 2162696 | tf_op jit(solution)/shard_map/ppermute | solution.py:35
  74.9 1.1 %shard_map.95 = (f32[27,128,128]{2,1,0:T(8,128)}, f32[1024,256]{1,0:T(8,128)}) custom-call(bf16[2816,128]{1,0:T(8,128)(2,1)S(1)} %bitcast.5), custom_call_target="tpu_custom_call" | custom-call | flops 8589934592 | bytes 1048576 | tf_op jit(solution)/shard_map/pallas_call | solution.py:428
  76.0 0.7 collective-permute-done.8.data_ref
  76.7 1.1 %shard_map.96 = (f32[27,128,128]{2,1,0:T(8,128)}, f32[1024,256]{1,0:T(8,128)}) custom-call(bf16[2816,128]{1,0:T(8,128)(2,1)S(1)} %collective-permute-done.8.data_ref, f32[27,128,128]{2,1,0:T(8,128)} %get-tuple-element.52.refs_0_, f32[1024,256]{1,0:T(8,128)} %get-tuple-element.53.refs_1_), custom_call_target="tpu_custom_call", output_to_operand_aliasing={{0}: (1, {}), {1}: (2, {})} | custom-call | bytes 1048576 | tf_op jit(solution)/shard_map/pallas_call | solution.py:429
  (19 shorter events, 0.4 us)
Async XLA Ops:
  0.6 0.8 copy-start.3
  0.6 1.1 %copy-start.1 = (bf16[1024,256]{1,0:T(8,128)(2,1)S(1)}, bf16[1024,256]{1,0:T(8,128)(2,1)}, u32[]{:S(2)}) copy-start(bf16[1024,256]{1,0:T(8,128)(2,1)} %w_down_ref.1) | copy-start | bytes 1572868
  0.7 1.0 %copy-start.4 = (s32[256]{0:T(256)S(1)}, s32[256]{0:T(256)}, u32[]{:S(2)}) copy-start(s32[256]{0:T(256)} %param.11) | copy-start | bytes 3076
  0.7 1.0 %copy-start.2 = (bf16[256,128]{1,0:T(8,128)(2,1)S(1)}, bf16[256,128]{1,0:T(8,128)(2,1)}, u32[]{:S(2)}) copy-start(bf16[256,128]{1,0:T(8,128)(2,1)} %features.1) | copy-start | bytes 196612
  2.4 11.4 %collective-permute-start = (bf16[96,128]{1,0:T(8,128)(2,1)S(1)}, bf16[96,128]{1,0:T(8,128)(2,1)S(1)}, u32[]{:S(2)}, u32[]{:S(2)}) collective-permute-start(bf16[96,128]{1,0:T(8,128)(2,1)S(1)} %get-tuple-element.34), channel_id=1, source_target_pairs={{1,2},{2,1},{3,4},{4,3},{5,6},{6,5},{7,8},{8,7},{9,10},{10,9},{11,... | collective-permute-start | bytes 73736 | tf_op jit(solution)/shard_map/ppermute | solution.py:35
  3.1 10.7 %collective-permute-start.1 = (bf16[96,128]{1,0:T(8,128)(2,1)S(1)}, bf16[96,128]{1,0:T(8,128)(2,1)S(1)}, u32[]{:S(2)}, u32[]{:S(2)}) collective-permute-start(bf16[96,128]{1,0:T(8,128)(2,1)S(1)} %get-tuple-element.35), channel_id=1, source_target_pairs={{0,1},{1,0},{2,3},{3,2},{4,5},{5,4},{6,7},{7,6},{8,9},{9,8},{10,11... | collective-permute-start | bytes 73736 | tf_op jit(solution)/shard_map/ppermute | solution.py:35
  9.5 9.6 %collective-permute-start.2 = (bf16[384,128]{1,0:T(8,128)(2,1)S(1)}, bf16[384,128]{1,0:T(8,128)(2,1)S(1)}, u32[]{:S(2)}, u32[]{:S(2)}) collective-permute-start(bf16[384,128]{1,0:T(8,128)(2,1)S(1)} %get-tuple-element.40), channel_id=1, source_target_pairs={{16,32},{32,16},{48,64},{64,48},{80,96},{96,80},{112,128},{128,112... | collective-permute-start | bytes 294920 | tf_op jit(solution)/shard_map/ppermute | solution.py:35
  13.8 2.2 %copy-start = (bf16[27,128,128]{2,1,0:T(8,128)(2,1)S(1)}, bf16[27,128,128]{2,1,0:T(8,128)(2,1)}, u32[]{:S(2)}) copy-start(bf16[27,128,128]{2,1,0:T(8,128)(2,1)} %w_sub_ref.1) | copy-start | bytes 2654212
  13.9 5.2 %collective-permute-start.3 = (bf16[80,128]{1,0:T(8,128)(2,1)S(1)}, bf16[80,128]{1,0:T(8,128)(2,1)S(1)}, u32[]{:S(2)}, u32[]{:S(2)}) collective-permute-start(bf16[80,128]{1,0:T(8,128)(2,1)S(1)} %get-tuple-element.41), channel_id=1, source_target_pairs={{16,32},{32,16},{48,64},{64,48},{80,96},{96,80},{112,128},{128,112... | collective-permute-start | bytes 61448 | tf_op jit(solution)/shard_map/ppermute | solution.py:35
  15.9 3.2 %collective-permute-start.4 = (bf16[464,128]{1,0:T(8,128)(2,1)S(1)}, bf16[464,128]{1,0:T(8,128)(2,1)S(1)}, u32[]{:S(2)}, u32[]{:S(2)}) collective-permute-start(bf16[464,128]{1,0:T(8,128)(2,1)S(1)} %get-tuple-element.42), channel_id=1, source_target_pairs={{0,16},{16,0},{32,48},{48,32},{64,80},{80,64},{96,112},{112,96},{1... | collective-permute-start | bytes 356360 | tf_op jit(solution)/shard_map/ppermute | solution.py:35
  20.4 2.3 %collective-permute-start.5 = (bf16[2816,128]{1,0:T(8,128)(2,1)S(1)}, bf16[2816,128]{1,0:T(8,128)(2,1)S(1)}, u32[]{:S(2)}, u32[]{:S(2)}) collective-permute-start(bf16[2816,128]{1,0:T(8,128)(2,1)S(1)} %get-tuple-element.50), channel_id=1, source_target_pairs={{0,16},{16,0},{32,48},{48,32},{64,80},{80,64},{96,112},{112,96},{1... | collective-permute-start | bytes 2162696 | tf_op jit(solution)/shard_map/ppermute | solution.py:35
  44.1 6.4 %collective-permute-start.6 = (bf16[88,128]{1,0:T(8,128)(2,1)S(1)}, bf16[88,128]{1,0:T(8,128)(2,1)S(1)}, u32[]{:S(2)}, u32[]{:S(2)}) collective-permute-start(bf16[88,128]{1,0:T(8,128)(2,1)S(1)} %shard_map.92.own_ref), channel_id=1, source_target_pairs={{0,4},{1,5},{2,6},{3,7},{4,0},{5,1},{6,2},{7,3},{8,12},{9,13},{10,... | collective-permute-start | bytes 67592 | tf_op jit(solution)/shard_map/ppermute | solution.py:382
  50.5 4.9 %collective-permute-start.7 = (bf16[88,128]{1,0:T(8,128)(2,1)S(1)}, bf16[88,128]{1,0:T(8,128)(2,1)S(1)}, u32[]{:S(2)}, u32[]{:S(2)}) collective-permute-start(bf16[88,128]{1,0:T(8,128)(2,1)S(1)} %shard_map.93.own_ref), channel_id=1, source_target_pairs={{0,12},{1,13},{2,14},{3,15},{4,8},{5,9},{6,10},{7,11},{8,4},{9,5},... | collective-permute-start | bytes 67592 | tf_op jit(solution)/shard_map/ppermute | solution.py:382
  70.7 6.0 %collective-permute-start.8 = (bf16[2816,128]{1,0:T(8,128)(2,1)S(1)}, bf16[2816,128]{1,0:T(8,128)(2,1)S(1)}, u32[]{:S(2)}, u32[]{:S(2)}) collective-permute-start(bf16[2816,128]{1,0:T(8,128)(2,1)S(1)} %bitcast.4), channel_id=1, source_target_pairs={{0,16},{16,0},{32,48},{48,32},{64,80},{80,64},{96,112},{112,96},{1... | collective-permute-start | bytes 2162696 | tf_op jit(solution)/shard_map/ppermute | solution.py:35

commit v6 on v5

--- a/solution.py
+++ b/solution.py
@@ -95,8 +95,8 @@
 
 def build_kernel(place_ref, ids, features, cot, w_down, grid_ref, hidden_ref, even_ref, odd_ref, x_odd_ref):
     onehot = cell_onehot(ids[...])
-    dense = dot(onehot, features[...])
-    active = dot(onehot, jnp.ones((onehot.shape[1], C), BF16)) > 0.5
+    both = dot(onehot, jnp.concatenate([features[...], jnp.ones((onehot.shape[1], C), BF16)], 1))
+    dense, active = both[:, :C], both[:, C:] > 0.5
     back_rows = dot(cot[...], w_down[...], ((1,), (1,))).astype(BF16)
     stacked = jnp.concatenate([back_rows[:, k * C : (k + 1) * C] for k in range(8)], 0)
     hidden_grad = jnp.where(active, dot(place_ref[...], stacked), 0.0)
@@ -163,6 +163,11 @@
     return jnp.concatenate([planes[:, k : k + LY + 2].reshape(rows, C).astype(BF16) for k in range(3)], 1)
 
 
+def inner_windows(planes):
+    rows = planes.shape[0] * LY * LZ
+    return jnp.concatenate([planes[:, k + 1 : k + 1 + LY].reshape(rows, C).astype(BF16) for k in range(3)], 1)
+
+
 def fold(taps):
     return shift_z(taps[:, :C], 1) + taps[:, C : 2 * C] + shift_z(taps[:, 2 * C :], -1)
 
@@ -181,7 +186,7 @@
     return value[:, 1 : LY + 1].reshape(value.shape[0] * LY * LZ, C)
 
 
-def early_kernel(grid_ref, hidden_ref, y_odd_ref, y_even_ref, w_sub, mid, hidden_mid, pre_ref, taps_ref):
+def early_kernel(grid_ref, hidden_ref, y_odd_ref, y_even_ref, w_sub, mid, hidden_mid, pre_ref, taps_ref, inner_ref):
     (low, low_grad), (high, high_grad) = y_halos(y_odd_ref, y_even_ref)
     mid[:, 0:2] = low.reshape(LX, 2, LZ, C)
     mid[:, LY + 2 :] = high.reshape(LX, 2, LZ, C)
@@ -194,7 +199,7 @@
     for step_x in range(3):
         part = fold(dot(rows, kernel_rows(w_sub, step_x)))
         pre_ref[2 - step_x : 2 - step_x + LX] += part.reshape(LX, LY + 2, LZ, C)
-    _, grad = activate(inner_rows(pre_ref[2:4]), inner_rows(hidden_mid[1:3]))
+    inner_ref[...], grad = activate(inner_rows(pre_ref[2:4]), inner_rows(hidden_mid[1:3]))
     spread = unfold(grad.astype(F32))
     for group in range(9):
         step_x, step_y = group // 3, group % 3
@@ -242,47 +247,48 @@
 
 
 def main_kernel(
-    place_ref, ids_ref, mid, hidden_mid, pre_ref, taps_ref, x_odd_ref, x_ends_ref, x_even_ref, cot_ref, w_sub,
-    send_ref, grad_ref, spread_ref, hidden_ref, side,
+    place_ref, ids_ref, mid, hidden_mid, pre_ref, taps_ref, inner_ref, x_odd_ref, x_ends_ref, x_even_ref, cot_ref, w_sub,
+    send_ref, spread_ref, hidden_ref, side, side_grad,
 ):
     x_odd = jnp.concatenate([x_odd_ref[...].astype(F32), x_ends_ref[...].astype(F32)], 0)
     x_even = x_even_ref[...].astype(F32)
     flag = parity("gx")
-    low_grad = store_side(side.at[0:2], pick(flag, x_odd, x_even))
-    high_grad = store_side(side.at[2:4], pick(flag, x_even, x_odd))
+    side_grad[0] = store_side(side.at[0:2], pick(flag, x_odd, x_even))
+    side_grad[1] = store_side(side.at[2:4], pick(flag, x_even, x_odd))
+    plane = LY * LZ
+    rows = inner_windows(side[1:3])
+    first = inner_rows(pre_ref[1:2]) + fold(dot(rows[:plane], kernel_rows(w_sub, 0)))
+    last = inner_rows(pre_ref[LX : LX + 1]) + fold(dot(rows[plane:], kernel_rows(w_sub, 2)))
+    hidden_grad = [inner_rows(hidden_mid[0:1]), inner_rows(hidden_mid[LX - 1 : LX])]
+    outer, grad = activate(jnp.concatenate([first, last], 0), jnp.concatenate(hidden_grad, 0))
+    spread_ref[...] = unfold(grad.astype(F32))
+    active = dot(cell_onehot(ids_ref[...]), jnp.ones((ids_ref.shape[1], C), BF16)) > 0.5
+    hidden = jnp.concatenate([outer[:plane], inner_ref[...], outer[plane:]], 0)
+    hidden_ref[...] = jnp.where(active, hidden, 0.0).astype(BF16)
+    store_of(1, send_ref, mid, side, spread_ref, hidden_ref, place_ref, cot_ref, taps_ref)
+
+
+def late_kernel(place_ref, mid, side, spread_ref, hidden_ref, cot_ref, taps_ref, w_down_ref, own_ref, coarse_ref):
+    coarse_ref[...] = dot(coarse_rows(place_ref, hidden_ref), w_down_ref[...]).astype(BF16)
+    store_of(0, own_ref, mid, side, spread_ref, hidden_ref, place_ref, cot_ref, taps_ref)
+
+
+def feature_kernel(ids_ref, side, side_grad, hidden_mid, pre_ref, w_sub_ref, after_ref, out_ref, done_ref, padded):
+    done_ref[...] = jnp.zeros_like(done_ref)
     column = (LY + 2) * LZ
-    centre = kernel_rows(w_sub, 1)
+    centre = kernel_rows(w_sub_ref, 1)
     rows = frame_rows(side[0:2])
-    outer = fold(dot(rows, kernel_rows(w_sub, 0)))
+    outer = fold(dot(rows, kernel_rows(w_sub_ref, 0)))
     first = pre_ref[0].reshape(column, C) + outer[:column] + fold(dot(rows[column:], centre))
     second = pre_ref[1].reshape(column, C) + outer[column:]
     rows = frame_rows(side[2:4])
-    outer = fold(dot(rows, kernel_rows(w_sub, 2)))
+    outer = fold(dot(rows, kernel_rows(w_sub_ref, 2)))
     last = pre_ref[LX + 1].reshape(column, C) + outer[column:] + fold(dot(rows[:column], centre))
     before = pre_ref[LX].reshape(column, C) + outer[:column]
     pre_act = jnp.concatenate([first, second, pre_ref[2:LX].reshape(2 * column, C), before, last], 0)
-    hidden_grad = jnp.concatenate([low_grad, hidden_mid[...].reshape(LX * column, C), high_grad], 0)
-    hidden, pre_grad = activate(pre_act, hidden_grad)
-    grad_ref[...] = pre_grad
-
-    def framed(value):
-        return value.reshape(LX + 2, LY + 2, LZ, C)
-
-    grad = framed(pre_grad.astype(F32))
-    spread_ref[...] = unfold(inner_rows(jnp.concatenate([grad[1:2], grad[LX : LX + 1]], 0)))
-    active = dot(cell_onehot(ids_ref[...]), jnp.ones((ids_ref.shape[1], C), BF16)) > 0.5
-    hidden_ref[...] = jnp.where(active, inner_rows(framed(hidden)[1 : LX + 1]), 0.0).astype(BF16)
-    store_of(1, send_ref, mid, side, spread_ref, hidden_ref, place_ref, cot_ref, taps_ref)
-
-
-def late_kernel(place_ref, mid, side, spread_ref, hidden_ref, cot_ref, taps_ref, w_down_ref, own_ref, coarse_ref):
-    coarse_ref[...] = dot(coarse_rows(place_ref, hidden_ref), w_down_ref[...]).astype(BF16)
-    store_of(0, own_ref, mid, side, spread_ref, hidden_ref, place_ref, cot_ref, taps_ref)
-
-
-def feature_kernel(ids_ref, grad_ref, w_sub_ref, out_ref, done_ref, padded):
-    done_ref[...] = jnp.zeros_like(done_ref)
-    padded[...] = grad_ref[...].astype(F32).reshape(LX + 2, LY + 2, LZ, C)
+    hidden_grad = jnp.concatenate([side_grad[0], hidden_mid[...].reshape(LX * column, C), side_grad[1]], 0)
+    _, pre_grad = activate(pre_act, hidden_grad)
+    padded[...] = pre_grad.astype(F32).reshape(LX + 2, LY + 2, LZ, C)
     parts = [jnp.zeros((CELLS, C), F32)] * 3
     for step_x in range(3):
         for step_y in range(3):
@@ -363,7 +369,7 @@
     )
 
 
-def reduce_all(own, send, after):
+def reduce_all(own, send, beside):
     rows, cols = lax.axis_size("gx"), lax.axis_size("gy")
     blocks = [
         [i * cols + j for i in range(core, rows, 2) for j in range(first, first + 4)]
@@ -377,11 +383,16 @@
     chunk = (CHUNK, C)
     (part,) = call(add_kernel, [((HALF, C), BF16)])(own, swap(send, "gx", 0))
     (total,) = call(sum_kernel, [(chunk, BF16)])(trade(part.reshape(PEERS, *chunk)))
-    for flip, shape, extra in ((2, chunk, (after,)), (6, (PEERS, *chunk), ())):
+    for flip, shape in ((2, chunk), (6, (PEERS, *chunk))):
         pairs = [(j, ((j >> 1) ^ flip) * 2 + (j & 1)) for j in range(cols)]
-        (total,) = call(pair_kernel, [(shape, BF16)])(total, lax.ppermute(total, "gy", pairs), *extra)
+        arrived = lax.ppermute(total, "gy", pairs)
+        extra = ()
+        if flip == 6:
+            result, mark = beside(total)
+            extra = (mark,)
+        (total,) = call(pair_kernel, [(shape, BF16)])(total, arrived, *extra)
     whole = trade(total).reshape(HALF, C)
-    return whole, swap(whole, "gx", 0)
+    return result, whole, swap(whole, "gx", 0)
 
 
 def local(features, w_sub, w_down, cell_ids, send_rows, map_in, map_out, cotangent):
@@ -390,7 +401,6 @@
     dense = ((CELLS, C), BF16)
     y_side = ((3 * LX * LZ, C), BF16)
     x_face_rows, x_ends = 3 * LY * LZ, 10 * LZ
-    frame = (((LX + 2) * (LY + 2) * LZ, C), BF16)
     packed = ((HALF, C), BF16)
     framed = pltpu.VMEM((LX + 2, LY + 2, LZ, C), F32)
 
@@ -406,22 +416,28 @@
     x_even, x_far = call(x_sides_kernel, outs, flops=LONG)(grid, hidden_grad, y_odd, y_even)
     x_even, x_far = swap_both(x_even, x_far, "gx")
     planes = (LX, LY + 4, LZ, C)
+    inner = (2 * LY * LZ, C)
     early = call(
         early_kernel,
-        [(planes, F32), ((LX, LY + 2, LZ, C), F32), ((LX + 2, LY + 2, LZ, C), F32), ((OFFSETS * C, C), F32)],
+        [(planes, F32), ((LX, LY + 2, LZ, C), F32), ((LX + 2, LY + 2, LZ, C), F32), ((OFFSETS * C, C), F32), (inner, F32)],
         flops=LONG,
     )(grid, hidden_grad, y_odd, y_even, w_sub)
-    mid, taps = early[0], early[3]
-    spread = ((2 * LY * LZ, 3 * C), BF16)
-    send, grad, *kept = call(main_kernel, [packed, frame, spread, dense, (planes, F32)], flops=LONG)(
+    mid, hidden_mid, pre_act, taps, _ = early
+    outs = [packed, ((2 * LY * LZ, 3 * C), BF16), dense, (planes, F32), ((2, (LY + 2) * LZ, C), F32)]
+    send, spread, hidden, side, side_grad = call(main_kernel, outs, flops=LONG)(
         to_corner, ids, *early, x_odd, x_far, x_even, cotangent, w_sub
     )
-    spread, hidden, side = kept
     own, coarse = call(late_kernel, [packed, ((U_DEV, C2), BF16)], flops=LONG)(
         to_corner, mid, side, spread, hidden, cotangent, taps, w_down
     )
-    feature_grad, done = call(feature_kernel, [((rows, C), BF16), ((16, C), BF16)], [framed], flops=LONG)(ids, grad, w_sub)
-    whole, other = reduce_all(own, send, done)
+
+    def beside(value):
+        outs = [((rows, C), BF16), ((16, C), BF16)]
+        return call(feature_kernel, outs, [framed], flops=LONG)(
+            ids, side, side_grad, hidden_mid, pre_act, w_sub, value
+        )
+
+    feature_grad, whole, other = reduce_all(own, send, beside)
     grads = [((OFFSETS, C, C), F32), ((8 * C, C2), F32)]
     scratch = [pltpu.VMEM((HALF // C, C, C), F32), pltpu.VMEM((8 * C, C2), F32), pltpu.SemaphoreType.DMA((4,))]
     in_hbm = [pl.BlockSpec(memory_space=pltpu.HBM)] * 2

time: 78.1 us -> 78.1 us (level)
  waiting for transfers between devices: 5.05 us -> 3.64 us
  starting transfers between devices: 24.3 us -> 25.2 us
    ppermute x2, waiting for transfers between devices: 2.62 us -> 1.2 us  [reduce_all(): arrived = lax.ppermute(total, 'gy', pairs)]
    ppermute x2, starting transfers between devices: 6.53 us -> 7.43 us  [reduce_all(): arrived = lax.ppermute(total, 'gy', pairs)]
  transfers between devices with their start and end apart: 9 -> 9, of which waited for: 4 -> 4; matrix products, arithmetic and copies ran while one was open for 0% -> 0% of each run, Pallas kernels for 9% -> 10%
where the time goes in v6:
time: 78.1 us; the launch traced here: 77.8 us
  blocking collectives  36.4 us (47%)
  starting transfers between devices  25.2 us (32%)
  Pallas kernels  11.1 us (14%)
  waiting for transfers between devices  3.64 us (5%)
  between operations  0.79 us (1%)
    all_to_all x2, blocking collectives, trade(): lax.all_to_all(value, AXES, 0, 0, axis_index_groups=blocks, tiled=True)  36.4 us
    ppermute x7, starting transfers between devices, swap(): return lax.ppermute(value, axis, swap_pairs(lax.axis_size(axis))[kind])  17.7 us
    ppermute x2, starting transfers between devices, reduce_all(): arrived = lax.ppermute(total, 'gy', pairs)  7.43 us
    pallas_call x1, Pallas kernels, beside(): call(feature_kernel, outs, [framed], flops=LONG)  3.06 us
    ppermute x7, waiting for transfers between devices, swap(): return lax.ppermute(value, axis, swap_pairs(lax.axis_size(axis))[kind])  2.44 us
    pallas_call x1, Pallas kernels, local(): call(late_kernel, [packed, ((U_DEV, C2), BF16)], flops=LONG)  1.89 us
    pallas_call x1, Pallas kernels, local(): call(early_kernel, [(planes, F32), ((LX, LY + 2, LZ, C), F32), ((LX + 2,...  1.6 us
  transfers between devices with their start and end apart: 9, of which 4 were waited for; matrix products, arithmetic and copies ran while one was open for 0% of the time, Pallas kernels for 10%

profile of v6, /device:TPU:1, one launch (start us, length us, event | category | flops | bytes accessed | tf_op | source)
XLA Modules:
  0.0 77.8 jit_solution(7556883415182533067)
XLA Ops:
  0.7 0.4 shard_map.84
  1.1 0.3 copy-done.3
  1.4 0.3 copy-done.1
  1.7 0.6 shard_map.85
  2.3 0.7 collective-permute-start
  3.0 6.5 %collective-permute-start.1 = (bf16[96,128]{1,0:T(8,128)(2,1)S(1)}, bf16[96,128]{1,0:T(8,128)(2,1)S(1)}, u32[]{:S(2)}, u32[]{:S(2)}) collective-permute-start(bf16[96,128]{1,0:T(8,128)(2,1)S(1)} %get-tuple-element.36), channel_id=1, source_target_pairs={{0,1},{1,0},{2,3},{3,2},{4,5},{5,4},{6,7},{7,6},{8,9},{9,8},{10,11... | collective-permute-start | bytes 73736 | tf_op jit(solution)/shard_map/ppermute | solution.py:35
  9.5 4.2 %collective-permute-start.2 = (bf16[384,128]{1,0:T(8,128)(2,1)S(1)}, bf16[384,128]{1,0:T(8,128)(2,1)S(1)}, u32[]{:S(2)}, u32[]{:S(2)}) collective-permute-start(bf16[384,128]{1,0:T(8,128)(2,1)S(1)} %get-tuple-element.42), channel_id=1, source_target_pairs={{16,32},{32,16},{48,64},{64,48},{80,96},{96,80},{112,128},{128,112... | collective-permute-start | bytes 294920 | tf_op jit(solution)/shard_map/ppermute | solution.py:35
  13.8 2.1 %collective-permute-start.3 = (bf16[80,128]{1,0:T(8,128)(2,1)S(1)}, bf16[80,128]{1,0:T(8,128)(2,1)S(1)}, u32[]{:S(2)}, u32[]{:S(2)}) collective-permute-start(bf16[80,128]{1,0:T(8,128)(2,1)S(1)} %get-tuple-element.43), channel_id=1, source_target_pairs={{16,32},{32,16},{48,64},{64,48},{80,96},{96,80},{112,128},{128,112... | collective-permute-start | bytes 61448 | tf_op jit(solution)/shard_map/ppermute | solution.py:35
  16.0 1.6 %shard_map.86 = (f32[4,20,8,128]{3,2,1,0:T(8,128)S(1)}, f32[4,18,8,128]{3,2,1,0:T(8,128)S(1)}, f32[6,18,8,128]{3,2,1,0:T(8,128)S(1)}, f32[3456,128]{1,0:T(8,128)S(1)}, f32[256,128]{1,0:T(8,128)S(1)}) custom-call(bf16[512,128]{1,0:T(8,128)(2,1)S(1)} %get-tuple-element.33.grid_ref, bf16[512,128]{1,0:T(8,128)(2,1)S(1)} %get-tuple-element.34.hidden_ref, ...), custom_call_target="tpu_custom_call" | custom-call | flops 8589934592 | bytes 1048576 | tf_op jit(solution)/shard_map/pallas_call | solution.py:420
  17.6 1.5 %collective-permute-done.3.x_ends_ref = bf16[80,128]{1,0:T(8,128)(2,1)S(1)} collective-permute-done((bf16[80,128]{1,0:T(8,128)(2,1)S(1)}, bf16[80,128]{1,0:T(8,128)(2,1)S(1)}, u32[]{:S(2)}, u32[]{:S(2)}) %collective-permute-start.3) | collective-permute-done | bytes 20512 | tf_op jit(solution)/shard_map/ppermute | solution.py:35
  19.0 0.9 %shard_map.88 = (bf16[2816,128]{1,0:T(8,128)(2,1)S(1)}, bf16[256,384]{1,0:T(8,128)(2,1)S(1)}, bf16[512,128]{1,0:T(8,128)(2,1)S(1)}, f32[4,20,8,128]{3,2,1,0:T(8,128)S(1)}, f32[2,144,128]{2,1,0:T(8,128)S(1)}) custom-call(bf16[512,512]{1,0:T(8,128)(2,1)S(1)} %get-tuple-element.31.place_ref, s32[1,256]{1,0:T(1,128)S(1)} %bitcast.7, ...), custom_call_target="tpu_custom_call" | custom-call | flops 8589934592 | bytes 1048576 | tf_op jit(solution)/shard_map/pallas_call | solution.py:427
  20.0 1.9 %shard_map.89 = (bf16[2816,128]{1,0:T(8,128)(2,1)S(1)}, bf16[64,256]{1,0:T(8,128)(2,1)}) custom-call(bf16[512,512]{1,0:T(8,128)(2,1)S(1)} %get-tuple-element.31.place_ref, f32[4,20,8,128]{3,2,1,0:T(8,128)S(1)} %get-tuple-element.37.mid, f32[4,20,8,128]{3,2,1,0:T(8,128)S(1)} %get-tuple-element.45.side, bf16[256,384]{1,0:T(8,128)(2,1)S(1)} %get-tuple-element.46.spread_ref, ...), custom_call_target="tpu_custom_call" | custom-call | flops 8589934592 | bytes 1048576 | tf_op jit(solution)/shard_map/pallas_call | solution.py:430
  21.9 0.3 collective-permute-done.5.other_ref
  22.2 0.2 shard_map.90
  22.4 21.2 %all_to_all.10.parts_ref = bf16[32,88,128]{2,1,0:T(8,128)(2,1)S(1)} all-to-all(bf16[32,88,128]{2,1,0:T(8,128)(2,1)S(1)} %bitcast.3), channel_id=1, replica_groups={{0,1,2,3,32,33,34,35,64,65,66,67,96,97,98,99,128,129,130,131,160,161,16..., dimensions={0} | all-to-all | bytes 1441792 | tf_op jit(solution)/shard_map/all_to_all | solution.py:381
  43.7 4.3 %collective-permute-start.6 = (bf16[88,128]{1,0:T(8,128)(2,1)S(1)}, bf16[88,128]{1,0:T(8,128)(2,1)S(1)}, u32[]{:S(2)}, u32[]{:S(2)}) collective-permute-start(bf16[88,128]{1,0:T(8,128)(2,1)S(1)} %shard_map.91.own_ref), channel_id=1, source_target_pairs={{0,4},{1,5},{2,6},{3,7},{4,0},{5,1},{6,2},{7,3},{8,12},{9,13},{10,... | collective-permute-start | bytes 67592 | tf_op jit(solution)/shard_map/ppermute | solution.py:388
  48.0 1.2 %collective-permute-done.6.other_ref = bf16[88,128]{1,0:T(8,128)(2,1)S(1)} collective-permute-done((bf16[88,128]{1,0:T(8,128)(2,1)S(1)}, bf16[88,128]{1,0:T(8,128)(2,1)S(1)}, u32[]{:S(2)}, u32[]{:S(2)}) %collective-permute-start.6) | collective-permute-done | bytes 22560 | tf_op jit(solution)/shard_map/ppermute | solution.py:388
  49.2 3.1 %collective-permute-start.7 = (bf16[88,128]{1,0:T(8,128)(2,1)S(1)}, bf16[88,128]{1,0:T(8,128)(2,1)S(1)}, u32[]{:S(2)}, u32[]{:S(2)}) collective-permute-start(bf16[88,128]{1,0:T(8,128)(2,1)S(1)} %shard_map.92.after_ref.own_ref), channel_id=1, source_target_pairs={{0,12},{1,13},{2,14},{3,15},{4,8},{5,9},{6,10},{7,11},{8,4},{9,5},... | collective-permute-start | bytes 67592 | tf_op jit(solution)/shard_map/ppermute | solution.py:388
  52.3 3.1 %shard_map.93 = (bf16[256,128]{1,0:T(8,128)(2,1)}, bf16[16,128]{1,0:T(8,128)(2,1)S(1)}) custom-call(s32[1,256]{1,0:T(1,128)S(1)} %bitcast.8, f32[4,20,8,128]{3,2,1,0:T(8,128)S(1)} %get-tuple-element.45.side, f32[2,144,128]{2,1,0:T(8,128)S(1)} %get-tuple-element.49.side_grad, f32[4,18,8,128]{3,2,1,0:T(8,128)S(1)} %get-tuple-element.38.hidden_mid, ...), custom_call_target="tpu_custom_call" | custom-call | flops 8589934592 | bytes 1048576 | tf_op jit(solution)/shard_map/pallas_call | solution.py:436
  55.4 15.2 %all_to_all.11 = bf16[32,88,128]{2,1,0:T(8,128)(2,1)S(1)} all-to-all(bf16[32,88,128]{2,1,0:T(8,128)(2,1)S(1)} %shard_map.94), channel_id=1, replica_groups={{0,1,2,3,32,33,34,35,64,65,66,67,96,97,98,99,128,129,130,131,160,161,16..., dimensions={0} | all-to-all | bytes 1441792 | tf_op jit(solution)/shard_map/all_to_all | solution.py:381
  70.7 4.1 %collective-permute-start.8 = (bf16[2816,128]{1,0:T(8,128)(2,1)S(1)}, bf16[2816,128]{1,0:T(8,128)(2,1)S(1)}, u32[]{:S(2)}, u32[]{:S(2)}) collective-permute-start(bf16[2816,128]{1,0:T(8,128)(2,1)S(1)} %bitcast.4), channel_id=1, source_target_pairs={{0,16},{16,0},{32,48},{48,32},{64,80},{80,64},{96,112},{112,96},{1... | collective-permute-start | bytes 2162696 | tf_op jit(solution)/shard_map/ppermute | solution.py:35
  74.8 1.1 %shard_map.95 = (f32[27,128,128]{2,1,0:T(8,128)}, f32[1024,256]{1,0:T(8,128)}) custom-call(bf16[2816,128]{1,0:T(8,128)(2,1)S(1)} %bitcast.5), custom_call_target="tpu_custom_call" | custom-call | flops 8589934592 | bytes 1048576 | tf_op jit(solution)/shard_map/pallas_call | solution.py:444
  75.9 0.7 collective-permute-done.8.data_ref
  76.6 1.1 %shard_map.96 = (f32[27,128,128]{2,1,0:T(8,128)}, f32[1024,256]{1,0:T(8,128)}) custom-call(bf16[2816,128]{1,0:T(8,128)(2,1)S(1)} %collective-permute-done.8.data_ref, f32[27,128,128]{2,1,0:T(8,128)} %get-tuple-element.54.refs_0_, f32[1024,256]{1,0:T(8,128)} %get-tuple-element.55.refs_1_), custom_call_target="tpu_custom_call", output_to_operand_aliasing={{0}: (1, {}), {1}: (2, {})} | custom-call | bytes 1048576 | tf_op jit(solution)/shard_map/pallas_call | solution.py:445
  (19 shorter events, 0.4 us)
Async XLA Ops:
  0.6 0.8 copy-start.3
  0.6 1.1 %copy-start.1 = (bf16[1024,256]{1,0:T(8,128)(2,1)S(1)}, bf16[1024,256]{1,0:T(8,128)(2,1)}, u32[]{:S(2)}) copy-start(bf16[1024,256]{1,0:T(8,128)(2,1)} %w_down_ref.1) | copy-start | bytes 1572868
  0.7 1.0 %copy-start.4 = (s32[256]{0:T(256)S(1)}, s32[256]{0:T(256)}, u32[]{:S(2)}) copy-start(s32[256]{0:T(256)} %param.11) | copy-start | bytes 3076
  0.7 1.0 %copy-start.2 = (bf16[256,128]{1,0:T(8,128)(2,1)S(1)}, bf16[256,128]{1,0:T(8,128)(2,1)}, u32[]{:S(2)}) copy-start(bf16[256,128]{1,0:T(8,128)(2,1)} %features.1) | copy-start | bytes 196612
  2.3 11.4 %collective-permute-start = (bf16[96,128]{1,0:T(8,128)(2,1)S(1)}, bf16[96,128]{1,0:T(8,128)(2,1)S(1)}, u32[]{:S(2)}, u32[]{:S(2)}) collective-permute-start(bf16[96,128]{1,0:T(8,128)(2,1)S(1)} %get-tuple-element.35), channel_id=1, source_target_pairs={{1,2},{2,1},{3,4},{4,3},{5,6},{6,5},{7,8},{8,7},{9,10},{10,9},{11,... | collective-permute-start | bytes 73736 | tf_op jit(solution)/shard_map/ppermute | solution.py:35
  3.0 10.7 %collective-permute-start.1 = (bf16[96,128]{1,0:T(8,128)(2,1)S(1)}, bf16[96,128]{1,0:T(8,128)(2,1)S(1)}, u32[]{:S(2)}, u32[]{:S(2)}) collective-permute-start(bf16[96,128]{1,0:T(8,128)(2,1)S(1)} %get-tuple-element.36), channel_id=1, source_target_pairs={{0,1},{1,0},{2,3},{3,2},{4,5},{5,4},{6,7},{7,6},{8,9},{9,8},{10,11... | collective-permute-start | bytes 73736 | tf_op jit(solution)/shard_map/ppermute | solution.py:35
  9.5 9.6 %collective-permute-start.2 = (bf16[384,128]{1,0:T(8,128)(2,1)S(1)}, bf16[384,128]{1,0:T(8,128)(2,1)S(1)}, u32[]{:S(2)}, u32[]{:S(2)}) collective-permute-start(bf16[384,128]{1,0:T(8,128)(2,1)S(1)} %get-tuple-element.42), channel_id=1, source_target_pairs={{16,32},{32,16},{48,64},{64,48},{80,96},{96,80},{112,128},{128,112... | collective-permute-start | bytes 294920 | tf_op jit(solution)/shard_map/ppermute | solution.py:35
  13.7 2.2 %copy-start = (bf16[27,128,128]{2,1,0:T(8,128)(2,1)S(1)}, bf16[27,128,128]{2,1,0:T(8,128)(2,1)}, u32[]{:S(2)}) copy-start(bf16[27,128,128]{2,1,0:T(8,128)(2,1)} %w_sub_ref.1) | copy-start | bytes 2654212
  13.8 5.2 %collective-permute-start.3 = (bf16[80,128]{1,0:T(8,128)(2,1)S(1)}, bf16[80,128]{1,0:T(8,128)(2,1)S(1)}, u32[]{:S(2)}, u32[]{:S(2)}) collective-permute-start(bf16[80,128]{1,0:T(8,128)(2,1)S(1)} %get-tuple-element.43), channel_id=1, source_target_pairs={{16,32},{32,16},{48,64},{64,48},{80,96},{96,80},{112,128},{128,112... | collective-permute-start | bytes 61448 | tf_op jit(solution)/shard_map/ppermute | solution.py:35
  15.8 3.2 %collective-permute-start.4 = (bf16[464,128]{1,0:T(8,128)(2,1)S(1)}, bf16[464,128]{1,0:T(8,128)(2,1)S(1)}, u32[]{:S(2)}, u32[]{:S(2)}) collective-permute-start(bf16[464,128]{1,0:T(8,128)(2,1)S(1)} %get-tuple-element.44), channel_id=1, source_target_pairs={{0,16},{16,0},{32,48},{48,32},{64,80},{80,64},{96,112},{112,96},{1... | collective-permute-start | bytes 356360 | tf_op jit(solution)/shard_map/ppermute | solution.py:35
  19.9 2.3 %collective-permute-start.5 = (bf16[2816,128]{1,0:T(8,128)(2,1)S(1)}, bf16[2816,128]{1,0:T(8,128)(2,1)S(1)}, u32[]{:S(2)}, u32[]{:S(2)}) collective-permute-start(bf16[2816,128]{1,0:T(8,128)(2,1)S(1)} %get-tuple-element.51), channel_id=1, source_target_pairs={{0,16},{16,0},{32,48},{48,32},{64,80},{80,64},{96,112},{112,96},{1... | collective-permute-start | bytes 2162696 | tf_op jit(solution)/shard_map/ppermute | solution.py:35
  43.7 5.5 %collective-permute-start.6 = (bf16[88,128]{1,0:T(8,128)(2,1)S(1)}, bf16[88,128]{1,0:T(8,128)(2,1)S(1)}, u32[]{:S(2)}, u32[]{:S(2)}) collective-permute-start(bf16[88,128]{1,0:T(8,128)(2,1)S(1)} %shard_map.91.own_ref), channel_id=1, source_target_pairs={{0,4},{1,5},{2,6},{3,7},{4,0},{5,1},{6,2},{7,3},{8,12},{9,13},{10,... | collective-permute-start | bytes 67592 | tf_op jit(solution)/shard_map/ppermute | solution.py:388
  49.2 6.2 %collective-permute-start.7 = (bf16[88,128]{1,0:T(8,128)(2,1)S(1)}, bf16[88,128]{1,0:T(8,128)(2,1)S(1)}, u32[]{:S(2)}, u32[]{:S(2)}) collective-permute-start(bf16[88,128]{1,0:T(8,128)(2,1)S(1)} %shard_map.92.after_ref.own_ref), channel_id=1, source_target_pairs={{0,12},{1,13},{2,14},{3,15},{4,8},{5,9},{6,10},{7,11},{8,4},{9,5},... | collective-permute-start | bytes 67592 | tf_op jit(solution)/shard_map/ppermute | solution.py:388
  70.7 5.9 %collective-permute-start.8 = (bf16[2816,128]{1,0:T(8,128)(2,1)S(1)}, bf16[2816,128]{1,0:T(8,128)(2,1)S(1)}, u32[]{:S(2)}, u32[]{:S(2)}) collective-permute-start(bf16[2816,128]{1,0:T(8,128)(2,1)S(1)} %bitcast.4), channel_id=1, source_target_pairs={{0,16},{16,0},{32,48},{48,32},{64,80},{80,64},{96,112},{112,96},{1... | collective-permute-start | bytes 2162696 | tf_op jit(solution)/shard_map/ppermute | solution.py:35

commit v7 on v6

--- a/solution.py
+++ b/solution.py
@@ -76,16 +76,21 @@
     return jnp.where(z == LZ - 1, 0.0, pltpu.roll(value, rows - 1, 0))
 
 
-def y_sides(dense, hidden_grad):
+def y_sides(dense, active, cot):
     def face(near, edge):
-        rows = [dense[:, near].reshape(2 * LX * LZ, C), hidden_grad[:, edge].reshape(LX * LZ, C)]
-        return jnp.concatenate(rows, 0)
+        first = edge // 2 * (LZ // 2)
+        coarse = [cot[k * 32 + first : k * 32 + first + LZ // 2] for k in range(2)]
+        coarse = jnp.concatenate(coarse, 0)
+        rows = [dense[:, near].reshape(2 * LX * LZ, C), active[:, edge].reshape(LX * LZ, C)]
+        return jnp.concatenate([*rows, coarse[:, :C], coarse[:, C:]], 0)
 
     return face(slice(0, 2), 0), face(slice(LY - 2, LY), LY - 1)
 
 
 def split_y(rows):
-    return rows[: 2 * LX * LZ].reshape(LX, 2 * LZ, C), rows[2 * LX * LZ :].reshape(LX, LZ, C)
+    feature, mask = 2 * LX * LZ, 3 * LX * LZ
+    cot = jnp.concatenate([rows[mask : mask + LZ], rows[mask + LZ :]], 1)
+    return rows[:feature].reshape(LX, 2 * LZ, C), rows[feature:mask].reshape(LX, LZ, C), cot
 
 
 def places_kernel(from_ref, to_ref):
@@ -93,19 +98,29 @@
     to_ref[...] = corner_onehot(0)
 
 
-def build_kernel(place_ref, ids, features, cot, w_down, grid_ref, hidden_ref, even_ref, odd_ref, x_odd_ref):
-    onehot = cell_onehot(ids[...])
-    both = dot(onehot, jnp.concatenate([features[...], jnp.ones((onehot.shape[1], C), BF16)], 1))
-    dense, active = both[:, :C], both[:, C:] > 0.5
-    back_rows = dot(cot[...], w_down[...], ((1,), (1,))).astype(BF16)
-    stacked = jnp.concatenate([back_rows[:, k * C : (k + 1) * C] for k in range(8)], 0)
-    hidden_grad = jnp.where(active, dot(place_ref[...], stacked), 0.0)
+def place_rows(ids, features):
+    onehot = cell_onehot(ids)
+    both = dot(onehot, jnp.concatenate([features, jnp.ones(features.shape, BF16)], 1))
+    return both[:, :C], both[:, C:]
+
+
+def build_kernel(place_ref, ids, features, cot, grid_ref, active_ref, even_ref, odd_ref):
+    dense, active = place_rows(ids[...], features[...])
     grid_ref[...] = dense.astype(BF16)
-    hidden_ref[...] = hidden_grad.astype(BF16)
-    low, high = y_sides(dense.reshape(LX, LY, LZ, C), hidden_grad.reshape(LX, LY, LZ, C))
+    active_ref[...] = active.astype(BF16)
+    shape = (LX, LY, LZ, C)
+    low, high = y_sides(dense.reshape(shape), active.reshape(shape), cot[...].astype(F32))
     side = parity("gy")
     even_ref[...] = pick(side, high, low).astype(BF16)
     odd_ref[...] = pick(side, low, high).astype(BF16)
+
+
+def back_kernel(place_ref, grid_ref, active_ref, cot, w_down, hidden_ref, x_odd_ref):
+    back_rows = dot(cot[...], w_down[...], ((1,), (1,))).astype(BF16)
+    stacked = jnp.concatenate([back_rows[:, k * C : (k + 1) * C] for k in range(8)], 0)
+    hidden_grad = jnp.where(active_ref[...].astype(F32) > 0.5, dot(place_ref[...], stacked), 0.0)
+    hidden_ref[...] = hidden_grad.astype(BF16)
+    dense = grid_ref[...].astype(F32)
     first = x_face(dense, hidden_grad, 0)
     last = x_face(dense, hidden_grad, LX - 1)
     x_odd_ref[...] = pick(parity("gx"), first, last).astype(BF16)
@@ -124,13 +139,15 @@
 
 
 def x_sides_kernel(grid_ref, hidden_ref, y_odd_ref, y_even_ref, even_ref, odd_ref):
-    (low, low_grad), (high, high_grad) = y_halos(y_odd_ref, y_even_ref)
+    (low, low_mask, low_cot), (high, high_mask, high_cot) = y_halos(y_odd_ref, y_even_ref)
 
     def corners(near, edge):
         rows = []
         for x in near:
             rows += [low[x], high[x]]
-        return jnp.concatenate([*rows, low_grad[edge], high_grad[edge]], 0)
+        at = edge // 2 * (LZ // 2)
+        coarse = jnp.concatenate([low_cot[at : at + LZ // 2], high_cot[at : at + LZ // 2]], 0)
+        return jnp.concatenate([*rows, low_mask[edge], high_mask[edge], coarse[:, :C], coarse[:, C:]], 0)
 
     first, last = corners((0, 1), 0), corners((LX - 2, LX - 1), LX - 1)
     dense, hidden_grad = grid_ref[...].astype(F32), hidden_ref[...].astype(F32)
@@ -147,7 +164,7 @@
     planes[:, 0:2] = ends[:, 0:2]
     planes[:, LY + 2 :] = ends[:, 2:4]
     grads = corner + 8 * LZ
-    return jnp.concatenate([rows[grads : grads + LZ], rows[face:corner], rows[grads + LZ :]], 0)
+    return jnp.concatenate([rows[grads : grads + LZ], rows[face:corner], rows[grads + LZ : grads + 2 * LZ]], 0)
 
 
 def kernel_rows(w_sub, step_x):
@@ -187,12 +204,12 @@
 
 
 def early_kernel(grid_ref, hidden_ref, y_odd_ref, y_even_ref, w_sub, mid, hidden_mid, pre_ref, taps_ref, inner_ref):
-    (low, low_grad), (high, high_grad) = y_halos(y_odd_ref, y_even_ref)
+    (low, low_mask, _), (high, high_mask, _) = y_halos(y_odd_ref, y_even_ref)
     mid[:, 0:2] = low.reshape(LX, 2, LZ, C)
     mid[:, LY + 2 :] = high.reshape(LX, 2, LZ, C)
     mid[:, 2 : LY + 2] = grid_ref[...].astype(F32).reshape(LX, LY, LZ, C)
-    hidden_mid[:, 0] = low_grad
-    hidden_mid[:, LY + 1] = high_grad
+    hidden_mid[:, 0] = low_mask
+    hidden_mid[:, LY + 1] = high_mask
     hidden_mid[:, 1 : LY + 1] = hidden_ref[...].astype(F32).reshape(LX, LY, LZ, C)
     rows = frame_rows(mid[...])
     pre_ref[...] = jnp.zeros_like(pre_ref)
@@ -273,8 +290,35 @@
     store_of(0, own_ref, mid, side, spread_ref, hidden_ref, place_ref, cot_ref, taps_ref)
 
 
-def feature_kernel(ids_ref, side, side_grad, hidden_mid, pre_ref, w_sub_ref, after_ref, out_ref, done_ref, padded):
-    done_ref[...] = jnp.zeros_like(done_ref)
+def ring_onehot():
+    cell = lax.broadcasted_iota(jnp.int32, (12 * LZ, 8 * 32), 0)
+    place = lax.broadcasted_iota(jnp.int32, (12 * LZ, 8 * 32), 1)
+    z, x, high = cell & 7, (cell >> 3) & 3, (cell >> 5) & 1
+    face = ((x & 1) * 4 + (1 - high) * 2 + (z & 1)) * 32 + high * 8 + (x >> 1) * 4 + (z >> 1)
+    far, end = (cell >> 4) & 1, (cell >> 3) & 1
+    ends = ((1 - far) * 4 + (1 - end) * 2 + (z & 1)) * 32 + 16 + far * 8 + end * 4 + (z >> 1)
+    return jnp.where(jnp.where(cell < 8 * LZ, face, ends) == place, 1.0, 0.0).astype(BF16)
+
+
+def ring_grads(y_odd_ref, y_even_ref, x_ends_ref, x_even_ref, w_down):
+    (_, _, low), (_, _, high) = y_halos(y_odd_ref, y_even_ref)
+
+    def tail(ref):
+        rows = ref[...].astype(F32)
+        rows = rows[rows.shape[0] - 2 * LZ :]
+        return jnp.concatenate([rows[:LZ], rows[LZ:]], 1)
+
+    odd, even = tail(x_ends_ref), tail(x_even_ref)
+    flag = parity("gx")
+    cot = jnp.concatenate([low, high, pick(flag, odd, even), pick(flag, even, odd)], 0).astype(BF16)
+    back_rows = dot(cot, w_down[...], ((1,), (1,))).astype(BF16)
+    stacked = jnp.concatenate([back_rows[:, k * C : (k + 1) * C] for k in range(8)], 0)
+    return dot(ring_onehot(), stacked)
+
+
+def ring_kernel(
+    side, side_grad, hidden_mid, pre_ref, w_sub_ref, y_odd_ref, y_even_ref, x_ends_ref, x_even_ref, w_down, after_ref, grad_ref
+):
     column = (LY + 2) * LZ
     centre = kernel_rows(w_sub_ref, 1)
     rows = frame_rows(side[0:2])
@@ -286,9 +330,24 @@
     last = pre_ref[LX + 1].reshape(column, C) + outer[column:] + fold(dot(rows[:column], centre))
     before = pre_ref[LX].reshape(column, C) + outer[:column]
     pre_act = jnp.concatenate([first, second, pre_ref[2:LX].reshape(2 * column, C), before, last], 0)
-    hidden_grad = jnp.concatenate([side_grad[0], hidden_mid[...].reshape(LX * column, C), side_grad[1]], 0)
+    ring = ring_grads(y_odd_ref, y_even_ref, x_ends_ref, x_even_ref, w_down)
+    size = LX * LZ
+    faces = [(hidden_mid[:, at] * ring[k * size : (k + 1) * size].reshape(LX, LZ, C))[:, None] for k, at in ((0, 0), (1, LY + 1))]
+    middle = jnp.concatenate([faces[0], hidden_mid[:, 1 : LY + 1], faces[1]], 1).reshape(LX * column, C)
+
+    def plane(k):
+        first = 2 * size + 2 * LZ * k
+        ends = [side_grad[k, :LZ] * ring[first : first + LZ], side_grad[k, column - LZ :] * ring[first + LZ : first + 2 * LZ]]
+        return jnp.concatenate([ends[0], side_grad[k, LZ : column - LZ], ends[1]], 0)
+
+    hidden_grad = jnp.concatenate([plane(0), middle, plane(1)], 0)
     _, pre_grad = activate(pre_act, hidden_grad)
-    padded[...] = pre_grad.astype(F32).reshape(LX + 2, LY + 2, LZ, C)
+    grad_ref[...] = pre_grad
+
+
+def feature_kernel(ids_ref, grad_ref, w_sub_ref, after_ref, out_ref, done_ref, padded):
+    done_ref[...] = jnp.zeros_like(done_ref)
+    padded[...] = grad_ref[...].astype(F32).reshape(LX + 2, LY + 2, LZ, C)
     parts = [jnp.zeros((CELLS, C), F32)] * 3
     for step_x in range(3):
         for step_y in range(3):
@@ -369,7 +428,7 @@
     )
 
 
-def reduce_all(own, send, beside):
+def reduce_all(own, send, first, second):
     rows, cols = lax.axis_size("gx"), lax.axis_size("gy")
     blocks = [
         [i * cols + j for i in range(core, rows, 2) for j in range(first, first + 4)]
@@ -386,11 +445,8 @@
     for flip, shape in ((2, chunk), (6, (PEERS, *chunk))):
         pairs = [(j, ((j >> 1) ^ flip) * 2 + (j & 1)) for j in range(cols)]
         arrived = lax.ppermute(total, "gy", pairs)
-        extra = ()
-        if flip == 6:
-            result, mark = beside(total)
-            extra = (mark,)
-        (total,) = call(pair_kernel, [(shape, BF16)])(total, arrived, *extra)
+        result, mark = first(total) if flip == 2 else second(total, result)
+        (total,) = call(pair_kernel, [(shape, BF16)])(total, arrived, mark)
     whole = trade(total).reshape(HALF, C)
     return result, whole, swap(whole, "gx", 0)
 
@@ -399,18 +455,20 @@
     ids = cell_ids[None]
     rows = features.shape[0]
     dense = ((CELLS, C), BF16)
-    y_side = ((3 * LX * LZ, C), BF16)
-    x_face_rows, x_ends = 3 * LY * LZ, 10 * LZ
+    y_side = ((3 * LX * LZ + 2 * LZ, C), BF16)
+    x_face_rows, x_ends = 3 * LY * LZ, 12 * LZ
     packed = ((HALF, C), BF16)
     framed = pltpu.VMEM((LX + 2, LY + 2, LZ, C), F32)
 
     place = ((CELLS, CELLS), BF16)
     from_corner, to_corner = call(places_kernel, [place, place], flops=LONG)()
-    outs = [dense, dense, y_side, y_side, ((x_face_rows, C), BF16)]
-    grid, hidden_grad, y_even, y_odd, x_odd = call(build_kernel, outs, flops=LONG)(
-        from_corner, ids, features, cotangent, w_down
+    grid, active, y_even, y_odd = call(build_kernel, [dense, dense, y_side, y_side], flops=LONG)(
+        from_corner, ids, features, cotangent
     )
     y_even, y_odd = swap_both(y_even, y_odd, "gy")
+    hidden_grad, x_odd = call(back_kernel, [dense, ((x_face_rows, C), BF16)], flops=LONG)(
+        from_corner, grid, active, cotangent, w_down
+    )
     x_odd = swap(x_odd, "gx", 1)
     outs = [((x_face_rows + x_ends, C), BF16), ((x_ends, C), BF16)]
     x_even, x_far = call(x_sides_kernel, outs, flops=LONG)(grid, hidden_grad, y_odd, y_even)
@@ -431,13 +489,18 @@
         to_corner, mid, side, spread, hidden, cotangent, taps, w_down
     )
 
-    def beside(value):
+    def first(value):
+        outs = [(((LX + 2) * (LY + 2) * LZ, C), BF16)]
+        (grad,) = call(ring_kernel, outs, flops=LONG)(
+            side, side_grad, hidden_mid, pre_act, w_sub, y_odd, y_even, x_far, x_even, w_down, value
+        )
+        return grad, grad
+
+    def second(value, grad):
         outs = [((rows, C), BF16), ((16, C), BF16)]
-        return call(feature_kernel, outs, [framed], flops=LONG)(
-            ids, side, side_grad, hidden_mid, pre_act, w_sub, value
-        )
-
-    feature_grad, whole, other = reduce_all(own, send, beside)
+        return call(feature_kernel, outs, [framed], flops=LONG)(ids, grad, w_sub, value)
+
+    feature_grad, whole, other = reduce_all(own, send, first, second)
     grads = [((OFFSETS, C, C), F32), ((8 * C, C2), F32)]
     scratch = [pltpu.VMEM((HALF // C, C, C), F32), pltpu.VMEM((8 * C, C2), F32), pltpu.SemaphoreType.DMA((4,))]
     in_hbm = [pl.BlockSpec(memory_space=pltpu.HBM)] * 2

time: 78.1 us -> 77.2 us (0.988)
  waiting for transfers between devices: 3.64 us -> 2.8 us
    ppermute x2, waiting for transfers between devices: 1.2 us -> 0.31 us  [reduce_all(): arrived = lax.ppermute(total, 'gy', pairs)]
    pallas_call x4 -> x6, Pallas kernels: 3.71 us -> 3.82 us  [the longest x1 2.07 us: second(): call(feature_kernel, outs, [framed], flops=LONG)(ids, grad, w_sub, value)]
  transfers between devices with their start and end apart: 9 -> 9, of which waited for: 4 -> 4; matrix products, arithmetic and copies ran while one was open for 0% -> 0% of each run, Pallas kernels for 10% -> 11%
where the time goes in v7:
time: 77.2 us; the launch traced here: 76.9 us
  blocking collectives  35.8 us (46%)
  starting transfers between devices  25.8 us (33%)
  Pallas kernels  11.2 us (15%)
  waiting for transfers between devices  2.8 us (4%)
  between operations  0.8 us (1%)
    all_to_all x2, blocking collectives, trade(): lax.all_to_all(value, AXES, 0, 0, axis_index_groups=blocks, tiled=True)  35.8 us
    ppermute x7, starting transfers between devices, swap(): return lax.ppermute(value, axis, swap_pairs(lax.axis_size(axis))[kind])  17.8 us
    ppermute x2, starting transfers between devices, reduce_all(): arrived = lax.ppermute(total, 'gy', pairs)  7.94 us
    ppermute x7, waiting for transfers between devices, swap(): return lax.ppermute(value, axis, swap_pairs(lax.axis_size(axis))[kind])  2.49 us
    pallas_call x1, Pallas kernels, second(): call(feature_kernel, outs, [framed], flops=LONG)(ids, grad, w_sub, value)  2.07 us
    pallas_call x1, Pallas kernels, local(): call(late_kernel, [packed, ((U_DEV, C2), BF16)], flops=LONG)  1.89 us
    pallas_call x1, Pallas kernels, local(): call(early_kernel, [(planes, F32), ((LX, LY + 2, LZ, C), F32), ((LX + 2,...  1.6 us
  transfers between devices with their start and end apart: 9, of which 4 were waited for; matrix products, arithmetic and copies ran while one was open for 0% of the time, Pallas kernels for 11%

profile of v7, /device:TPU:1, one launch (start us, length us, event | category | flops | bytes accessed | tf_op | source)
XLA Modules:
  0.0 76.9 jit_solution(9450777362758091301)
XLA Ops:
  0.7 0.4 shard_map.84
  1.0 0.3 copy-done.3
  1.5 0.2 shard_map.85
  1.8 0.7 collective-permute-start
  2.4 6.5 %collective-permute-start.1 = (bf16[112,128]{1,0:T(8,128)(2,1)S(1)}, bf16[112,128]{1,0:T(8,128)(2,1)S(1)}, u32[]{:S(2)}, u32[]{:S(2)}) collective-permute-start(bf16[112,128]{1,0:T(8,128)(2,1)S(1)} %get-tuple-element.38), channel_id=1, source_target_pairs={{0,1},{1,0},{2,3},{3,2},{4,5},{5,4},{6,7},{7,6},{8,9},{9,8},{10,11... | collective-permute-start | bytes 86024 | tf_op jit(solution)/shard_map/ppermute | solution.py:35
  8.9 0.6 shard_map.86
  9.5 4.2 %collective-permute-start.2 = (bf16[384,128]{1,0:T(8,128)(2,1)S(1)}, bf16[384,128]{1,0:T(8,128)(2,1)S(1)}, u32[]{:S(2)}, u32[]{:S(2)}) collective-permute-start(bf16[384,128]{1,0:T(8,128)(2,1)S(1)} %get-tuple-element.44), channel_id=1, source_target_pairs={{16,32},{32,16},{48,64},{64,48},{80,96},{96,80},{112,128},{128,112... | collective-permute-start | bytes 294920 | tf_op jit(solution)/shard_map/ppermute | solution.py:35
  13.8 2.1 %collective-permute-start.3 = (bf16[96,128]{1,0:T(8,128)(2,1)S(1)}, bf16[96,128]{1,0:T(8,128)(2,1)S(1)}, u32[]{:S(2)}, u32[]{:S(2)}) collective-permute-start(bf16[96,128]{1,0:T(8,128)(2,1)S(1)} %get-tuple-element.45), channel_id=1, source_target_pairs={{16,32},{32,16},{48,64},{64,48},{80,96},{96,80},{112,128},{128,112... | collective-permute-start | bytes 73736 | tf_op jit(solution)/shard_map/ppermute | solution.py:35
  16.0 1.6 %shard_map.87 = (f32[4,20,8,128]{3,2,1,0:T(8,128)S(1)}, f32[4,18,8,128]{3,2,1,0:T(8,128)S(1)}, f32[6,18,8,128]{3,2,1,0:T(8,128)S(1)}, f32[3456,128]{1,0:T(8,128)S(1)}, f32[256,128]{1,0:T(8,128)S(1)}) custom-call(bf16[512,128]{1,0:T(8,128)(2,1)S(1)} %get-tuple-element.34.grid_ref, bf16[512,128]{1,0:T(8,128)(2,1)S(1)} %get-tuple-element.36.hidden_ref, ...), custom_call_target="tpu_custom_call" | custom-call | flops 8589934592 | bytes 1048576 | tf_op jit(solution)/shard_map/pallas_call | solution.py:478
  17.6 1.5 %collective-permute-done.3.x_ends_ref = bf16[96,128]{1,0:T(8,128)(2,1)S(1)} collective-permute-done((bf16[96,128]{1,0:T(8,128)(2,1)S(1)}, bf16[96,128]{1,0:T(8,128)(2,1)S(1)}, u32[]{:S(2)}, u32[]{:S(2)}) %collective-permute-start.3) | collective-permute-done | bytes 24608 | tf_op jit(solution)/shard_map/ppermute | solution.py:35
  19.1 0.9 %shard_map.89 = (bf16[2816,128]{1,0:T(8,128)(2,1)S(1)}, bf16[256,384]{1,0:T(8,128)(2,1)S(1)}, bf16[512,128]{1,0:T(8,128)(2,1)S(1)}, f32[4,20,8,128]{3,2,1,0:T(8,128)S(1)}, f32[2,144,128]{2,1,0:T(8,128)S(1)}) custom-call(bf16[512,512]{1,0:T(8,128)(2,1)S(1)} %get-tuple-element.32.place_ref, s32[1,256]{1,0:T(1,128)S(1)} %bitcast.7, ...), custom_call_target="tpu_custom_call" | custom-call | flops 8589934592 | bytes 1048576 | tf_op jit(solution)/shard_map/pallas_call | solution.py:485
  20.1 1.9 %shard_map.90 = (bf16[2816,128]{1,0:T(8,128)(2,1)S(1)}, bf16[64,256]{1,0:T(8,128)(2,1)}) custom-call(bf16[512,512]{1,0:T(8,128)(2,1)S(1)} %get-tuple-element.32.place_ref, f32[4,20,8,128]{3,2,1,0:T(8,128)S(1)} %get-tuple-element.39.mid, f32[4,20,8,128]{3,2,1,0:T(8,128)S(1)} %get-tuple-element.47.side, bf16[256,384]{1,0:T(8,128)(2,1)S(1)} %get-tuple-element.48.spread_ref, ...), custom_call_target="tpu_custom_call" | custom-call | flops 8589934592 | bytes 1048576 | tf_op jit(solution)/shard_map/pallas_call | solution.py:488
  22.0 0.3 collective-permute-done.5.other_ref
  22.5 20.7 %all_to_all.10.parts_ref = bf16[32,88,128]{2,1,0:T(8,128)(2,1)S(1)} all-to-all(bf16[32,88,128]{2,1,0:T(8,128)(2,1)S(1)} %bitcast.3), channel_id=1, replica_groups={{0,1,2,3,32,33,34,35,64,65,66,67,96,97,98,99,128,129,130,131,160,161,16..., dimensions={0} | all-to-all | bytes 1441792 | tf_op jit(solution)/shard_map/all_to_all | solution.py:440
  43.2 4.3 %collective-permute-start.6 = (bf16[88,128]{1,0:T(8,128)(2,1)S(1)}, bf16[88,128]{1,0:T(8,128)(2,1)S(1)}, u32[]{:S(2)}, u32[]{:S(2)}) collective-permute-start(bf16[88,128]{1,0:T(8,128)(2,1)S(1)} %shard_map.92.after_ref.own_ref), channel_id=1, source_target_pairs={{0,4},{1,5},{2,6},{3,7},{4,0},{5,1},{6,2},{7,3},{8,12},{9,13},{10,... | collective-permute-start | bytes 67592 | tf_op jit(solution)/shard_map/ppermute | solution.py:447
  47.5 0.9 %shard_map.93.refs_0_.grad_ref = bf16[864,128]{1,0:T(8,128)(2,1)S(1)} custom-call(f32[4,20,8,128]{3,2,1,0:T(8,128)S(1)} %get-tuple-element.47.side, f32[2,144,128]{2,1,0:T(8,128)S(1)} %get-tuple-element.51.side_grad, f32[4,18,8,128]{3,2,1,0:T(8,128)S(1)} %get-tuple-element.40.hidden_mid, f32[6,18,8,128]{3,2,1,0:T(8,128)S(1)} %get-tuple-element.41.pre_ref, ...), custom_call_target="tpu_custom_call" | custom-call | flops 8589934592 | bytes 1048576 | tf_op jit(solution)/shard_map/pallas_call | solution.py:494
  48.4 0.3 collective-permute-done.6.other_ref
  48.7 3.7 %collective-permute-start.7 = (bf16[88,128]{1,0:T(8,128)(2,1)S(1)}, bf16[88,128]{1,0:T(8,128)(2,1)S(1)}, u32[]{:S(2)}, u32[]{:S(2)}) collective-permute-start(bf16[88,128]{1,0:T(8,128)(2,1)S(1)} %shard_map.94.after_ref.own_ref), channel_id=1, source_target_pairs={{0,12},{1,13},{2,14},{3,15},{4,8},{5,9},{6,10},{7,11},{8,4},{9,5},... | collective-permute-start | bytes 67592 | tf_op jit(solution)/shard_map/ppermute | solution.py:447
  52.4 2.1 %shard_map.95 = (bf16[256,128]{1,0:T(8,128)(2,1)}, bf16[16,128]{1,0:T(8,128)(2,1)S(1)}) custom-call(s32[1,256]{1,0:T(1,128)S(1)} %bitcast.8, bf16[864,128]{1,0:T(8,128)(2,1)S(1)} %shard_map.93.refs_0_.grad_ref, bf16[27,128,128]{2,1,0:T(8,128)(2,1)S(1)} %copy-done, bf16[88,128]{1,0:T(8,128)(2,1)S(1)} %shard_map.94.after_ref.own_ref), custom_call_target="tpu_custom_call" | custom-call | flops 8589934592 | bytes 1048576 | tf_op jit(solution)/shard_map/pallas_call | solution.py:501
  54.5 15.2 %all_to_all.11 = bf16[32,88,128]{2,1,0:T(8,128)(2,1)S(1)} all-to-all(bf16[32,88,128]{2,1,0:T(8,128)(2,1)S(1)} %shard_map.96), channel_id=1, replica_groups={{0,1,2,3,32,33,34,35,64,65,66,67,96,97,98,99,128,129,130,131,160,161,16..., dimensions={0} | all-to-all | bytes 1441792 | tf_op jit(solution)/shard_map/all_to_all | solution.py:440
  69.7 4.2 %collective-permute-start.8 = (bf16[2816,128]{1,0:T(8,128)(2,1)S(1)}, bf16[2816,128]{1,0:T(8,128)(2,1)S(1)}, u32[]{:S(2)}, u32[]{:S(2)}) collective-permute-start(bf16[2816,128]{1,0:T(8,128)(2,1)S(1)} %bitcast.4), channel_id=1, source_target_pairs={{0,16},{16,0},{32,48},{48,32},{64,80},{80,64},{96,112},{112,96},{1... | collective-permute-start | bytes 2162696 | tf_op jit(solution)/shard_map/ppermute | solution.py:35
  73.9 1.1 %shard_map.97 = (f32[27,128,128]{2,1,0:T(8,128)}, f32[1024,256]{1,0:T(8,128)}) custom-call(bf16[2816,128]{1,0:T(8,128)(2,1)S(1)} %bitcast.5), custom_call_target="tpu_custom_call" | custom-call | flops 8589934592 | bytes 1048576 | tf_op jit(solution)/shard_map/pallas_call | solution.py:507
  75.0 0.7 collective-permute-done.8.data_ref
  75.7 1.1 %shard_map.98 = (f32[27,128,128]{2,1,0:T(8,128)}, f32[1024,256]{1,0:T(8,128)}) custom-call(bf16[2816,128]{1,0:T(8,128)(2,1)S(1)} %collective-permute-done.8.data_ref, f32[27,128,128]{2,1,0:T(8,128)} %get-tuple-element.56.refs_0_, f32[1024,256]{1,0:T(8,128)} %get-tuple-element.57.refs_1_), custom_call_target="tpu_custom_call", output_to_operand_aliasing={{0}: (1, {}), {1}: (2, {})} | custom-call | bytes 1048576 | tf_op jit(solution)/shard_map/pallas_call | solution.py:508
  (21 shorter events, 0.7 us)
Async XLA Ops:
  0.6 0.8 copy-start.3
  0.6 0.8 copy-start.4
  0.7 0.9 %copy-start.2 = (bf16[256,128]{1,0:T(8,128)(2,1)S(1)}, bf16[256,128]{1,0:T(8,128)(2,1)}, u32[]{:S(2)}) copy-start(bf16[256,128]{1,0:T(8,128)(2,1)} %features.1) | copy-start | bytes 196612
  1.5 7.4 %copy-start.1 = (bf16[1024,256]{1,0:T(8,128)(2,1)S(1)}, bf16[1024,256]{1,0:T(8,128)(2,1)}, u32[]{:S(2)}) copy-start(bf16[1024,256]{1,0:T(8,128)(2,1)} %w_down.3) | copy-start | bytes 1572868
  1.8 12.0 %collective-permute-start = (bf16[112,128]{1,0:T(8,128)(2,1)S(1)}, bf16[112,128]{1,0:T(8,128)(2,1)S(1)}, u32[]{:S(2)}, u32[]{:S(2)}) collective-permute-start(bf16[112,128]{1,0:T(8,128)(2,1)S(1)} %get-tuple-element.37), channel_id=1, source_target_pairs={{1,2},{2,1},{3,4},{4,3},{5,6},{6,5},{7,8},{8,7},{9,10},{10,9},{11,... | collective-permute-start | bytes 86024 | tf_op jit(solution)/shard_map/ppermute | solution.py:35
  2.4 11.3 %collective-permute-start.1 = (bf16[112,128]{1,0:T(8,128)(2,1)S(1)}, bf16[112,128]{1,0:T(8,128)(2,1)S(1)}, u32[]{:S(2)}, u32[]{:S(2)}) collective-permute-start(bf16[112,128]{1,0:T(8,128)(2,1)S(1)} %get-tuple-element.38), channel_id=1, source_target_pairs={{0,1},{1,0},{2,3},{3,2},{4,5},{5,4},{6,7},{7,6},{8,9},{9,8},{10,11... | collective-permute-start | bytes 86024 | tf_op jit(solution)/shard_map/ppermute | solution.py:35
  9.5 9.6 %collective-permute-start.2 = (bf16[384,128]{1,0:T(8,128)(2,1)S(1)}, bf16[384,128]{1,0:T(8,128)(2,1)S(1)}, u32[]{:S(2)}, u32[]{:S(2)}) collective-permute-start(bf16[384,128]{1,0:T(8,128)(2,1)S(1)} %get-tuple-element.44), channel_id=1, source_target_pairs={{16,32},{32,16},{48,64},{64,48},{80,96},{96,80},{112,128},{128,112... | collective-permute-start | bytes 294920 | tf_op jit(solution)/shard_map/ppermute | solution.py:35
  13.8 2.2 %copy-start = (bf16[27,128,128]{2,1,0:T(8,128)(2,1)S(1)}, bf16[27,128,128]{2,1,0:T(8,128)(2,1)}, u32[]{:S(2)}) copy-start(bf16[27,128,128]{2,1,0:T(8,128)(2,1)} %w_sub_ref.3) | copy-start | bytes 2654212
  13.8 5.3 %collective-permute-start.3 = (bf16[96,128]{1,0:T(8,128)(2,1)S(1)}, bf16[96,128]{1,0:T(8,128)(2,1)S(1)}, u32[]{:S(2)}, u32[]{:S(2)}) collective-permute-start(bf16[96,128]{1,0:T(8,128)(2,1)S(1)} %get-tuple-element.45), channel_id=1, source_target_pairs={{16,32},{32,16},{48,64},{64,48},{80,96},{96,80},{112,128},{128,112... | collective-permute-start | bytes 73736 | tf_op jit(solution)/shard_map/ppermute | solution.py:35
  15.9 3.2 %collective-permute-start.4 = (bf16[480,128]{1,0:T(8,128)(2,1)S(1)}, bf16[480,128]{1,0:T(8,128)(2,1)S(1)}, u32[]{:S(2)}, u32[]{:S(2)}) collective-permute-start(bf16[480,128]{1,0:T(8,128)(2,1)S(1)} %get-tuple-element.46), channel_id=1, source_target_pairs={{0,16},{16,0},{32,48},{48,32},{64,80},{80,64},{96,112},{112,96},{1... | collective-permute-start | bytes 368648 | tf_op jit(solution)/shard_map/ppermute | solution.py:35
  20.0 2.3 %collective-permute-start.5 = (bf16[2816,128]{1,0:T(8,128)(2,1)S(1)}, bf16[2816,128]{1,0:T(8,128)(2,1)S(1)}, u32[]{:S(2)}, u32[]{:S(2)}) collective-permute-start(bf16[2816,128]{1,0:T(8,128)(2,1)S(1)} %get-tuple-element.53), channel_id=1, source_target_pairs={{0,16},{16,0},{32,48},{48,32},{64,80},{80,64},{96,112},{112,96},{1... | collective-permute-start | bytes 2162696 | tf_op jit(solution)/shard_map/ppermute | solution.py:35
  43.2 5.5 %collective-permute-start.6 = (bf16[88,128]{1,0:T(8,128)(2,1)S(1)}, bf16[88,128]{1,0:T(8,128)(2,1)S(1)}, u32[]{:S(2)}, u32[]{:S(2)}) collective-permute-start(bf16[88,128]{1,0:T(8,128)(2,1)S(1)} %shard_map.92.after_ref.own_ref), channel_id=1, source_target_pairs={{0,4},{1,5},{2,6},{3,7},{4,0},{5,1},{6,2},{7,3},{8,12},{9,13},{10,... | collective-permute-start | bytes 67592 | tf_op jit(solution)/shard_map/ppermute | solution.py:447
  48.7 5.7 %collective-permute-start.7 = (bf16[88,128]{1,0:T(8,128)(2,1)S(1)}, bf16[88,128]{1,0:T(8,128)(2,1)S(1)}, u32[]{:S(2)}, u32[]{:S(2)}) collective-permute-start(bf16[88,128]{1,0:T(8,128)(2,1)S(1)} %shard_map.94.after_ref.own_ref), channel_id=1, source_target_pairs={{0,12},{1,13},{2,14},{3,15},{4,8},{5,9},{6,10},{7,11},{8,4},{9,5},... | collective-permute-start | bytes 67592 | tf_op jit(solution)/shard_map/ppermute | solution.py:447
  69.7 6.0 %collective-permute-start.8 = (bf16[2816,128]{1,0:T(8,128)(2,1)S(1)}, bf16[2816,128]{1,0:T(8,128)(2,1)S(1)}, u32[]{:S(2)}, u32[]{:S(2)}) collective-permute-start(bf16[2816,128]{1,0:T(8,128)(2,1)S(1)} %bitcast.4), channel_id=1, source_target_pairs={{0,16},{16,0},{32,48},{48,32},{64,80},{80,64},{96,112},{112,96},{1... | collective-permute-start | bytes 2162696 | tf_op jit(solution)/shard_map/ppermute | solution.py:35

commit v8 on v7

--- a/solution.py
+++ b/solution.py
@@ -285,8 +285,7 @@
     store_of(1, send_ref, mid, side, spread_ref, hidden_ref, place_ref, cot_ref, taps_ref)
 
 
-def late_kernel(place_ref, mid, side, spread_ref, hidden_ref, cot_ref, taps_ref, w_down_ref, own_ref, coarse_ref):
-    coarse_ref[...] = dot(coarse_rows(place_ref, hidden_ref), w_down_ref[...]).astype(BF16)
+def late_kernel(place_ref, mid, side, spread_ref, hidden_ref, cot_ref, taps_ref, own_ref):
     store_of(0, own_ref, mid, side, spread_ref, hidden_ref, place_ref, cot_ref, taps_ref)
 
 
@@ -317,8 +316,10 @@
 
 
 def ring_kernel(
-    side, side_grad, hidden_mid, pre_ref, w_sub_ref, y_odd_ref, y_even_ref, x_ends_ref, x_even_ref, w_down, after_ref, grad_ref
+    side, side_grad, hidden_mid, pre_ref, w_sub_ref, y_odd_ref, y_even_ref, x_ends_ref, x_even_ref, w_down, place_ref, hidden_ref, after_ref,
+    grad_ref, coarse_ref,
 ):
+    coarse_ref[...] = dot(coarse_rows(place_ref, hidden_ref), w_down[...]).astype(BF16)
     column = (LY + 2) * LZ
     centre = kernel_rows(w_sub_ref, 1)
     rows = frame_rows(side[0:2])
@@ -485,22 +486,24 @@
     send, spread, hidden, side, side_grad = call(main_kernel, outs, flops=LONG)(
         to_corner, ids, *early, x_odd, x_far, x_even, cotangent, w_sub
     )
-    own, coarse = call(late_kernel, [packed, ((U_DEV, C2), BF16)], flops=LONG)(
-        to_corner, mid, side, spread, hidden, cotangent, taps, w_down
+    (own,) = call(late_kernel, [packed], flops=LONG)(
+        to_corner, mid, side, spread, hidden, cotangent, taps
     )
 
     def first(value):
-        outs = [(((LX + 2) * (LY + 2) * LZ, C), BF16)]
-        (grad,) = call(ring_kernel, outs, flops=LONG)(
-            side, side_grad, hidden_mid, pre_act, w_sub, y_odd, y_even, x_far, x_even, w_down, value
+        outs = [(((LX + 2) * (LY + 2) * LZ, C), BF16), ((U_DEV, C2), BF16)]
+        grad, coarse = call(ring_kernel, outs, flops=LONG)(
+            side, side_grad, hidden_mid, pre_act, w_sub, y_odd, y_even, x_far, x_even, w_down, to_corner, hidden, value
         )
-        return grad, grad
-
-    def second(value, grad):
+        return (grad, coarse), grad
+
+    def second(value, earlier):
+        grad, coarse = earlier
         outs = [((rows, C), BF16), ((16, C), BF16)]
-        return call(feature_kernel, outs, [framed], flops=LONG)(ids, grad, w_sub, value)
-
-    feature_grad, whole, other = reduce_all(own, send, first, second)
+        feature_grad, mark = call(feature_kernel, outs, [framed], flops=LONG)(ids, grad, w_sub, value)
+        return (feature_grad, coarse), mark
+
+    (feature_grad, coarse), whole, other = reduce_all(own, send, first, second)
     grads = [((OFFSETS, C, C), F32), ((8 * C, C2), F32)]
     scratch = [pltpu.VMEM((HALF // C, C, C), F32), pltpu.VMEM((8 * C, C2), F32), pltpu.SemaphoreType.DMA((4,))]
     in_hbm = [pl.BlockSpec(memory_space=pltpu.HBM)] * 2

time: 77.2 us -> 77.2 us (level)
    pallas_call x1, Pallas kernels: 1.89 us -> 0.81 us  [local(): call(late_kernel, [packed], flops=LONG)]
    ppermute x7, waiting for transfers between devices: 2.49 us -> 3.56 us  [swap(): return lax.ppermute(value, axis, swap_pairs(lax.axis_size(axis))[kind])]
  transfers between devices with their start and end apart: 9 -> 9, of which waited for: 4 -> 3; matrix products, arithmetic and copies ran while one was open for 0% -> 0% of each run, Pallas kernels for 11% -> 10%
where the time goes in v8:
time: 77.2 us; the launch traced here: 76.9 us
  blocking collectives  35.7 us (46%)
  starting transfers between devices  25.6 us (33%)
  Pallas kernels  10.7 us (14%)
  waiting for transfers between devices  3.56 us (5%)
  between operations  0.8 us (1%)
    all_to_all x2, blocking collectives, trade(): lax.all_to_all(value, AXES, 0, 0, axis_index_groups=blocks, tiled=True)  35.7 us
    ppermute x7, starting transfers between devices, swap(): return lax.ppermute(value, axis, swap_pairs(lax.axis_size(axis))[kind])  17.8 us
    ppermute x2, starting transfers between devices, reduce_all(): arrived = lax.ppermute(total, 'gy', pairs)  7.81 us
    ppermute x7, waiting for transfers between devices, swap(): return lax.ppermute(value, axis, swap_pairs(lax.axis_size(axis))[kind])  3.56 us
    pallas_call x1, Pallas kernels, second(): call(feature_kernel, outs, [framed], flops=LONG)(ids, grad, w_sub, value)  2.07 us
    pallas_call x1, Pallas kernels, local(): call(early_kernel, [(planes, F32), ((LX, LY + 2, LZ, C), F32), ((LX + 2,...  1.6 us
  transfers between devices with their start and end apart: 9, of which 3 were waited for; matrix products, arithmetic and copies ran while one was open for 0% of the time, Pallas kernels for 10%

profile of v8, /device:TPU:1, one launch (start us, length us, event | category | flops | bytes accessed | tf_op | source)
XLA Modules:
  0.0 76.9 jit_solution(14698575940120327404)
XLA Ops:
  0.7 0.4 shard_map.84
  1.0 0.3 copy-done.3
  1.5 0.2 shard_map.85
  1.8 0.7 collective-permute-start
  2.4 6.5 %collective-permute-start.1 = (bf16[112,128]{1,0:T(8,128)(2,1)S(1)}, bf16[112,128]{1,0:T(8,128)(2,1)S(1)}, u32[]{:S(2)}, u32[]{:S(2)}) collective-permute-start(bf16[112,128]{1,0:T(8,128)(2,1)S(1)} %get-tuple-element.38), channel_id=1, source_target_pairs={{0,1},{1,0},{2,3},{3,2},{4,5},{5,4},{6,7},{7,6},{8,9},{9,8},{10,11... | collective-permute-start | bytes 86024 | tf_op jit(solution)/shard_map/ppermute | solution.py:35
  8.9 0.6 shard_map.86
  9.5 4.2 %collective-permute-start.2 = (bf16[384,128]{1,0:T(8,128)(2,1)S(1)}, bf16[384,128]{1,0:T(8,128)(2,1)S(1)}, u32[]{:S(2)}, u32[]{:S(2)}) collective-permute-start(bf16[384,128]{1,0:T(8,128)(2,1)S(1)} %get-tuple-element.44), channel_id=1, source_target_pairs={{16,32},{32,16},{48,64},{64,48},{80,96},{96,80},{112,128},{128,112... | collective-permute-start | bytes 294920 | tf_op jit(solution)/shard_map/ppermute | solution.py:35
  13.8 2.1 %collective-permute-start.3 = (bf16[96,128]{1,0:T(8,128)(2,1)S(1)}, bf16[96,128]{1,0:T(8,128)(2,1)S(1)}, u32[]{:S(2)}, u32[]{:S(2)}) collective-permute-start(bf16[96,128]{1,0:T(8,128)(2,1)S(1)} %get-tuple-element.45), channel_id=1, source_target_pairs={{16,32},{32,16},{48,64},{64,48},{80,96},{96,80},{112,128},{128,112... | collective-permute-start | bytes 73736 | tf_op jit(solution)/shard_map/ppermute | solution.py:35
  16.0 1.6 %shard_map.87 = (f32[4,20,8,128]{3,2,1,0:T(8,128)S(1)}, f32[4,18,8,128]{3,2,1,0:T(8,128)S(1)}, f32[6,18,8,128]{3,2,1,0:T(8,128)S(1)}, f32[3456,128]{1,0:T(8,128)S(1)}, f32[256,128]{1,0:T(8,128)S(1)}) custom-call(bf16[512,128]{1,0:T(8,128)(2,1)S(1)} %get-tuple-element.34.grid_ref, bf16[512,128]{1,0:T(8,128)(2,1)S(1)} %get-tuple-element.36.hidden_ref, ...), custom_call_target="tpu_custom_call" | custom-call | flops 8589934592 | bytes 1048576 | tf_op jit(solution)/shard_map/pallas_call | solution.py:479
  17.6 1.5 %collective-permute-done.3.x_ends_ref = bf16[96,128]{1,0:T(8,128)(2,1)S(1)} collective-permute-done((bf16[96,128]{1,0:T(8,128)(2,1)S(1)}, bf16[96,128]{1,0:T(8,128)(2,1)S(1)}, u32[]{:S(2)}, u32[]{:S(2)}) %collective-permute-start.3) | collective-permute-done | bytes 24608 | tf_op jit(solution)/shard_map/ppermute | solution.py:35
  19.1 0.9 %shard_map.89 = (bf16[2816,128]{1,0:T(8,128)(2,1)S(1)}, bf16[256,384]{1,0:T(8,128)(2,1)S(1)}, bf16[512,128]{1,0:T(8,128)(2,1)S(1)}, f32[4,20,8,128]{3,2,1,0:T(8,128)S(1)}, f32[2,144,128]{2,1,0:T(8,128)S(1)}) custom-call(bf16[512,512]{1,0:T(8,128)(2,1)S(1)} %get-tuple-element.32.place_ref, s32[1,256]{1,0:T(1,128)S(1)} %bitcast.7, ...), custom_call_target="tpu_custom_call" | custom-call | flops 8589934592 | bytes 1048576 | tf_op jit(solution)/shard_map/pallas_call | solution.py:486
  20.1 0.8 %shard_map.90.own_ref = bf16[2816,128]{1,0:T(8,128)(2,1)S(1)} custom-call(bf16[512,512]{1,0:T(8,128)(2,1)S(1)} %get-tuple-element.32.place_ref, f32[4,20,8,128]{3,2,1,0:T(8,128)S(1)} %get-tuple-element.39.mid, f32[4,20,8,128]{3,2,1,0:T(8,128)S(1)} %get-tuple-element.47.side, bf16[256,384]{1,0:T(8,128)(2,1)S(1)} %get-tuple-element.50.spread_ref, ...), custom_call_target="tpu_custom_call" | custom-call | flops 8589934592 | bytes 1048576 | tf_op jit(solution)/shard_map/pallas_call | solution.py:489
  21.0 1.4 %collective-permute-done.5.other_ref = bf16[2816,128]{1,0:T(8,128)(2,1)S(1)} collective-permute-done((bf16[2816,128]{1,0:T(8,128)(2,1)S(1)}, bf16[2816,128]{1,0:T(8,128)(2,1)S(1)}, u32[]{:S(2)}, u32[]{:S(2)}) %collective-permute-start.5) | collective-permute-done | bytes 720928 | tf_op jit(solution)/shard_map/ppermute | solution.py:35
  22.3 0.2 shard_map.91
  22.5 20.5 %all_to_all.10.parts_ref = bf16[32,88,128]{2,1,0:T(8,128)(2,1)S(1)} all-to-all(bf16[32,88,128]{2,1,0:T(8,128)(2,1)S(1)} %bitcast.3), channel_id=1, replica_groups={{0,1,2,3,32,33,34,35,64,65,66,67,96,97,98,99,128,129,130,131,160,161,16..., dimensions={0} | all-to-all | bytes 1441792 | tf_op jit(solution)/shard_map/all_to_all | solution.py:441
  43.1 4.3 %collective-permute-start.6 = (bf16[88,128]{1,0:T(8,128)(2,1)S(1)}, bf16[88,128]{1,0:T(8,128)(2,1)S(1)}, u32[]{:S(2)}, u32[]{:S(2)}) collective-permute-start(bf16[88,128]{1,0:T(8,128)(2,1)S(1)} %shard_map.92.after_ref.own_ref), channel_id=1, source_target_pairs={{0,4},{1,5},{2,6},{3,7},{4,0},{5,1},{6,2},{7,3},{8,12},{9,13},{10,... | collective-permute-start | bytes 67592 | tf_op jit(solution)/shard_map/ppermute | solution.py:448
  47.4 1.5 %shard_map.93 = (bf16[864,128]{1,0:T(8,128)(2,1)S(1)}, bf16[64,256]{1,0:T(8,128)(2,1)}) custom-call(f32[4,20,8,128]{3,2,1,0:T(8,128)S(1)} %get-tuple-element.47.side, f32[2,144,128]{2,1,0:T(8,128)S(1)} %get-tuple-element.48.side_grad, f32[4,18,8,128]{3,2,1,0:T(8,128)S(1)} %get-tuple-element.40.hidden_mid, f32[6,18,8,128]{3,2,1,0:T(8,128)S(1)} %get-tuple-element.41.pre_ref, ...), custom_call_target="tpu_custom_call" | custom-call | flops 8589934592 | bytes 1048576 | tf_op jit(solution)/shard_map/pallas_call | solution.py:495
  48.9 3.5 %collective-permute-start.7 = (bf16[88,128]{1,0:T(8,128)(2,1)S(1)}, bf16[88,128]{1,0:T(8,128)(2,1)S(1)}, u32[]{:S(2)}, u32[]{:S(2)}) collective-permute-start(bf16[88,128]{1,0:T(8,128)(2,1)S(1)} %shard_map.94.after_ref.own_ref), channel_id=1, source_target_pairs={{0,12},{1,13},{2,14},{3,15},{4,8},{5,9},{6,10},{7,11},{8,4},{9,5},... | collective-permute-start | bytes 67592 | tf_op jit(solution)/shard_map/ppermute | solution.py:448
  52.4 2.1 %shard_map.95 = (bf16[256,128]{1,0:T(8,128)(2,1)}, bf16[16,128]{1,0:T(8,128)(2,1)S(1)}) custom-call(s32[1,256]{1,0:T(1,128)S(1)} %bitcast.8, bf16[864,128]{1,0:T(8,128)(2,1)S(1)} %get-tuple-element.53.refs_0_.grad_ref, bf16[27,128,128]{2,1,0:T(8,128)(2,1)S(1)} %copy-done, bf16[88,128]{1,0:T(8,128)(2,1)S(1)} %shard_map.94.after_ref.own_ref), custom_call_target="tpu_custom_call" | custom-call | flops 8589934592 | bytes 1048576 | tf_op jit(solution)/shard_map/pallas_call | solution.py:503
  54.5 15.2 %all_to_all.11 = bf16[32,88,128]{2,1,0:T(8,128)(2,1)S(1)} all-to-all(bf16[32,88,128]{2,1,0:T(8,128)(2,1)S(1)} %shard_map.96), channel_id=1, replica_groups={{0,1,2,3,32,33,34,35,64,65,66,67,96,97,98,99,128,129,130,131,160,161,16..., dimensions={0} | all-to-all | bytes 1441792 | tf_op jit(solution)/shard_map/all_to_all | solution.py:441
  69.7 4.2 %collective-permute-start.8 = (bf16[2816,128]{1,0:T(8,128)(2,1)S(1)}, bf16[2816,128]{1,0:T(8,128)(2,1)S(1)}, u32[]{:S(2)}, u32[]{:S(2)}) collective-permute-start(bf16[2816,128]{1,0:T(8,128)(2,1)S(1)} %bitcast.4), channel_id=1, source_target_pairs={{0,16},{16,0},{32,48},{48,32},{64,80},{80,64},{96,112},{112,96},{1... | collective-permute-start | bytes 2162696 | tf_op jit(solution)/shard_map/ppermute | solution.py:35
  73.9 1.1 %shard_map.97 = (f32[27,128,128]{2,1,0:T(8,128)}, f32[1024,256]{1,0:T(8,128)}) custom-call(bf16[2816,128]{1,0:T(8,128)(2,1)S(1)} %bitcast.5), custom_call_target="tpu_custom_call" | custom-call | flops 8589934592 | bytes 1048576 | tf_op jit(solution)/shard_map/pallas_call | solution.py:510
  75.0 0.7 collective-permute-done.8.data_ref
  75.7 1.1 %shard_map.98 = (f32[27,128,128]{2,1,0:T(8,128)}, f32[1024,256]{1,0:T(8,128)}) custom-call(bf16[2816,128]{1,0:T(8,128)(2,1)S(1)} %collective-permute-done.8.data_ref, f32[27,128,128]{2,1,0:T(8,128)} %get-tuple-element.56.refs_0_, f32[1024,256]{1,0:T(8,128)} %get-tuple-element.57.refs_1_), custom_call_target="tpu_custom_call", output_to_operand_aliasing={{0}: (1, {}), {1}: (2, {})} | custom-call | bytes 1048576 | tf_op jit(solution)/shard_map/pallas_call | solution.py:511
  (21 shorter events, 0.6 us)
Async XLA Ops:
  0.6 0.8 copy-start.3
  0.6 0.8 copy-start.4
  0.7 0.9 %copy-start.2 = (bf16[256,128]{1,0:T(8,128)(2,1)S(1)}, bf16[256,128]{1,0:T(8,128)(2,1)}, u32[]{:S(2)}) copy-start(bf16[256,128]{1,0:T(8,128)(2,1)} %features.1) | copy-start | bytes 196612
  1.5 7.4 %copy-start.1 = (bf16[1024,256]{1,0:T(8,128)(2,1)S(1)}, bf16[1024,256]{1,0:T(8,128)(2,1)}, u32[]{:S(2)}) copy-start(bf16[1024,256]{1,0:T(8,128)(2,1)} %w_down.3) | copy-start | bytes 1572868
  1.8 12.0 %collective-permute-start = (bf16[112,128]{1,0:T(8,128)(2,1)S(1)}, bf16[112,128]{1,0:T(8,128)(2,1)S(1)}, u32[]{:S(2)}, u32[]{:S(2)}) collective-permute-start(bf16[112,128]{1,0:T(8,128)(2,1)S(1)} %get-tuple-element.37), channel_id=1, source_target_pairs={{1,2},{2,1},{3,4},{4,3},{5,6},{6,5},{7,8},{8,7},{9,10},{10,9},{11,... | collective-permute-start | bytes 86024 | tf_op jit(solution)/shard_map/ppermute | solution.py:35
  2.4 11.3 %collective-permute-start.1 = (bf16[112,128]{1,0:T(8,128)(2,1)S(1)}, bf16[112,128]{1,0:T(8,128)(2,1)S(1)}, u32[]{:S(2)}, u32[]{:S(2)}) collective-permute-start(bf16[112,128]{1,0:T(8,128)(2,1)S(1)} %get-tuple-element.38), channel_id=1, source_target_pairs={{0,1},{1,0},{2,3},{3,2},{4,5},{5,4},{6,7},{7,6},{8,9},{9,8},{10,11... | collective-permute-start | bytes 86024 | tf_op jit(solution)/shard_map/ppermute | solution.py:35
  9.5 9.6 %collective-permute-start.2 = (bf16[384,128]{1,0:T(8,128)(2,1)S(1)}, bf16[384,128]{1,0:T(8,128)(2,1)S(1)}, u32[]{:S(2)}, u32[]{:S(2)}) collective-permute-start(bf16[384,128]{1,0:T(8,128)(2,1)S(1)} %get-tuple-element.44), channel_id=1, source_target_pairs={{16,32},{32,16},{48,64},{64,48},{80,96},{96,80},{112,128},{128,112... | collective-permute-start | bytes 294920 | tf_op jit(solution)/shard_map/ppermute | solution.py:35
  13.8 2.2 %copy-start = (bf16[27,128,128]{2,1,0:T(8,128)(2,1)S(1)}, bf16[27,128,128]{2,1,0:T(8,128)(2,1)}, u32[]{:S(2)}) copy-start(bf16[27,128,128]{2,1,0:T(8,128)(2,1)} %w_sub_ref.3) | copy-start | bytes 2654212
  13.8 5.3 %collective-permute-start.3 = (bf16[96,128]{1,0:T(8,128)(2,1)S(1)}, bf16[96,128]{1,0:T(8,128)(2,1)S(1)}, u32[]{:S(2)}, u32[]{:S(2)}) collective-permute-start(bf16[96,128]{1,0:T(8,128)(2,1)S(1)} %get-tuple-element.45), channel_id=1, source_target_pairs={{16,32},{32,16},{48,64},{64,48},{80,96},{96,80},{112,128},{128,112... | collective-permute-start | bytes 73736 | tf_op jit(solution)/shard_map/ppermute | solution.py:35
  15.9 3.2 %collective-permute-start.4 = (bf16[480,128]{1,0:T(8,128)(2,1)S(1)}, bf16[480,128]{1,0:T(8,128)(2,1)S(1)}, u32[]{:S(2)}, u32[]{:S(2)}) collective-permute-start(bf16[480,128]{1,0:T(8,128)(2,1)S(1)} %get-tuple-element.46), channel_id=1, source_target_pairs={{0,16},{16,0},{32,48},{48,32},{64,80},{80,64},{96,112},{112,96},{1... | collective-permute-start | bytes 368648 | tf_op jit(solution)/shard_map/ppermute | solution.py:35
  20.0 2.3 %collective-permute-start.5 = (bf16[2816,128]{1,0:T(8,128)(2,1)S(1)}, bf16[2816,128]{1,0:T(8,128)(2,1)S(1)}, u32[]{:S(2)}, u32[]{:S(2)}) collective-permute-start(bf16[2816,128]{1,0:T(8,128)(2,1)S(1)} %get-tuple-element.51), channel_id=1, source_target_pairs={{0,16},{16,0},{32,48},{48,32},{64,80},{80,64},{96,112},{112,96},{1... | collective-permute-start | bytes 2162696 | tf_op jit(solution)/shard_map/ppermute | solution.py:35
  43.1 5.8 %collective-permute-start.6 = (bf16[88,128]{1,0:T(8,128)(2,1)S(1)}, bf16[88,128]{1,0:T(8,128)(2,1)S(1)}, u32[]{:S(2)}, u32[]{:S(2)}) collective-permute-start(bf16[88,128]{1,0:T(8,128)(2,1)S(1)} %shard_map.92.after_ref.own_ref), channel_id=1, source_target_pairs={{0,4},{1,5},{2,6},{3,7},{4,0},{5,1},{6,2},{7,3},{8,12},{9,13},{10,... | collective-permute-start | bytes 67592 | tf_op jit(solution)/shard_map/ppermute | solution.py:448
  48.9 5.6 %collective-permute-start.7 = (bf16[88,128]{1,0:T(8,128)(2,1)S(1)}, bf16[88,128]{1,0:T(8,128)(2,1)S(1)}, u32[]{:S(2)}, u32[]{:S(2)}) collective-permute-start(bf16[88,128]{1,0:T(8,128)(2,1)S(1)} %shard_map.94.after_ref.own_ref), channel_id=1, source_target_pairs={{0,12},{1,13},{2,14},{3,15},{4,8},{5,9},{6,10},{7,11},{8,4},{9,5},... | collective-permute-start | bytes 67592 | tf_op jit(solution)/shard_map/ppermute | solution.py:448
  69.7 6.0 %collective-permute-start.8 = (bf16[2816,128]{1,0:T(8,128)(2,1)S(1)}, bf16[2816,128]{1,0:T(8,128)(2,1)S(1)}, u32[]{:S(2)}, u32[]{:S(2)}) collective-permute-start(bf16[2816,128]{1,0:T(8,128)(2,1)S(1)} %bitcast.4), channel_id=1, source_target_pairs={{0,16},{16,0},{32,48},{48,32},{64,80},{80,64},{96,112},{112,96},{1... | collective-permute-start | bytes 2162696 | tf_op jit(solution)/shard_map/ppermute | solution.py:35
